TPU v7x, 32 devices: a whole 2x2x4 slice. The times are simulated.
32 devices in a mesh: member: 4 (over y, x), space: 8 (over z, core).
Axes of the slice: x: 2, y: 2, z: 4, core: 2. Of those that a mesh axis runs over, the one named last changes fastest.
Arguments:
- initial_fields: bfloat16 [128, 64, 1024], P('member', None, 'space'), may hold values from -4 to 4
- encode_weight: bfloat16 [64, 256], replicated, may hold values from -0.75 to 0.75
- send_weight: bfloat16 [1, 256, 256], replicated, may hold values from -0.375 to 0.375
- receive_weight: bfloat16 [1, 256, 256], replicated, may hold values from -0.375 to 0.375
- update_weight: bfloat16 [1, 256, 256], replicated, may hold values from -0.375 to 0.375
- norm_gain: bfloat16 [1, 256], replicated, may hold values from 0.099609375 to 1.8984375
- decode_weight: bfloat16 [256, 64], replicated, may hold values from -0.375 to 0.375
- edge_senders: int32 [1024, 4], P('space'), may hold values from 0 to 191
- halo_nodes: int32 [2, 256], P(None, 'space'), may hold values from 0 to 127, as said below
- observed_perturbation: bfloat16 [32, 128, 256], P(('member', 'space')), may hold values from -2.5 to 2.5
- observed_values: bfloat16 [32, 2, 256], P(('member', 'space')), may hold values from -3.5 to 3.5, as said below
- region_neighbours: int32 [32, 8], P(('member', 'space')), may hold values from 0 to 31, as said below
Outputs:
- analysis: bfloat16 [128, 64, 1024], P('member', None, 'space')
Inputs may be any that keep to these rules, and one draw needn't show every extreme that they name: edge_senders[n, k] indexes the list of the 128 nodes of n's space block, followed by the 32 nodes that halo_nodes row 0 names in the block before and the 32 that row 1 names in the block after (blocks wrap around). For each space block b, halo_nodes[0, b * 32 : (b + 1) * 32] are distinct node indices within block b - 1 and halo_nodes[1, ...] distinct ones within block b + 1, taken modulo 8. `region_neighbours`: each row lists 8 distinct regions other than r = a * 8 + b; each is ((a + p) mod 4) * 8 + ((b + s) mod 8) with either p = 0 and 1 <= |s| <= 2, or |p| = 1 and |s| <= 1. `observed_values`: row 0 of each region holds positive inverse error variances of at least 0.25.
All inputs are finite; a program needn't handle non-finite values.
Results may differ from a plain program's by a relative error of at most 0.0059.
Values may be sent and summed in bfloat16 or wider, within the bound.
No kernel may reach another device: no remote copies, remote signals or barrier semaphores. Data moves between devices by JAX's collectives and lax.ppermute only.
A program may use at most 64 MiB of HBM per device.

v0:
```python
import jax
import jax.numpy as jnp
from jax import lax
from jax.sharding import PartitionSpec as P

ITERS_NS = 5


EPSILON = 1e-05
FULL_PRECISION = lax.Precision.HIGHEST


def extended_2(cells, sides, width):
    for axis, dim in sides:
        count = lax.axis_size(axis)
        head = lax.slice_in_dim(cells, 0, width, axis=dim)
        tail = lax.slice_in_dim(cells, cells.shape[dim] - width, cells.shape[dim], axis=dim)
        cells = jnp.concatenate(
            [
                lax.ppermute(tail, axis, [(i, (i + 1) % count) for i in range(count)]),
                cells,
                lax.ppermute(head, axis, [((i + 1) % count, i) for i in range(count)]),
            ],
            axis=dim,
        )
    return cells


def normalize(messages, gains):
    mean_square = jnp.mean(messages * messages, axis=-1, keepdims=True)
    return messages * lax.rsqrt(mean_square + EPSILON) * gains.astype(jnp.float32)


def inverse_root(system):
    extent = system.shape[0]
    identity = jnp.eye(extent, dtype=jnp.float32)
    scaling = jnp.sqrt(jnp.sum(system * system))
    iterate = system / scaling
    inverse = identity
    for _ in range(ITERS_NS):
        correction = 1.5 * identity - 0.5 * jnp.dot(inverse, iterate, precision=FULL_PRECISION)
        iterate = jnp.dot(iterate, correction, precision=FULL_PRECISION)
        inverse = jnp.dot(correction, inverse, precision=FULL_PRECISION)
    return (inverse, scaling)


def analyse(states, gram_matrix, forcing):
    ensemble = states.shape[0]
    identity = jnp.eye(ensemble, dtype=jnp.float32)
    system = identity + gram_matrix / (ensemble - 1)
    inverse, scaling = inverse_root(system)
    inner = jnp.dot(inverse, forcing, precision=FULL_PRECISION)
    mean_weights = jnp.dot(inverse, inner, precision=FULL_PRECISION) / (scaling * (ensemble - 1))
    transform = inverse / jnp.sqrt(scaling) + mean_weights[:, None]
    mean_state = jnp.mean(states, axis=0)
    anomalies = states - mean_state
    moved = jnp.einsum("ij,is->js", transform, anomalies, precision=FULL_PRECISION)
    return (mean_state + moved).astype(jnp.bfloat16)


def offsets(neighbours, own_row, own_column, row_count, column_count):
    near_row = (neighbours // column_count - own_row + 1) % row_count - 1
    near_column = (neighbours % column_count - own_column + 2) % column_count - 2
    distance = (near_row * near_row + near_column * near_column).astype(jnp.float32)
    return (near_row, near_column, 1.0 / (1.0 + distance / 2.0))


def collect(square, framed):
    flat = square.reshape((9,) + square.shape[2:])
    return jnp.concatenate([flat, framed[0:1], framed[3:4]], axis=0)


def body(
    initial_fields,
    encode_weight,
    send_weight,
    receive_weight,
    update_weight,
    norm_gain,
    decode_weight,
    edge_senders,
    halo_nodes,
    observed_perturbation,
    observed_values,
    region_neighbours,
):
    halo_count = halo_nodes.shape[1]
    stream = jnp.einsum(
        "mcn,ch->mnh", initial_fields, encode_weight, preferred_element_type=jnp.float32
    )
    wanted = extended_2(halo_nodes, (("space", 1),), halo_count)
    picked = jnp.concatenate([wanted[1, :halo_count], wanted[0, 2 * halo_count :]])
    rounded = stream.astype(jnp.bfloat16)
    sent = jnp.einsum(
        "mnh,hk->mnk", rounded, send_weight[0], preferred_element_type=jnp.float32
    ).astype(jnp.bfloat16)
    received = jnp.einsum(
        "mnh,hk->mnk", rounded, receive_weight[0], preferred_element_type=jnp.float32
    )
    outgoing = jnp.take(sent, picked, axis=1)
    framed_rows = extended_2(outgoing, (("space", 1),), halo_count)
    extended = jnp.concatenate(
        [sent, framed_rows[:, :halo_count], framed_rows[:, 3 * halo_count :]], axis=1
    )
    messages = jnp.zeros_like(received)
    for slot_index in range(edge_senders.shape[1]):
        sender_rows = jnp.take(extended, edge_senders[:, slot_index], axis=1)
        messages = messages + jax.nn.silu(sender_rows.astype(jnp.float32) + received)
    normed = normalize(messages, norm_gain[0]).astype(jnp.bfloat16)
    stream = stream + jnp.einsum(
        "mnh,hk->mnk", normed, update_weight[0], preferred_element_type=jnp.float32
    )
    field_change = jnp.einsum(
        "mnh,hc->mcn",
        stream.astype(jnp.bfloat16),
        decode_weight,
        preferred_element_type=jnp.float32,
    )
    predicted_fields = (initial_fields.astype(jnp.float32) + field_change).astype(jnp.bfloat16)
    regional_states = lax.all_to_all(
        predicted_fields, "member", split_axis=2, concat_axis=0, tiled=True
    )
    ensemble = regional_states.shape[0]
    states = regional_states.reshape(ensemble, -1).astype(jnp.float32)
    near_row, near_column, weights = offsets(
        region_neighbours[0],
        lax.axis_index("member"),
        lax.axis_index("space"),
        lax.axis_size("member"),
        lax.axis_size("space"),
    )
    slot = jnp.where(
        near_column == -2, 9, jnp.where(near_column == 2, 10, (near_row + 1) * 3 + near_column + 1)
    )
    slot_range = jnp.arange(11, dtype=jnp.int32)
    slot_weight = jnp.sum(
        weights[:, None] * (slot[:, None] == slot_range[None, :]).astype(jnp.float32), axis=0
    )
    slot_weight = slot_weight + (slot_range == 4).astype(jnp.float32)
    perturbation = observed_perturbation[0]
    values = observed_values[0].astype(jnp.float32)
    wide_perturbation = perturbation.astype(jnp.float32)
    local_gram = jnp.einsum(
        "io,jo->ij",
        wide_perturbation * values[0][None, :],
        wide_perturbation,
        precision=FULL_PRECISION,
    )
    local_forcing = jnp.dot(wide_perturbation, values[0] * values[1], precision=FULL_PRECISION)
    payload = jnp.concatenate([local_gram, local_forcing[None, :]], axis=0)[None, None]
    square = extended_2(payload, (("member", 0), ("space", 1)), 1)
    paired = jnp.stack([square[1, 2], square[1, 0]])
    framed = extended_2(paired.astype(jnp.bfloat16), (("space", 0),), 1).astype(paired.dtype)
    candidates = collect(square, framed)
    gram_matrix = jnp.einsum(
        "c,cij->ij", slot_weight, candidates[:, :ensemble], precision=FULL_PRECISION
    )
    forcing = jnp.dot(slot_weight, candidates[:, ensemble], precision=FULL_PRECISION)
    analysed = analyse(states, gram_matrix, forcing).reshape(regional_states.shape)
    return lax.all_to_all(analysed, "member", split_axis=0, concat_axis=2, tiled=True)


def solution(mesh):
    placed = (
        P("member", None, "space"),
        P(),
        P(),
        P(),
        P(),
        P(),
        P(),
        P("space", None),
        P(None, "space"),
        P(("member", "space"), None, None),
        P(("member", "space"), None, None),
        P(("member", "space"), None),
    )
    return jax.shard_map(
        body, mesh=mesh, in_specs=placed, out_specs=P("member", None, "space"), check_vma=False
    )
```

profile of v0, /device:TPU:0, one launch (start us, length us, event | category | flops | bytes accessed | tf_op | source)
XLA Modules:
  0.0 120.3 jit_solution(5657904464719869651)
XLA Ops:
  0.0 4.5 %collective-permute-start.1 = (s32[2,32]{1,0:T(2,128)}, s32[2,32]{1,0:T(2,128)S(1)}, u32[]{:S(2)}, u32[]{:S(2)}) collective-permute-start(s32[2,32]{1,0:T(2,128)} %param.22), channel_id=1, source_target_pairs={{1,0},{2,1},{3,2},{4,3},{5,4},{6,5},{7,6},{0,7},{9,8},{10,9},{11,1... | collective-permute-start | bytes 776 | tf_op jit(solution)/shard_map/ppermute | solution.py:22
  4.5 0.7 convert_element_type.104
  5.2 0.7 slice.83
  5.9 1.0 fusion.28
  6.8 1.2 %fusion.20 = f32[128,128]{1,0:T(8,128)S(1)} fusion(bf16[1,128,256]{2,1,0:T(8,128)(2,1)} %param.23, f32[256]{0:T(256)S(1)} %bitcast.180), kind=kOutput, calls=%fused_computation.49 | convolution fusion | flops 50397184 | bytes 132096 | tf_op jit(solution)/shard_map/io,jo->ij/dot_general | solution.py:143
  8.0 2.5 %collective-permute-start.5 = (f32[1,1,129,128]{3,2,1,0:T(8,128)S(1)}, f32[1,1,129,128]{3,2,1,0:T(8,128)S(1)}, u32[]{:S(2)}, u32[]{:S(2)}) collective-permute-start(f32[1,1,129,128]{3,2,1,0:T(8,128)S(1)} %maximum_bitcast_fusion), channel_id=1, source_target_pairs={{8,0},{16,8},{24,16},{0,24},{9,1},{17,9},{25,17},{1,25},{10,2},{18... | collective-permute-start | bytes 198152 | tf_op jit(solution)/shard_map/ppermute | solution.py:22
  10.5 0.8 compare_and_fusion.3
  11.4 1.8 %fusion.40 = f32[32,128,256]{2,1,0:T(8,128)S(1)} fusion(bf16[32,64,128]{2,1,0:T(8,128)(2,1)} %param.14, bf16[64,256]{1,0:T(8,128)(2,1)} %param.15), kind=kOutput, calls=%fused_computation.78 | convolution fusion | flops 134217728 | bytes 4751360 | tf_op jit(solution)/shard_map/mcn,ch->mnh/dot_general | solution.py:88
  13.2 0.7 convolution_convert_fusion
  14.1 2.5 %copy.107 = bf16[32,128,256]{2,0,1:T(8,128)(2,1)} copy(bf16[32,128,256]{2,1,0:T(8,128)(2,1)S(1)} %convolution_convert_fusion) | data formatting | bytes 4194304 | tf_op jit(solution)/shard_map/convert_element_type | solution.py:96
  16.8 2.2 %gather_fusion = bf16[64,32,256]{2,1,0:T(8,128)(2,1)S(1)} fusion(bf16[32,128,256]{2,0,1:T(8,128)(2,1)} %copy.107, s32[1024]{0:T(1024)S(1)} %pad_clamp_fusion.4), kind=kCustom, calls=%fused_computation.4 | custom fusion | bytes 2097408 | tf_op jit(solution)/shard_map/jit(_take)/gather | solution.py:100
  19.1 0.6 fusion.15
  19.8 3.3 %collective-permute-start.7 = (f32[3,1,129,128]{3,2,1,0:T(8,128)S(1)}, f32[3,1,129,128]{3,2,1,0:T(8,128)S(1)}, u32[]{:S(2)}, u32[]{:S(2)}) collective-permute-start(f32[3,1,129,128]{3,2,1,0:T(8,128)S(1)} %pad_maximum_fusion.3), channel_id=1, source_target_pairs={{1,0},{2,1},{3,2},{4,3},{5,4},{6,5},{7,6},{0,7},{9,8},{10,9},{11,1... | collective-permute-start | bytes 594440 | tf_op jit(solution)/shard_map/ppermute | solution.py:22
  23.1 1.1 fusion.68
  24.1 0.5 collective-permute-start.2
  24.6 3.0 %collective-permute-done.7 = f32[3,1,129,128]{3,2,1,0:T(8,128)S(1)} collective-permute-done((f32[3,1,129,128]{3,2,1,0:T(8,128)S(1)}, f32[3,1,129,128]{3,2,1,0:T(8,128)S(1)}, u32[]{:S(2)}, u32[]{:S(2)}) %collective-permute-start.7) | collective-permute-done | bytes 198176 | tf_op jit(solution)/shard_map/ppermute | solution.py:22
  27.6 3.7 %collective-permute-start.9 = (bf16[1,129,128]{2,1,0:T(8,128)(2,1)S(1)}, bf16[1,129,128]{2,1,0:T(8,128)(2,1)S(1)}, u32[]{:S(2)}, u32[]{:S(2)}) collective-permute-start(bf16[1,129,128]{2,1,0:T(8,128)(2,1)S(1)} %fusion.37), channel_id=1, source_target_pairs={{1,0},{2,1},{3,2},{4,3},{5,4},{6,5},{7,6},{0,7},{9,8},{10,9},{11,1... | collective-permute-start | bytes 99080 | tf_op jit(solution)/shard_map/ppermute | solution.py:22
  31.3 8.2 %collective-permute-done.6 = f32[3,1,129,128]{3,2,1,0:T(8,128)S(1)} collective-permute-done((f32[3,1,129,128]{3,2,1,0:T(8,128)S(1)}, f32[3,1,129,128]{3,2,1,0:T(8,128)S(1)}, u32[]{:S(2)}, u32[]{:S(2)}) %collective-permute-start.6) | collective-permute-done | bytes 198176 | tf_op jit(solution)/shard_map/ppermute | solution.py:20
  39.5 0.9 collective-permute-start.8
  40.5 4.2 %collective-permute-done.8 = bf16[1,129,128]{2,1,0:T(8,128)(2,1)S(1)} collective-permute-done((bf16[1,129,128]{2,1,0:T(8,128)(2,1)S(1)}, bf16[1,129,128]{2,1,0:T(8,128)(2,1)S(1)}, u32[]{:S(2)}, u32[]{:S(2)}) %collective-permute-start.8) | collective-permute-done | bytes 33056 | tf_op jit(solution)/shard_map/ppermute | solution.py:20
  44.8 1.0 fusion.13
  45.9 0.7 multiply_reduce_fusion.1
  47.6 0.2 fusion.44
  50.3 2.3 %pad_maximum_fusion = bf16[32,192,256]{2,1,0:T(8,128)(2,1)S(1)} fusion(bf16[32,32,256]{2,1,0:T(8,128)(2,1)} %collective-permute-done.3, bf16[32,32,256]{2,1,0:T(8,128)(2,1)} %collective-permute-done.2, bf16[32,128,256]{2,1,0:T(8,128)(2,1)S(1)} %convolution_convert_fusion), kind=kLoop, calls=%fused_computation.9 | loop fusion | flops 9437184 | bytes 6291456 | tf_op jit(solution)/shard_map/concatenate | solution.py:102
  52.6 1.8 %copy.109 = bf16[32,192,256]{2,0,1:T(8,128)(2,1)S(1)} copy(bf16[32,192,256]{2,1,0:T(8,128)(2,1)S(1)} %pad_maximum_fusion) | data formatting | bytes 6291456 | tf_op jit(solution)/shard_map/concatenate | solution.py:102
  54.4 2.1 %gather_fusion.4 = bf16[128,32,256]{2,1,0:T(8,128)(2,1)} fusion(bf16[32,192,256]{2,0,1:T(8,128)(2,1)S(1)} %copy.109, s32[1024]{0:T(1024)S(1)} %get-tuple-element.33), kind=kCustom, calls=%fused_computation.3.clone | custom fusion | bytes 4194816 | tf_op jit(solution)/shard_map/jit(_take)/gather | solution.py:107
  56.4 2.0 %gather_fusion.3 = bf16[128,32,256]{2,1,0:T(8,128)(2,1)} fusion(bf16[32,192,256]{2,0,1:T(8,128)(2,1)S(1)} %copy.109, s32[1024]{0:T(1024)S(1)} %get-tuple-element.34), kind=kCustom, calls=%fused_computation.2.clone | custom fusion | bytes 4194816 | tf_op jit(solution)/shard_map/jit(_take)/gather | solution.py:107
  58.4 2.0 %gather_fusion.2 = bf16[128,32,256]{2,1,0:T(8,128)(2,1)} fusion(bf16[32,192,256]{2,0,1:T(8,128)(2,1)S(1)} %copy.109, s32[1024]{0:T(1024)S(1)} %get-tuple-element.35), kind=kCustom, calls=%fused_computation.1.clone | custom fusion | bytes 4194816 | tf_op jit(solution)/shard_map/jit(_take)/gather | solution.py:107
  60.4 2.0 %gather_fusion.1 = bf16[128,32,256]{2,1,0:T(8,128)(2,1)} fusion(bf16[32,192,256]{2,0,1:T(8,128)(2,1)S(1)} %copy.109, s32[1024]{0:T(1024)S(1)} %get-tuple-element.36), kind=kCustom, calls=%fused_computation.clone | custom fusion | bytes 4194816 | tf_op jit(solution)/shard_map/jit(_take)/gather | solution.py:107
  62.4 13.8 %multiply_reduce_fusion = (f32[32,128]{1,0:T(8,128)S(1)}, f32[32,128,256]{2,1,0:T(8,128)}) fusion(bf16[128,32,256]{2,1,0:T(8,128)(2,1)} %gather_fusion.4, pred[128]{0:T(512)(128)(4,1)S(1)} %get-tuple-element.23, bf16[128,32,256]{2,1,0:T(8,128)(2,1)} %gather_fusion.3, pred[128]{0:T(512)(128)(4,1)S(1)} %get-tuple-element.25, ...), kind=kOutput, calls=%fused_computation.7 | convolution fusion | flops 572518400 | bytes 16925184 | tf_op jit(solution)/shard_map/mnh,hk->mnk/dot_general | solution.py:97
  76.2 4.9 %fusion.6 = bf16[32,64,128]{2,1,0:T(8,128)(2,1)S(1)} fusion(f32[32,128,256]{2,1,0:T(8,128)} %copy-done.1, f32[32,128,256]{2,1,0:T(8,128)} %get-tuple-element.32, f32[256]{0:T(256)S(1)} %bitcast.179, f32[32,128]{1,0:T(8,128)S(1)} %add_rsqrt_fusion, bf16[32,64,128]{2,1,0:T(8,128)(2,1)S(1)} %copy-done.2, bf16[1,256,256]{2,1,0:T(8,128)(2,1)S(1)} %copy-done.3, ...), kind=kOutput, calls=%fused_computation.22 | convolution fusion | flops 677117952 | bytes 9618432 | tf_op jit(solution)/shard_map/mnh,hc->mcn/dot_general | solution.py:113
  81.2 1.6 %copy.117 = bf16[32,64,128]{1,0,2:T(8,128)(2,1)S(1)} copy(bf16[32,64,128]{2,1,0:T(8,128)(2,1)S(1)} %fusion.6) | data formatting | bytes 1048576 | tf_op jit(solution)/shard_map/convert_element_type | solution.py:119
  82.8 1.6 %reshape.333 = bf16[4,2,32768]{2,1,0:T(2,128)(2,1)} reshape(bf16[128,32,64]{2,1,0:T(8,128)(2,1)S(1)} %bitcast.169) | data formatting | bytes 1048576
  84.3 3.9 %all-to-all-start = ((bf16[4,2,32768]{2,1,0:T(2,128)(2,1)}), bf16[4,2,32768]{2,1,0:T(2,128)(2,1)S(1)}, u32[]{:S(2)}, u32[]{:S(2)}) async-start(bf16[4,2,32768]{2,1,0:T(2,128)(2,1)} %reshape.333), calls=%async_computation | async-start | bytes 1048576 | tf_op jit(solution)/shard_map/all_to_all | solution.py:120
  88.4 0.2 fusion.12
  88.6 7.0 %all-to-all-done = bf16[4,2,32768]{2,1,0:T(2,128)(2,1)S(1)} async-done(((bf16[4,2,32768]{2,1,0:T(2,128)(2,1)}), bf16[4,2,32768]{2,1,0:T(2,128)(2,1)S(1)}, u32[]{:S(2)}, u32[]{:S(2)}) %all-to-all-start) | async-done | bytes 524320 | tf_op jit(solution)/shard_map/all_to_all | solution.py:120
  95.7 0.7 reshape.334
  96.4 1.1 copy.118
  97.5 0.4 copy.121
  98.0 2.7 %copy.122 = f32[4,32,64,32]{3,2,1,0:T(8,128)} copy(f32[4,32,64,32]{2,3,0,1:T(8,128)S(1)} %bitcast.166) | data formatting | bytes 2097152 | tf_op jit(solution)/shard_map/convert_element_type | solution.py:124
  100.7 3.6 %reshape.264 = f32[128,2048]{1,0:T(8,128)S(1)} reshape(f32[4,32,64,32]{3,2,1,0:T(8,128)} %copy.122) | data formatting | bytes 2097152 | tf_op jit(solution)/shard_map/convert_element_type | solution.py:124
  104.6 1.2 fusion
  105.8 0.3 copy.123
  106.1 1.7 %copy.124 = bf16[128,64,32]{1,2,0:T(8,128)(2,1)S(1)} copy(bf16[128,64,32]{0,2,1:T(8,128)(2,1)S(1)} %bitcast.174) | data formatting | bytes 1048576 | tf_op jit(solution)/shard_map/reshape | solution.py:159
  107.8 0.9 reshape.335
  108.6 9.7 %all_to_all.27 = bf16[4,2,32768]{2,1,0:T(2,128)(2,1)S(1)} all-to-all(bf16[4,2,32768]{2,1,0:T(2,128)(2,1)S(1)} %reshape.335), channel_id=1, replica_groups=mesh['member'=4,'space'=8] {'member'}, dimensions={0} | all-to-all | bytes 1048576 | tf_op jit(solution)/shard_map/all_to_all | solution.py:160
  118.3 0.7 reshape.336
  119.2 1.1 copy.126
  (70 shorter events, 4.0 us)
Async XLA Ops:
  0.0 62.4 %copy-start = (bf16[1,256,256]{2,1,0:T(8,128)(2,1)S(1)}, bf16[1,256,256]{2,1,0:T(8,128)(2,1)}, u32[]{:S(2)}) copy-start(bf16[1,256,256]{2,1,0:T(8,128)(2,1)} %param.17) | copy-start | bytes 393220
  0.0 13.2 %copy-start.4 = (bf16[1,256,256]{2,1,0:T(8,128)(2,1)S(1)}, bf16[1,256,256]{2,1,0:T(8,128)(2,1)}, u32[]{:S(2)}) copy-start(bf16[1,256,256]{2,1,0:T(8,128)(2,1)} %param.16) | copy-start | bytes 393220
  0.0 16.6 %collective-permute-start.1 = (s32[2,32]{1,0:T(2,128)}, s32[2,32]{1,0:T(2,128)S(1)}, u32[]{:S(2)}, u32[]{:S(2)}) collective-permute-start(s32[2,32]{1,0:T(2,128)} %param.22), channel_id=1, source_target_pairs={{1,0},{2,1},{3,2},{4,3},{5,4},{6,5},{7,6},{0,7},{9,8},{10,9},{11,1... | collective-permute-start | bytes 776 | tf_op jit(solution)/shard_map/ppermute | solution.py:22
  4.5 12.2 %collective-permute-start = (s32[2,32]{1,0:T(2,128)}, s32[2,32]{1,0:T(2,128)S(1)}, u32[]{:S(2)}, u32[]{:S(2)}) collective-permute-start(s32[2,32]{1,0:T(2,128)} %param.22), channel_id=1, source_target_pairs={{0,1},{1,2},{2,3},{3,4},{4,5},{5,6},{6,7},{7,0},{8,9},{9,10},{10,1... | collective-permute-start | bytes 776 | tf_op jit(solution)/shard_map/ppermute | solution.py:20
  8.0 11.7 %collective-permute-start.5 = (f32[1,1,129,128]{3,2,1,0:T(8,128)S(1)}, f32[1,1,129,128]{3,2,1,0:T(8,128)S(1)}, u32[]{:S(2)}, u32[]{:S(2)}) collective-permute-start(f32[1,1,129,128]{3,2,1,0:T(8,128)S(1)} %maximum_bitcast_fusion), channel_id=1, source_target_pairs={{8,0},{16,8},{24,16},{0,24},{9,1},{17,9},{25,17},{1,25},{10,2},{18... | collective-permute-start | bytes 198152 | tf_op jit(solution)/shard_map/ppermute | solution.py:22
  10.5 9.2 %collective-permute-start.4 = (f32[1,1,129,128]{3,2,1,0:T(8,128)S(1)}, f32[1,1,129,128]{3,2,1,0:T(8,128)S(1)}, u32[]{:S(2)}, u32[]{:S(2)}) collective-permute-start(f32[1,1,129,128]{3,2,1,0:T(8,128)S(1)} %maximum_bitcast_fusion), channel_id=1, source_target_pairs={{0,8},{8,16},{16,24},{24,0},{1,9},{9,17},{17,25},{25,1},{2,10},{10... | collective-permute-start | bytes 198152 | tf_op jit(solution)/shard_map/ppermute | solution.py:20
  13.2 3.5 %copy-start.1 = (f32[32,128,256]{2,1,0:T(8,128)}, f32[32,128,256]{2,1,0:T(8,128)S(1)}, u32[]{:S(2)}) copy-start(f32[32,128,256]{2,1,0:T(8,128)S(1)} %fusion.40) | copy-start | bytes 12582916
  13.2 0.8 copy-start.7
  13.2 3.4 %copy-start.6 = (bf16[1,256]{1,0:T(2,128)(2,1)S(1)}, bf16[1,256]{1,0:T(2,128)(2,1)}, u32[]{:S(2)}) copy-start(bf16[1,256]{1,0:T(2,128)(2,1)} %param.19) | copy-start | bytes 1540
  19.8 7.8 %collective-permute-start.7 = (f32[3,1,129,128]{3,2,1,0:T(8,128)S(1)}, f32[3,1,129,128]{3,2,1,0:T(8,128)S(1)}, u32[]{:S(2)}, u32[]{:S(2)}) collective-permute-start(f32[3,1,129,128]{3,2,1,0:T(8,128)S(1)} %pad_maximum_fusion.3), channel_id=1, source_target_pairs={{1,0},{2,1},{3,2},{4,3},{5,4},{6,5},{7,6},{0,7},{9,8},{10,9},{11,1... | collective-permute-start | bytes 594440 | tf_op jit(solution)/shard_map/ppermute | solution.py:22
  24.1 26.2 %collective-permute-start.3 = (bf16[32,32,256]{2,1,0:T(8,128)(2,1)}, bf16[32,32,256]{2,1,0:T(8,128)(2,1)}, u32[]{:S(2)}, u32[]{:S(2)}) collective-permute-start(bf16[32,32,256]{2,1,0:T(8,128)(2,1)} %get-tuple-element.18), channel_id=1, source_target_pairs={{1,0},{2,1},{3,2},{4,3},{5,4},{6,5},{7,6},{0,7},{9,8},{10,9},{11,1... | collective-permute-start | bytes 1572872 | tf_op jit(solution)/shard_map/ppermute | solution.py:22
  24.1 26.2 %collective-permute-start.2 = (bf16[32,32,256]{2,1,0:T(8,128)(2,1)}, bf16[32,32,256]{2,1,0:T(8,128)(2,1)}, u32[]{:S(2)}, u32[]{:S(2)}) collective-permute-start(bf16[32,32,256]{2,1,0:T(8,128)(2,1)} %get-tuple-element.17), channel_id=1, source_target_pairs={{0,1},{1,2},{2,3},{3,4},{4,5},{5,6},{6,7},{7,0},{8,9},{9,10},{10,1... | collective-permute-start | bytes 1572872 | tf_op jit(solution)/shard_map/ppermute | solution.py:20
  24.6 14.9 %collective-permute-start.6 = (f32[3,1,129,128]{3,2,1,0:T(8,128)S(1)}, f32[3,1,129,128]{3,2,1,0:T(8,128)S(1)}, u32[]{:S(2)}, u32[]{:S(2)}) collective-permute-start(f32[3,1,129,128]{3,2,1,0:T(8,128)S(1)} %pad_maximum_fusion.3), channel_id=1, source_target_pairs={{0,1},{1,2},{2,3},{3,4},{4,5},{5,6},{6,7},{7,0},{8,9},{9,10},{10,1... | collective-permute-start | bytes 594440 | tf_op jit(solution)/shard_map/ppermute | solution.py:20
  27.6 12.8 %collective-permute-start.9 = (bf16[1,129,128]{2,1,0:T(8,128)(2,1)S(1)}, bf16[1,129,128]{2,1,0:T(8,128)(2,1)S(1)}, u32[]{:S(2)}, u32[]{:S(2)}) collective-permute-start(bf16[1,129,128]{2,1,0:T(8,128)(2,1)S(1)} %fusion.37), channel_id=1, source_target_pairs={{1,0},{2,1},{3,2},{4,3},{5,4},{6,5},{7,6},{0,7},{9,8},{10,9},{11,1... | collective-permute-start | bytes 99080 | tf_op jit(solution)/shard_map/ppermute | solution.py:22
  39.5 5.2 %collective-permute-start.8 = (bf16[1,129,128]{2,1,0:T(8,128)(2,1)S(1)}, bf16[1,129,128]{2,1,0:T(8,128)(2,1)S(1)}, u32[]{:S(2)}, u32[]{:S(2)}) collective-permute-start(bf16[1,129,128]{2,1,0:T(8,128)(2,1)S(1)} %fusion.36), channel_id=1, source_target_pairs={{0,1},{1,2},{2,3},{3,4},{4,5},{5,6},{6,7},{7,0},{8,9},{9,10},{10,1... | collective-permute-start | bytes 99080 | tf_op jit(solution)/shard_map/ppermute | solution.py:20
  62.4 13.8 %copy-start.2 = (bf16[32,64,128]{2,1,0:T(8,128)(2,1)S(1)}, bf16[32,64,128]{2,1,0:T(8,128)(2,1)}, u32[]{:S(2)}) copy-start(bf16[32,64,128]{2,1,0:T(8,128)(2,1)} %param.14) | copy-start | bytes 1572868
  62.4 13.8 %copy-start.3 = (bf16[1,256,256]{2,1,0:T(8,128)(2,1)S(1)}, bf16[1,256,256]{2,1,0:T(8,128)(2,1)}, u32[]{:S(2)}) copy-start(bf16[1,256,256]{2,1,0:T(8,128)(2,1)} %param.18) | copy-start | bytes 393220
  62.4 13.8 %copy-start.5 = (bf16[256,64]{0,1:T(8,128)(2,1)S(1)}, bf16[256,64]{0,1:T(8,128)(2,1)}, u32[]{:S(2)}) copy-start(bf16[256,64]{0,1:T(8,128)(2,1)} %param.20) | copy-start | bytes 98308
  84.3 11.3 %all-to-all-start = ((bf16[4,2,32768]{2,1,0:T(2,128)(2,1)}), bf16[4,2,32768]{2,1,0:T(2,128)(2,1)S(1)}, u32[]{:S(2)}, u32[]{:S(2)}) async-start(bf16[4,2,32768]{2,1,0:T(2,128)(2,1)} %reshape.333), calls=%async_computation | async-start | bytes 1048576 | tf_op jit(solution)/shard_map/all_to_all | solution.py:120
where the time goes:
time: 121 us; the launch traced here: 120 us
  local copies, waits for them, and re-layouts  33.2 us (27%)
  matrix products  28.9 us (24%)
  waiting for transfers between devices  22.4 us (19%)
  starting transfers between devices  19.3 us (16%)
  blocking collectives  9.7 us (8%)
  other arithmetic  5.65 us (5%)
  between operations  1.21 us (1%)
    ppermute x5, starting transfers between devices, extended_2(): lax.ppermute(head, axis, [((i + 1) % count, i) for i in range(count)])  14 us
    dot_general x1, matrix products, body(): jnp.einsum('mnh,hk->mnk', rounded, receive_weight[0], preferred_element_t...  13.8 us
    ppermute x5, waiting for transfers between devices, extended_2(): lax.ppermute(tail, axis, [(i, (i + 1) % count) for i in range(count)])  12.4 us
    all_to_all x1, blocking collectives, body(): lax.all_to_all(analysed, 'member', split_axis=0, concat_axis=2, tiled=True)  9.7 us
    gather x4, local copies, waits for them, and re-layouts, body(): sender_rows = jnp.take(extended, edge_senders[:, slot_index], axis=1)  8.04 us
    all_to_all x1, waiting for transfers between devices, body(): lax.all_to_all(predicted_fields, 'member', split_axis=2, concat_axis=0, t...  7.03 us
    convert_element_type x3, local copies, waits for them, and re-layouts, body(): states = regional_states.reshape(ensemble, -1).astype(jnp.float32)  6.73 us
    dot_general x1, matrix products, body(): jnp.einsum('mnh,hc->mcn', stream.astype(jnp.bfloat16), decode_weight, pre...  4.93 us
  transfers between devices with their start and end apart: 11, of which 4 were waited for; matrix products, arithmetic and copies ran while one was open for 16% of the time, Pallas kernels for 0%

commit v1 on v0

v1 whole, which is shorter than its diff:
```python
import functools

import jax
import jax.numpy as jnp
from jax import lax
from jax.experimental import pallas as pl
from jax.experimental.pallas import tpu as pltpu
from jax.sharding import PartitionSpec as P

ITERS_NS = 5
EPSILON = 1e-05
F32 = jnp.float32
BF16 = jnp.bfloat16
FULL_PRECISION = lax.Precision.HIGHEST
VMEM = pl.BlockSpec(memory_space=pltpu.VMEM)
SMEM = pl.BlockSpec(memory_space=pltpu.SMEM)
TAIL = 16


def dot(left, right):
    return jnp.dot(left, right, preferred_element_type=F32)


def dot_t(left, right):
    return lax.dot_general(left, right, (((1,), (1,)), ((), ())), preferred_element_type=F32)


def split(value):
    high = value.astype(BF16)
    return high, (value - high.astype(F32)).astype(BF16)


def call(kernel, shapes, inputs, specs=None, scratch=(), flops=0):
    return pl.pallas_call(
        kernel,
        out_shape=shapes,
        in_specs=specs or [VMEM] * len(inputs),
        out_specs=jax.tree.map(lambda _: VMEM, shapes),
        scratch_shapes=list(scratch),
        compiler_params=pltpu.CompilerParams(vmem_limit_bytes=40 * 1024 * 1024),
        cost_estimate=pl.CostEstimate(flops=flops, bytes_accessed=1 << 20, transcendentals=0),
    )(*inputs)


def gram_kernel(perturbation, values, lists, out):
    ensemble = perturbation.shape[1]
    members = perturbation[0]
    wide = values[0].astype(F32)
    high, low = split(members.astype(F32) * wide[0:1])
    gram = dot_t(high, members) + dot_t(low, members)
    high, low = split(jnp.broadcast_to(wide[0:1] * wide[1:2], (TAIL, wide.shape[1])))
    forcing = dot_t(high, members) + dot_t(low, members)
    high, low = split(forcing)
    row = lax.broadcasted_iota(jnp.int32, forcing.shape, 0)
    tail = jnp.where(row == 0, high.astype(F32), jnp.where(row == 1, low.astype(F32), lists[...].astype(F32)))
    out[:ensemble, :] = gram.astype(BF16)
    out[ensemble:, :] = tail.astype(BF16)


def paired(fields, pair):
    half = fields.shape[0] // 2
    return jnp.concatenate([fields[pair], fields[pair + half]], axis=0)


def pick_kernel(halo_count, fields, own, before, after, to_before, to_after, column, scratch):
    half = fields.shape[0] // 2
    nodes = fields.shape[2]
    rows = own.shape[0]
    ensemble = rows - TAIL
    wanted_before = before[ensemble:, :].astype(F32)[3:4]
    wanted_after = after[ensemble:, :].astype(F32)[2:3]
    node = lax.broadcasted_iota(jnp.int32, (nodes, wanted_before.shape[1]), 0).astype(F32)
    chosen = jnp.concatenate(
        [(node == wanted).astype(F32).T[:halo_count].astype(BF16) for wanted in (wanted_before, wanted_after)],
        axis=0,
    )
    for pair in range(half):
        picked = dot_t(chosen, paired(fields, pair))
        scratch[pl.ds(pair, 2 * halo_count, stride=half), :] = picked
    size = halo_count * half
    to_before[:size, :] = scratch[:size, :].astype(BF16)
    to_after[:size, :] = scratch[size:, :].astype(BF16)
    to_before[size:, :] = after[...]
    to_after[size:, :] = before[...]
    column[:rows, :] = before[...]
    column[rows : 2 * rows, :] = own[...]
    column[2 * rows :, :] = after[...]


def block_diagonal(weight):
    zero = jnp.zeros_like(weight)
    return jnp.concatenate(
        [jnp.concatenate([weight, zero], axis=1), jnp.concatenate([zero, weight], axis=1)], axis=0
    )


def halves(wide, nodes, half, hidden):
    return jnp.concatenate(
        [wide[:, :hidden].reshape(nodes, half, hidden), wide[:, hidden:].reshape(nodes, half, hidden)], axis=1
    )


def own_kernel(fields, encode, send, receive, rearranged, sent, received, scratch):
    half = fields.shape[0] // 2
    nodes = fields.shape[2]
    hidden = encode.shape[1]
    for pair in range(half):
        scratch[pl.ds(pair, nodes, stride=half), :] = paired(fields, pair).astype(F32).T
    both = block_diagonal(encode[...])
    send_half = send[0] * 0.5
    receive_half = receive[0] * 0.5
    step_nodes = 16
    size = step_nodes * half

    def step(index, carry):
        start = pl.multiple_of(index * size, size)
        rows = scratch[pl.ds(start, size), :].astype(BF16)
        rearranged[pl.ds(start, size), :] = rows
        stream = halves(dot(rows, both), step_nodes, half, hidden)
        rounded = stream.astype(BF16).reshape(step_nodes * 2 * half, hidden)
        shape = (step_nodes, 2 * half, hidden)
        at = pl.ds(index * step_nodes, step_nodes)
        sent[at] = dot(rounded, send_half).astype(BF16).reshape(shape)
        received[at] = dot(rounded, receive_half).reshape(shape)
        return carry

    lax.fori_loop(0, nodes // step_nodes, step, 0)


def message_kernel(
    halo_count,
    edges,
    rearranged,
    sent,
    received,
    from_before,
    from_after,
    encode,
    send,
    update,
    gain,
    decode,
    out,
    extended,
    normed,
):
    nodes, members, hidden = sent.shape
    half = members // 2
    degree = edges.shape[0] // nodes
    regions = out.shape[0]
    channels = decode.shape[1]
    both = block_diagonal(encode[...])
    send_half = send[0] * 0.5
    extended[:nodes] = sent[...]
    for side, source in enumerate((from_before, from_after)):
        stream = halves(dot(source[: halo_count * half, :], both), halo_count, half, hidden)
        rounded = stream.astype(BF16).reshape(halo_count * members, hidden)
        start = nodes + side * halo_count
        extended[start : start + halo_count] = (
            dot(rounded, send_half).astype(BF16).reshape(halo_count, members, hidden)
        )
    zero = jnp.zeros_like(decode[...])
    decode_even = jnp.concatenate([decode[...], zero], axis=1)
    decode_odd = jnp.concatenate([zero, decode[...]], axis=1)
    step_nodes = 8
    per_region = nodes // regions // step_nodes
    gains = gain[...].astype(F32)

    def step(index, carry):
        base = index * step_nodes
        for offset in range(step_nodes):
            node = base + offset
            here = received[node]
            messages = jnp.zeros_like(here)
            for slot in range(degree):
                moved = extended[edges[node * degree + slot]].astype(F32) + here
                messages = messages + (moved + moved * jnp.tanh(moved))
            mean_square = jnp.mean(messages * messages, axis=-1, keepdims=True)
            scaled = messages * lax.rsqrt(mean_square + EPSILON) * gains
            normed[offset * members : (offset + 1) * members, :] = scaled.astype(BF16)
        start = pl.multiple_of(base * half, step_nodes * half)
        fields = rearranged[pl.ds(start, step_nodes * half), :]
        stream = halves(dot(fields, both), step_nodes, half, hidden).reshape(step_nodes * members, hidden)
        stream = stream + dot(normed[...], update[0])
        final = stream.astype(BF16).reshape(step_nodes // 2, 2, members, hidden)
        rows = step_nodes // 2 * members
        change = dot(final[:, 0].reshape(rows, hidden), decode_even) + dot(
            final[:, 1].reshape(rows, hidden), decode_odd
        )
        wide = fields.astype(F32).reshape(step_nodes // 2, 2, half, 2 * channels)
        even, odd = wide[:, 0], wide[:, 1]
        low = lax.broadcasted_iota(jnp.int32, even.shape, 2) < channels
        first = jnp.where(low, even, pltpu.roll(odd, channels, 2))
        second = jnp.where(low, pltpu.roll(even, channels, 2), odd)
        initial = jnp.concatenate([first, second], axis=1)
        forecast = (initial + change.reshape(initial.shape)).astype(BF16)
        region = index // per_region
        within = index % per_region
        width = 2 * channels
        for pair in range(step_nodes // 2):
            lane = pl.multiple_of((within * (step_nodes // 2) + pair) * width, width)
            out[region, :, pl.ds(lane, width)] = forecast[pair]
        return carry

    lax.fori_loop(0, nodes // step_nodes, step, 0)


def weights_kernel(slot_weight, own, before, after, from_before, from_after, up, down, out):
    rows, ensemble = own.shape
    near = from_before.shape[0] - rows
    total = None
    sources = [(up, 0), (up, rows), (up, 2 * rows), (before, 0), (own, 0), (after, 0)]
    sources += [(down, 0), (down, rows), (down, 2 * rows), (from_before, near), (from_after, near)]
    for slot, (source, start) in enumerate(sources):
        part = slot_weight[slot] * source[start : start + rows, :].astype(F32)
        total = part if total is None else total + part
    identity = (
        lax.broadcasted_iota(jnp.int32, (ensemble, ensemble), 0)
        == lax.broadcasted_iota(jnp.int32, (ensemble, ensemble), 1)
    ).astype(F32)
    full = functools.partial(jnp.dot, precision=FULL_PRECISION, preferred_element_type=F32)
    system = identity + total[:ensemble] / (ensemble - 1)
    squares = jnp.sum(jnp.sum(system * system, axis=1, keepdims=True), axis=0, keepdims=True)
    scaling = jnp.sqrt(squares)
    iterate = system / scaling
    correction = 1.5 * identity - 0.5 * iterate
    inverse = correction
    for _ in range(ITERS_NS - 1):
        iterate = full(iterate, correction)
        correction = 1.5 * identity - 0.5 * full(inverse, iterate)
        inverse = full(correction, inverse)
    tail = total[ensemble:]
    forcing = jnp.broadcast_to(tail[0:1] + tail[1:2], (8, ensemble))
    mean_weights = full(full(forcing, inverse), inverse)[0:1] / (scaling * (ensemble - 1))
    transform = inverse / jnp.sqrt(scaling) + mean_weights
    rest = (1.0 - jnp.sum(transform, axis=1, keepdims=True)) / ensemble
    high, low = split(transform + rest)
    out[:, :ensemble] = high
    out[:, ensemble:] = low


def analysis_kernel(weights, states, out):
    groups, members, width = states.shape
    ensemble = groups * members
    step_width = 256

    def step(index, carry):
        at = pl.ds(pl.multiple_of(index * step_width, step_width), step_width)
        columns = states[:, :, at].reshape(ensemble, step_width)
        analysed = dot(weights[...], jnp.concatenate([columns, columns], axis=0))
        out[:, :, at] = analysed.astype(BF16).reshape(groups, members, step_width)
        return carry

    lax.fori_loop(0, width // step_width, step, 0, unroll=True)


def output_kernel(analysed, out, scratch):
    regions, members, width = analysed.shape
    half = members // 2
    channels = out.shape[1]
    nodes = out.shape[2]
    low = lax.broadcasted_iota(jnp.int32, (half, 2 * channels), 1) < channels
    per_region = nodes // regions // 2
    for region in range(regions):
        for pair in range(per_region):
            block = analysed[region, :, pair * 2 * channels : (pair + 1) * 2 * channels].astype(F32)
            first, second = block[:half], block[half:]
            node = region * per_region * 2 + pair * 2
            scratch[node * half : (node + 1) * half, :] = jnp.where(low, first, pltpu.roll(second, channels, 1))
            scratch[(node + 1) * half : (node + 2) * half, :] = jnp.where(
                low, pltpu.roll(first, channels, 1), second
            )
    for pair in range(half):
        block = scratch[pl.ds(pair, nodes, stride=half), :].T.astype(BF16)
        out[pair] = block[:channels]
        out[pair + half] = block[channels:]


def slot_weights(neighbours, own_row, own_column, row_count, column_count):
    near_row = (neighbours // column_count - own_row + 1) % row_count - 1
    near_column = (neighbours % column_count - own_column + 2) % column_count - 2
    distance = (near_row * near_row + near_column * near_column).astype(F32)
    weights = 1.0 / (1.0 + distance / 2.0)
    slot = jnp.where(
        near_column == -2, 9, jnp.where(near_column == 2, 10, (near_row + 1) * 3 + near_column + 1)
    )
    slot_range = jnp.arange(11, dtype=jnp.int32)
    chosen = (slot[:, None] == slot_range[None, :]).astype(F32)
    return jnp.sum(weights[:, None] * chosen, axis=0) + (slot_range == 4).astype(F32)


def ring(value, axis, shift):
    count = lax.axis_size(axis)
    return lax.ppermute(value, axis, [(i, (i + shift) % count) for i in range(count)])


def body(
    initial_fields,
    encode_weight,
    send_weight,
    receive_weight,
    update_weight,
    norm_gain,
    decode_weight,
    edge_senders,
    halo_nodes,
    observed_perturbation,
    observed_values,
    region_neighbours,
):
    members, channels, nodes = initial_fields.shape
    hidden = encode_weight.shape[1]
    half = members // 2
    halo_count = halo_nodes.shape[1]
    ensemble = observed_perturbation.shape[1]
    groups = lax.axis_size("member")
    rows = ensemble + TAIL
    struct = jax.ShapeDtypeStruct
    lists = jnp.pad(halo_nodes.astype(BF16), ((2, TAIL - 4), (0, ensemble - halo_count)))
    own = call(
        gram_kernel, struct((rows, ensemble), BF16), (observed_perturbation, observed_values, lists), flops=1 << 24
    )
    before = ring(own, "space", 1)
    after = ring(own, "space", -1)
    rearranged, sent, received = call(
        own_kernel,
        (
            struct((nodes * half, 2 * channels), BF16),
            struct((nodes, members, hidden), BF16),
            struct((nodes, members, hidden), F32),
        ),
        (initial_fields, encode_weight, send_weight, receive_weight),
        scratch=[pltpu.VMEM((nodes * half, 2 * channels), F32)],
        flops=1 << 30,
    )
    size = halo_count * half
    to_before, to_after, column = call(
        functools.partial(pick_kernel, halo_count),
        (
            struct((size + rows, 2 * channels), BF16),
            struct((size + rows, 2 * channels), BF16),
            struct((3 * rows, ensemble), BF16),
        ),
        (initial_fields, own, before, after),
        scratch=[pltpu.VMEM((2 * size, 2 * channels), F32)],
        flops=1 << 27,
    )
    from_before = ring(to_after, "space", 1)
    from_after = ring(to_before, "space", -1)
    up = ring(column, "member", 1)
    down = ring(column, "member", -1)
    width = nodes // groups * channels
    predicted = call(
        functools.partial(message_kernel, halo_count),
        struct((groups, members, width), BF16),
        (
            edge_senders.reshape(-1),
            rearranged,
            sent,
            received,
            from_before,
            from_after,
            encode_weight,
            send_weight,
            update_weight,
            norm_gain,
            decode_weight,
        ),
        specs=[SMEM] + [VMEM] * 10,
        scratch=[
            pltpu.VMEM((nodes + 2 * halo_count, members, hidden), BF16),
            pltpu.VMEM((8 * members, hidden), BF16),
        ],
        flops=1 << 32,
    )
    states = lax.all_to_all(predicted, "member", split_axis=0, concat_axis=0, tiled=True)
    slot_weight = slot_weights(
        region_neighbours[0],
        lax.axis_index("member"),
        lax.axis_index("space"),
        lax.axis_size("member"),
        lax.axis_size("space"),
    )
    weights = call(
        weights_kernel,
        struct((ensemble, 2 * ensemble), BF16),
        (slot_weight, own, before, after, from_before, from_after, up, down),
        specs=[SMEM] + [VMEM] * 7,
        flops=1 << 30,
    )
    analysed = call(analysis_kernel, struct((groups, members, width), BF16), (weights, states), flops=1 << 28)
    returned = lax.all_to_all(analysed, "member", split_axis=0, concat_axis=0, tiled=True)
    return call(
        output_kernel,
        struct((members, channels, nodes), BF16),
        (returned,),
        scratch=[pltpu.VMEM((nodes * half, 2 * channels), F32)],
        flops=1 << 20,
    )


def solution(mesh):
    placed = (
        P("member", None, "space"),
        P(),
        P(),
        P(),
        P(),
        P(),
        P(),
        P("space", None),
        P(None, "space"),
        P(("member", "space"), None, None),
        P(("member", "space"), None, None),
        P(("member", "space"), None),
    )
    return jax.shard_map(
        body, mesh=mesh, in_specs=placed, out_specs=P("member", None, "space"), check_vma=False
    )
```

time: 121 us -> 73.2 us (0.60)
  the two profiles are of different devices: /device:TPU:0 before, /device:TPU:25 now
where the time goes in v1:
time: 73.2 us; the launch traced here: 72.5 us
  Pallas kernels  21.2 us (29%)
  waiting for transfers between devices  15.5 us (21%)
  local copies, waits for them, and re-layouts  12.2 us (17%)
  blocking collectives  10.8 us (15%)
  starting transfers between devices  9.96 us (14%)
  other arithmetic  2.72 us (4%)
    pallas_call x7, Pallas kernels, call(): pl.pallas_call(kernel, out_shape=shapes, in_specs=specs or [VMEM] * len(i...  21.2 us
    ppermute x6, waiting for transfers between devices, ring(): lax.ppermute(value, axis, [(i, (i + shift) % count) for i in range(count)])  15.5 us
    unnamed x34, local copies, waits for them, and re-layouts  12.1 us
    all_to_all x1, blocking collectives, body(): lax.all_to_all(analysed, 'member', split_axis=0, concat_axis=0, tiled=True)  10.8 us
    ppermute x6, starting transfers between devices, ring(): lax.ppermute(value, axis, [(i, (i + shift) % count) for i in range(count)])  6.49 us
    all_to_all x1, starting transfers between devices, body(): lax.all_to_all(predicted, 'member', split_axis=0, concat_axis=0, tiled=True)  3.47 us
  transfers between devices with their start and end apart: 7, of which 4 were waited for; matrix products, arithmetic and copies ran while one was open for 4% of the time, Pallas kernels for 9%

profile of v1, /device:TPU:25, one launch (start us, length us, event | category | flops | bytes accessed | tf_op | source)
XLA Modules:
  0.0 72.5 jit_solution(13653038241077699709)
XLA Ops:
  0.0 0.0 copy-start.15
  0.0 0.7 convert_element_type.18
  0.7 0.8 %copy-done.2 = bf16[1,128,256]{2,1,0:T(8,128)(2,1)S(1)} copy-done((bf16[1,128,256]{2,1,0:T(8,128)(2,1)S(1)}, bf16[1,128,256]{2,1,0:T(8,128)(2,1)}, u32[]{:S(2)}) %copy-start.2) | copy-done | bytes 65560
  1.6 0.7 copy-done.3
  2.2 0.2 shard_map.118.own
  2.5 0.7 %collective-permute-start.1 = (bf16[144,128]{1,0:T(8,128)(2,1)S(1)}, bf16[144,128]{1,0:T(8,128)(2,1)S(1)}, u32[]{:S(2)}, u32[]{:S(2)}) collective-permute-start(bf16[144,128]{1,0:T(8,128)(2,1)S(1)} %shard_map.118.own), channel_id=1, source_target_pairs={{0,7},{1,0},{2,1},{3,2},{4,3},{5,4},{6,5},{7,6},{8,15},{9,8},{10,9... | collective-permute-start | bytes 110600 | tf_op jit(solution)/shard_map/ppermute | solution.py:294
  3.2 2.9 %collective-permute-start = (bf16[144,128]{1,0:T(8,128)(2,1)S(1)}, bf16[144,128]{1,0:T(8,128)(2,1)S(1)}, u32[]{:S(2)}, u32[]{:S(2)}) collective-permute-start(bf16[144,128]{1,0:T(8,128)(2,1)S(1)} %shard_map.118.own), channel_id=1, source_target_pairs={{0,1},{1,2},{2,3},{3,4},{4,5},{5,6},{6,7},{7,0},{8,9},{9,10},{10,1... | collective-permute-start | bytes 110600 | tf_op jit(solution)/shard_map/ppermute | solution.py:294
  6.1 1.2 %compare_select_fusion.5 = (s32[8]{0:T(128)S(1)}, s32[8]{0:T(128)S(1)}, s32[8]{0:T(128)}) fusion(s32[]{:T(128)S(6)} %axis_index.25, s32[1,8]{1,0:T(1,128)} %param.23, s32[]{:T(128)S(6)} %axis_index.22), kind=kLoop, calls=%fused_computation.10 | loop fusion | flops 424 | bytes 136 | tf_op jit(solution)/shard_map/jit(_where)/select_n | solution.py:284
  7.3 1.0 %copy-done = bf16[32,64,128]{2,1,0:T(8,128)(2,1)S(1)} copy-done((bf16[32,64,128]{2,1,0:T(8,128)(2,1)S(1)}, bf16[32,64,128]{2,1,0:T(8,128)(2,1)}, u32[]{:S(2)}) %copy-start) | copy-done | bytes 524312
  8.4 0.9 %copy-done.4 = bf16[1,256,256]{2,1,0:T(8,128)(2,1)S(1)} copy-done((bf16[1,256,256]{2,1,0:T(8,128)(2,1)S(1)}, bf16[1,256,256]{2,1,0:T(8,128)(2,1)}, u32[]{:S(2)}) %copy-start.4) | copy-done | bytes 131096
  9.3 0.9 %copy-done.5 = bf16[1,256,256]{2,1,0:T(8,128)(2,1)S(1)} copy-done((bf16[1,256,256]{2,1,0:T(8,128)(2,1)S(1)}, bf16[1,256,256]{2,1,0:T(8,128)(2,1)}, u32[]{:S(2)}) %copy-start.5) | copy-done | bytes 131096
  10.2 0.8 %copy-done.8 = bf16[64,256]{1,0:T(8,128)(2,1)S(1)} copy-done((bf16[64,256]{1,0:T(8,128)(2,1)S(1)}, bf16[64,256]{1,0:T(8,128)(2,1)}, u32[]{:S(2)}) %copy-start.8) | copy-done | bytes 32792
  10.9 3.7 %shard_map.121 = (bf16[2048,128]{1,0:T(8,128)(2,1)S(1)}, bf16[128,32,256]{2,1,0:T(8,128)(2,1)S(1)}, f32[128,32,256]{2,1,0:T(8,128)S(1)}) custom-call(bf16[32,64,128]{2,1,0:T(8,128)(2,1)S(1)} %copy-done, bf16[64,256]{1,0:T(8,128)(2,1)S(1)} %copy-done.8, bf16[1,256,256]{2,1,0:T(8,128)(2,1)S(1)} %copy-done.5, bf16[1,256,256]{2,1,0:T(8,128)(2,1)S(1)} %copy-done.4), custom_call_target="tpu_custom_call" | custom-call | flops 1073741824 | bytes 1048576 | tf_op jit(solution)/shard_map/pallas_call | solution.py:34
  14.6 0.0 copy-start.11
  14.6 1.9 %copy-done.11 = f32[128,32,256]{2,1,0:T(8,128)} copy-done((f32[128,32,256]{2,1,0:T(8,128)}, f32[128,32,256]{2,1,0:T(8,128)S(1)}, u32[]{:S(2)}) %copy-start.11) | copy-done | bytes 4194328
  16.5 0.8 %copy-done.13 = bf16[2048,128]{1,0:T(8,128)(2,1)} copy-done((bf16[2048,128]{1,0:T(8,128)(2,1)}, bf16[2048,128]{1,0:T(8,128)(2,1)S(1)}, u32[]{:S(2)}) %copy-start.13) | copy-done | bytes 524312
  17.3 0.9 %copy.17.decode = bf16[256,64]{1,0:T(8,128)(2,1)S(1)} copy(bf16[256,64]{0,1:T(8,128)(2,1)} %param.18) | data formatting | bytes 65536 | tf_op args[6]
  18.2 0.0 copy-done.15
  18.2 0.1 copy.16
  18.3 0.1 reshape.109.edges
  18.4 0.0 collective-permute-done.1.after
  18.4 0.0 collective-permute-done.before
  18.5 0.0 copy-done.1
  18.5 0.6 shard_map.119
  19.0 0.1 collective-permute-start.2
  19.1 0.5 collective-permute-start.3
  19.6 0.7 add_divide_fusion
  20.3 2.3 %collective-permute-done.2.from_before = bf16[656,128]{1,0:T(8,128)(2,1)S(1)} collective-permute-done((bf16[656,128]{1,0:T(8,128)(2,1)S(1)}, bf16[656,128]{1,0:T(8,128)(2,1)S(1)}, u32[]{:S(2)}, u32[]{:S(2)}) %collective-permute-start.2) | collective-permute-done | bytes 167968 | tf_op jit(solution)/shard_map/ppermute | solution.py:294
  22.6 3.2 %collective-permute-done.3.from_after = bf16[656,128]{1,0:T(8,128)(2,1)S(1)} collective-permute-done((bf16[656,128]{1,0:T(8,128)(2,1)S(1)}, bf16[656,128]{1,0:T(8,128)(2,1)S(1)}, u32[]{:S(2)}, u32[]{:S(2)}) %collective-permute-start.3) | collective-permute-done | bytes 167968 | tf_op jit(solution)/shard_map/ppermute | solution.py:294
  25.7 0.0 copy-done.10
  25.7 0.0 copy-done.9
  25.7 0.0 copy-done.6
  25.8 0.0 copy-done.7
  25.8 0.0 copy-start.12
  25.8 2.2 %copy-done.12 = f32[128,32,256]{2,1,0:T(8,128)S(1)} copy-done((f32[128,32,256]{2,1,0:T(8,128)S(1)}, f32[128,32,256]{2,1,0:T(8,128)}, u32[]{:S(2)}) %copy-start.12) | copy-done | bytes 4194328
  28.0 1.0 %copy-done.14 = bf16[2048,128]{1,0:T(8,128)(2,1)S(1)} copy-done((bf16[2048,128]{1,0:T(8,128)(2,1)S(1)}, bf16[2048,128]{1,0:T(8,128)(2,1)}, u32[]{:S(2)}) %copy-start.14) | copy-done | bytes 524312
  29.0 11.9 %shard_map.122 = bf16[4,32,2048]{2,1,0:T(8,128)(2,1)} custom-call(s32[512]{0:T(512)S(1)} %reshape.109.edges, bf16[2048,128]{1,0:T(8,128)(2,1)S(1)} %copy-done.14, bf16[128,32,256]{2,1,0:T(8,128)(2,1)S(1)} %get-tuple-element.15.sent, f32[128,32,256]{2,1,0:T(8,128)S(1)} %copy-done.12, bf16[656,128]{1,0:T(8,128)(2,1)S(1)} %collective-permute-done.2.from_before, ...), custom_call_target="tpu_custom_call" | custom-call | flops 4294967296 | bytes 1048576 | tf_op jit(solution)/shard_map/pallas_call | solution.py:34
  40.9 3.5 %all-to-all-start = ((bf16[4,32,2048]{2,1,0:T(8,128)(2,1)}), bf16[4,32,2048]{2,1,0:T(8,128)(2,1)S(1)}, u32[]{:S(2)}, u32[]{:S(2)}) async-start(bf16[4,32,2048]{2,1,0:T(8,128)(2,1)} %shard_map.122), calls=%async_computation | async-start | bytes 1048576 | tf_op jit(solution)/shard_map/all_to_all | solution.py:376
  44.4 0.1 select_reduce_fusion
  44.5 2.3 %collective-permute-start.5 = (bf16[432,128]{1,0:T(8,128)(2,1)S(1)}, bf16[432,128]{1,0:T(8,128)(2,1)S(1)}, u32[]{:S(2)}, u32[]{:S(2)}) collective-permute-start(bf16[432,128]{1,0:T(8,128)(2,1)S(1)} %get-tuple-element.13), channel_id=1, source_target_pairs={{0,24},{8,0},{16,8},{24,16},{1,25},{9,1},{17,9},{25,17},{2,26},{10... | collective-permute-start | bytes 331784 | tf_op jit(solution)/shard_map/ppermute | solution.py:294
  46.8 0.0 collective-permute-start.4
  46.8 8.2 %collective-permute-done.5.down = bf16[432,128]{1,0:T(8,128)(2,1)S(1)} collective-permute-done((bf16[432,128]{1,0:T(8,128)(2,1)S(1)}, bf16[432,128]{1,0:T(8,128)(2,1)S(1)}, u32[]{:S(2)}, u32[]{:S(2)}) %collective-permute-start.5) | collective-permute-done | bytes 110624 | tf_op jit(solution)/shard_map/ppermute | solution.py:294
  55.0 1.8 %collective-permute-done.4.up = bf16[432,128]{1,0:T(8,128)(2,1)S(1)} collective-permute-done((bf16[432,128]{1,0:T(8,128)(2,1)S(1)}, bf16[432,128]{1,0:T(8,128)(2,1)S(1)}, u32[]{:S(2)}, u32[]{:S(2)}) %collective-permute-start.4) | collective-permute-done | bytes 110624 | tf_op jit(solution)/shard_map/ppermute | solution.py:294
  56.8 3.2 %shard_map.120.weights = bf16[128,256]{1,0:T(8,128)(2,1)S(1)} custom-call(f32[11]{0:T(128)S(1)} %fusion.3.slot_weight, bf16[144,128]{1,0:T(8,128)(2,1)S(1)} %shard_map.118.own, bf16[144,128]{1,0:T(8,128)(2,1)S(1)} %collective-permute-done.before, bf16[144,128]{1,0:T(8,128)(2,1)S(1)} %collective-permute-done.1.after, ...), custom_call_target="tpu_custom_call" | custom-call | flops 1073741824 | bytes 1048576 | tf_op jit(solution)/shard_map/pallas_call | solution.py:34
  60.1 0.0 all-to-all-done.states
  60.1 0.3 shard_map.123
  60.4 10.8 %all_to_all.10.analysed = bf16[4,32,2048]{2,1,0:T(8,128)(2,1)S(1)} all-to-all(bf16[4,32,2048]{2,1,0:T(8,128)(2,1)S(1)} %shard_map.123), channel_id=1, replica_groups=mesh['member'=4,'space'=8] {'member'}, dimensions={0} | all-to-all | bytes 1048576 | tf_op jit(solution)/shard_map/all_to_all | solution.py:392
  71.2 1.3 %shard_map.124 = bf16[32,64,128]{2,1,0:T(8,128)(2,1)} custom-call(bf16[4,32,2048]{2,1,0:T(8,128)(2,1)S(1)} %all_to_all.10.analysed), custom_call_target="tpu_custom_call" | custom-call | flops 1048576 | bytes 1048576 | tf_op jit(solution)/shard_map/pallas_call | solution.py:34
  (15 shorter events, 0.0 us)
Async XLA Ops:
  0.0 18.2 %copy-start.15 = (s32[128,4]{0,1:T(4,128)S(1)}, s32[128,4]{0,1:T(4,128)}, u32[]{:S(2)}) copy-start(s32[128,4]{0,1:T(4,128)} %param.19) | copy-start | bytes 6148
  0.0 25.7 %copy-start.10 = (bf16[1,256]{1,0:T(2,128)(2,1)S(1)}, bf16[1,256]{1,0:T(2,128)(2,1)}, u32[]{:S(2)}) copy-start(bf16[1,256]{1,0:T(2,128)(2,1)} %gain.1) | copy-start | bytes 1540
  0.7 0.8 %copy-start.2 = (bf16[1,128,256]{2,1,0:T(8,128)(2,1)S(1)}, bf16[1,128,256]{2,1,0:T(8,128)(2,1)}, u32[]{:S(2)}) copy-start(bf16[1,128,256]{2,1,0:T(8,128)(2,1)} %perturbation.1) | copy-start | bytes 196612
  1.6 0.7 copy-start.3
  2.2 23.5 %copy-start.9 = (bf16[64,256]{1,0:T(8,128)(2,1)S(1)}, bf16[64,256]{1,0:T(8,128)(2,1)}, u32[]{:S(2)}) copy-start(bf16[64,256]{1,0:T(8,128)(2,1)} %encode.3) | copy-start | bytes 98308
  2.5 16.0 %collective-permute-start.1 = (bf16[144,128]{1,0:T(8,128)(2,1)S(1)}, bf16[144,128]{1,0:T(8,128)(2,1)S(1)}, u32[]{:S(2)}, u32[]{:S(2)}) collective-permute-start(bf16[144,128]{1,0:T(8,128)(2,1)S(1)} %shard_map.118.own), channel_id=1, source_target_pairs={{0,7},{1,0},{2,1},{3,2},{4,3},{5,4},{6,5},{7,6},{8,15},{9,8},{10,9... | collective-permute-start | bytes 110600 | tf_op jit(solution)/shard_map/ppermute | solution.py:294
  3.2 15.3 %collective-permute-start = (bf16[144,128]{1,0:T(8,128)(2,1)S(1)}, bf16[144,128]{1,0:T(8,128)(2,1)S(1)}, u32[]{:S(2)}, u32[]{:S(2)}) collective-permute-start(bf16[144,128]{1,0:T(8,128)(2,1)S(1)} %shard_map.118.own), channel_id=1, source_target_pairs={{0,1},{1,2},{2,3},{3,4},{4,5},{5,6},{6,7},{7,0},{8,9},{9,10},{10,1... | collective-permute-start | bytes 110600 | tf_op jit(solution)/shard_map/ppermute | solution.py:294
  7.3 1.0 %copy-start = (bf16[32,64,128]{2,1,0:T(8,128)(2,1)S(1)}, bf16[32,64,128]{2,1,0:T(8,128)(2,1)}, u32[]{:S(2)}) copy-start(bf16[32,64,128]{2,1,0:T(8,128)(2,1)} %fields.3) | copy-start | bytes 1572868
  8.4 0.9 %copy-start.4 = (bf16[1,256,256]{2,1,0:T(8,128)(2,1)S(1)}, bf16[1,256,256]{2,1,0:T(8,128)(2,1)}, u32[]{:S(2)}) copy-start(bf16[1,256,256]{2,1,0:T(8,128)(2,1)} %receive.1) | copy-start | bytes 393220
  9.3 0.9 %copy-start.5 = (bf16[1,256,256]{2,1,0:T(8,128)(2,1)S(1)}, bf16[1,256,256]{2,1,0:T(8,128)(2,1)}, u32[]{:S(2)}) copy-start(bf16[1,256,256]{2,1,0:T(8,128)(2,1)} %send.3) | copy-start | bytes 393220
  10.2 0.8 %copy-start.8 = (bf16[64,256]{1,0:T(8,128)(2,1)S(1)}, bf16[64,256]{1,0:T(8,128)(2,1)}, u32[]{:S(2)}) copy-start(bf16[64,256]{1,0:T(8,128)(2,1)} %encode.3) | copy-start | bytes 98308
  10.9 7.5 %copy-start.1 = (bf16[32,64,128]{2,1,0:T(8,128)(2,1)S(1)}, bf16[32,64,128]{2,1,0:T(8,128)(2,1)}, u32[]{:S(2)}) copy-start(bf16[32,64,128]{2,1,0:T(8,128)(2,1)} %fields.3) | copy-start | bytes 1572868
  10.9 14.8 %copy-start.6 = (bf16[1,256,256]{2,1,0:T(8,128)(2,1)S(1)}, bf16[1,256,256]{2,1,0:T(8,128)(2,1)}, u32[]{:S(2)}) copy-start(bf16[1,256,256]{2,1,0:T(8,128)(2,1)} %send.3) | copy-start | bytes 393220
  10.9 14.8 %copy-start.7 = (bf16[1,256,256]{2,1,0:T(8,128)(2,1)S(1)}, bf16[1,256,256]{2,1,0:T(8,128)(2,1)}, u32[]{:S(2)}) copy-start(bf16[1,256,256]{2,1,0:T(8,128)(2,1)} %update.1) | copy-start | bytes 393220
  14.6 1.9 %copy-start.11 = (f32[128,32,256]{2,1,0:T(8,128)}, f32[128,32,256]{2,1,0:T(8,128)S(1)}, u32[]{:S(2)}) copy-start(f32[128,32,256]{2,1,0:T(8,128)S(1)} %get-tuple-element.16.received) | copy-start | bytes 12582916
  16.5 0.8 %copy-start.13 = (bf16[2048,128]{1,0:T(8,128)(2,1)}, bf16[2048,128]{1,0:T(8,128)(2,1)S(1)}, u32[]{:S(2)}) copy-start(bf16[2048,128]{1,0:T(8,128)(2,1)S(1)} %get-tuple-element.14.rearranged) | copy-start | bytes 1572868
  19.0 3.5 %collective-permute-start.2 = (bf16[656,128]{1,0:T(8,128)(2,1)S(1)}, bf16[656,128]{1,0:T(8,128)(2,1)S(1)}, u32[]{:S(2)}, u32[]{:S(2)}) collective-permute-start(bf16[656,128]{1,0:T(8,128)(2,1)S(1)} %get-tuple-element.11), channel_id=1, source_target_pairs={{0,1},{1,2},{2,3},{3,4},{4,5},{5,6},{6,7},{7,0},{8,9},{9,10},{10,1... | collective-permute-start | bytes 503816 | tf_op jit(solution)/shard_map/ppermute | solution.py:294
  19.1 6.6 %collective-permute-start.3 = (bf16[656,128]{1,0:T(8,128)(2,1)S(1)}, bf16[656,128]{1,0:T(8,128)(2,1)S(1)}, u32[]{:S(2)}, u32[]{:S(2)}) collective-permute-start(bf16[656,128]{1,0:T(8,128)(2,1)S(1)} %get-tuple-element.12), channel_id=1, source_target_pairs={{0,7},{1,0},{2,1},{3,2},{4,3},{5,4},{6,5},{7,6},{8,15},{9,8},{10,9... | collective-permute-start | bytes 503816 | tf_op jit(solution)/shard_map/ppermute | solution.py:294
  25.8 2.2 %copy-start.12 = (f32[128,32,256]{2,1,0:T(8,128)S(1)}, f32[128,32,256]{2,1,0:T(8,128)}, u32[]{:S(2)}) copy-start(f32[128,32,256]{2,1,0:T(8,128)} %copy-done.11) | copy-start | bytes 12582916
  28.0 1.0 %copy-start.14 = (bf16[2048,128]{1,0:T(8,128)(2,1)S(1)}, bf16[2048,128]{1,0:T(8,128)(2,1)}, u32[]{:S(2)}) copy-start(bf16[2048,128]{1,0:T(8,128)(2,1)} %copy-done.13) | copy-start | bytes 1572868
  40.9 19.2 %all-to-all-start = ((bf16[4,32,2048]{2,1,0:T(8,128)(2,1)}), bf16[4,32,2048]{2,1,0:T(8,128)(2,1)S(1)}, u32[]{:S(2)}, u32[]{:S(2)}) async-start(bf16[4,32,2048]{2,1,0:T(8,128)(2,1)} %shard_map.122), calls=%async_computation | async-start | bytes 1048576 | tf_op jit(solution)/shard_map/all_to_all | solution.py:376
  44.5 10.5 %collective-permute-start.5 = (bf16[432,128]{1,0:T(8,128)(2,1)S(1)}, bf16[432,128]{1,0:T(8,128)(2,1)S(1)}, u32[]{:S(2)}, u32[]{:S(2)}) collective-permute-start(bf16[432,128]{1,0:T(8,128)(2,1)S(1)} %get-tuple-element.13), channel_id=1, source_target_pairs={{0,24},{8,0},{16,8},{24,16},{1,25},{9,1},{17,9},{25,17},{2,26},{10... | collective-permute-start | bytes 331784 | tf_op jit(solution)/shard_map/ppermute | solution.py:294
  46.8 10.0 %collective-permute-start.4 = (bf16[432,128]{1,0:T(8,128)(2,1)S(1)}, bf16[432,128]{1,0:T(8,128)(2,1)S(1)}, u32[]{:S(2)}, u32[]{:S(2)}) collective-permute-start(bf16[432,128]{1,0:T(8,128)(2,1)S(1)} %get-tuple-element.13), channel_id=1, source_target_pairs={{0,8},{8,16},{16,24},{24,0},{1,9},{9,17},{17,25},{25,1},{2,10},{10... | collective-permute-start | bytes 331784 | tf_op jit(solution)/shard_map/ppermute | solution.py:294

commit v2 on v1

v2 whole, which is shorter than its diff:
```python
import functools

import jax
import jax.numpy as jnp
from jax import lax
from jax.experimental import pallas as pl
from jax.experimental.pallas import tpu as pltpu
from jax.sharding import PartitionSpec as P

ITERS_NS = 5
EPSILON = 1e-05
F32 = jnp.float32
BF16 = jnp.bfloat16
FULL_PRECISION = lax.Precision.HIGHEST
VMEM = pl.BlockSpec(memory_space=pltpu.VMEM)
SMEM = pl.BlockSpec(memory_space=pltpu.SMEM)
TAIL = 16
NOWHERE = -1048576.0
BATCH = 8
HBM = pl.BlockSpec(memory_space=pltpu.HBM)


def dot(left, right):
    return jnp.dot(left, right, preferred_element_type=F32)


def dot_t(left, right):
    return lax.dot_general(left, right, (((1,), (1,)), ((), ())), preferred_element_type=F32)


def split(value):
    high = value.astype(BF16)
    return high, (value - high.astype(F32)).astype(BF16)


def placed_in(space, *values):
    return tuple(pltpu.with_memory_space_constraint(value, space) for value in values)


def call(kernel, shapes, inputs, specs=None, outs=None, scratch=(), flops=0, aliases=None):
    return pl.pallas_call(
        kernel,
        out_shape=shapes,
        in_specs=specs or [VMEM] * len(inputs),
        out_specs=outs or jax.tree.map(lambda _: VMEM, shapes),
        scratch_shapes=list(scratch),
        input_output_aliases=aliases or {},
        compiler_params=pltpu.CompilerParams(vmem_limit_bytes=16 * 1024 * 1024),
        cost_estimate=pl.CostEstimate(flops=flops, bytes_accessed=1 << 20, transcendentals=0),
    )(*inputs)


def gram_kernel(perturbation, values, halo_nodes, out, held, held_values, held_lists, sems):
    copies = [
        pltpu.make_async_copy(source, target, sems.at[index])
        for index, (source, target) in enumerate(
            ((perturbation, held), (values, held_values), (halo_nodes, held_lists))
        )
    ]
    for copy in copies:
        copy.start()
    for copy in copies:
        copy.wait()
    ensemble = held.shape[1]
    members = held[0]
    wide = held_values[0].astype(F32)
    high, low = split(members.astype(F32) * wide[0:1])
    gram = dot_t(high, members) + dot_t(low, members)
    high, low = split(jnp.broadcast_to(wide[0:1] * wide[1:2], (TAIL, wide.shape[1])))
    forcing = dot_t(high, members) + dot_t(low, members)
    high, low = split(forcing)
    lists = held_lists[...].astype(F32)
    lists = jnp.concatenate([lists, jnp.zeros((2, ensemble - lists.shape[1]), F32)], axis=1)
    row = lax.broadcasted_iota(jnp.int32, forcing.shape, 0)
    tail = jnp.where(row == 0, high.astype(F32), low.astype(F32))
    tail = jnp.where(row == 2, lists[0:1], jnp.where(row == 3, lists[1:2], tail))
    out[:ensemble, :] = gram.astype(BF16)
    out[ensemble:, :] = tail.astype(BF16)


def paired(fields, pair):
    half = fields.shape[0] // 2
    return jnp.concatenate([fields[pair], fields[pair + half]], axis=0)


def pick_kernel(halo_count, columns, before, after, up, down, to_before, to_after, scratch):
    half, nodes, _ = columns.shape
    rows = before.shape[0]
    ensemble = rows - TAIL
    wanted_before = before[ensemble:, :].astype(F32)[3:4]
    wanted_after = after[ensemble:, :].astype(F32)[2:3]
    node = lax.broadcasted_iota(jnp.int32, (nodes, wanted_before.shape[1]), 0).astype(F32)
    chosen = jnp.concatenate(
        [(node == wanted).astype(F32).T[:halo_count].astype(BF16) for wanted in (wanted_before, wanted_after)],
        axis=0,
    )
    for pair in range(half):
        picked = dot(chosen, columns[pair])
        scratch[pl.ds(pair, 2 * halo_count, stride=half), :] = picked
    size = halo_count * half
    to_before[:size, :] = scratch[:size, :].astype(BF16)
    to_after[:size, :] = scratch[size:, :].astype(BF16)
    for target, beyond in ((to_before, after), (to_after, before)):
        for index, source in enumerate((beyond, up, down)):
            target[size + index * rows : size + (index + 1) * rows, :] = source[...]


def block_diagonal(weight):
    zero = jnp.zeros_like(weight)
    return jnp.concatenate(
        [jnp.concatenate([weight, zero], axis=1), jnp.concatenate([zero, weight], axis=1)], axis=0
    )


def halves(wide, nodes, half, hidden):
    return jnp.concatenate(
        [wide[:, :hidden].reshape(nodes, half, hidden), wide[:, hidden:].reshape(nodes, half, hidden)], axis=1
    )


def own_kernel(partners, fields, encode, send, receive, columns, rearranged, sent, received, held, held_encode, held_send, held_receive, scratch, sems):
    half = fields.shape[0] // 2
    nodes = fields.shape[2]
    hidden = encode.shape[1]
    copies = [
        pltpu.make_async_copy(source, target, sems.at[index])
        for index, (source, target) in enumerate(
            ((fields, held), (encode, held_encode), (send, held_send), (receive, held_receive))
        )
    ]
    for copy in copies:
        copy.start()
    for copy in copies:
        copy.wait()
    for pair in range(half):
        column = paired(held, pair).astype(F32).T
        scratch[pl.ds(pair, nodes, stride=half), :] = column
        columns[pair] = column.astype(BF16)
    both = block_diagonal(held_encode[...])
    send_half = held_send[0] * 0.5
    receive_half = held_receive[0] * 0.5
    sent[nodes] = jnp.full(sent.shape[1:], NOWHERE, BF16)
    step_nodes = 32
    size = step_nodes * half
    for index in range(nodes // step_nodes):
        rows = scratch[index * size : (index + 1) * size, :].astype(BF16)
        rearranged[index * size : (index + 1) * size, :] = rows
        stream = halves(dot(rows, both), step_nodes, half, hidden)
        rounded = stream.astype(BF16).reshape(step_nodes * 2 * half, hidden)
        shape = (step_nodes, 2 * half, hidden)
        at = slice(index * step_nodes, (index + 1) * step_nodes)
        sent[at] = dot(rounded, send_half).astype(BF16).reshape(shape)
        received[at] = dot(rounded, receive_half).reshape(shape)


def activated(sender, here):
    moved = sender.astype(F32) + here
    return moved + moved * jnp.tanh(moved)


def own_message_kernel(halo_total, edges, sent, received, messages, halo_edges, halo_edge_count):
    nodes, members, hidden = received.shape
    degree = edges.shape[0]
    group = 4

    def step(index, count):
        for offset in range(group):
            node = index * group + offset
            here = received[node]
            total = None
            for slot in range(degree):
                sender = edges[slot, node]
                value = activated(sent[jnp.minimum(sender, nodes)], here)
                total = value if total is None else total + value
                halo_edges[count] = node * halo_total + sender - nodes
                count = count + jnp.where(sender < nodes, 0, 1)
            messages[node] = total
        return count

    count = lax.fori_loop(0, nodes // group, step, 0)
    for index in range(BATCH):
        halo_edges[count + index] = nodes * halo_total
    halo_edge_count[0] = count
    messages[nodes] = jnp.zeros((members, hidden), F32)


def message_kernel(
    halo_count,
    partners,
    halo_edges,
    halo_edge_count,
    rearranged,
    received,
    started,
    from_before,
    from_after,
    encode,
    send,
    update,
    gain,
    decode,
    *outputs,
):
    *outs, messages, extended = outputs
    nodes, members, hidden = received.shape
    half = members // 2
    regions = len(outs)
    channels = decode.shape[0]
    both = block_diagonal(encode[...])
    send_half = send[0] * 0.5
    for side, source in enumerate((from_before, from_after)):
        stream = halves(dot(source[: halo_count * half, :], both), halo_count, half, hidden)
        rounded = stream.astype(BF16).reshape(halo_count * members, hidden)
        extended[side * halo_count : (side + 1) * halo_count] = (
            dot(rounded, send_half).astype(BF16).reshape(halo_count, members, hidden)
        )

    def batch(index, carry):
        found = []
        for offset in range(BATCH):
            code = halo_edges[index * BATCH + offset]
            node = code // (2 * halo_count)
            here = received[jnp.minimum(node, nodes - 1)]
            found.append((node, activated(extended[code % (2 * halo_count)], here)))
        for node, value in found:
            messages[node] = messages[node] + value
        return carry

    lax.fori_loop(0, (halo_edge_count[0] + BATCH - 1) // BATCH, batch, 0)
    zero = jnp.zeros_like(decode[...])
    decode_even = jnp.concatenate([decode[...], zero], axis=0)
    decode_odd = jnp.concatenate([zero, decode[...]], axis=0)
    gains = gain[...].astype(F32)
    chunk = nodes // regions
    pairs = chunk // 2
    width = 2 * channels
    average = jnp.full((hidden, width), 1.0 / hidden, BF16)
    low = lax.broadcasted_iota(jnp.int32, (pairs, half, width), 2) < channels
    for index, out in enumerate(outs):
        base = partners[index] * chunk
        fields = rearranged[pl.ds(pl.multiple_of(base * half, chunk * half), chunk * half), :]
        stream = halves(dot(fields, both), chunk, half, hidden).reshape(chunk * members, hidden)
        message = messages[pl.ds(base, chunk)].reshape(chunk * members, hidden)
        mean_square = dot((message * message).astype(BF16), average)
        scale = lax.rsqrt(mean_square + EPSILON)
        scaled = message * jnp.concatenate([scale] * (hidden // width), axis=1) * gains
        stream = stream + dot(scaled.astype(BF16), update[0])
        final = stream.astype(BF16).reshape(pairs, 2, members, hidden)
        rows = pairs * members
        change = dot_t(final[:, 0].reshape(rows, hidden), decode_even) + dot_t(
            final[:, 1].reshape(rows, hidden), decode_odd
        )
        wide = fields.astype(F32).reshape(pairs, 2, half, width)
        even, odd = wide[:, 0], wide[:, 1]
        first = jnp.where(low, even, pltpu.roll(odd, channels, 2))
        second = jnp.where(low, pltpu.roll(even, channels, 2), odd)
        initial = jnp.concatenate([first, second], axis=1)
        forecast = (initial + change.reshape(initial.shape)).astype(BF16)
        for pair in range(pairs):
            out[:, pair * width : (pair + 1) * width] = forecast[pair]


def weights_kernel(partners, neighbours, own, before, after, up, down, from_before, from_after, out):
    rows, ensemble = own.shape
    first = from_before.shape[0] - 3 * rows
    row_count = (partners.shape[0] - 2) // 2
    column_count = partners[partners.shape[0] - 1]
    own_row, own_column = partners[0], partners[partners.shape[0] - 2]
    offsets = []
    for index in range(neighbours.shape[1]):
        region = neighbours[0, index]
        near_row = (region // column_count - own_row + 1 + row_count) % row_count - 1
        near_column = (region % column_count - own_column + 2 + column_count) % column_count - 2
        offsets.append((near_row, near_column))
    sources = {(0, -1): (before, 0), (0, 1): (after, 0), (-1, 0): (up, 0), (1, 0): (down, 0)}
    for column, source in ((-1, from_before), (1, from_after)):
        for index, place in enumerate(((0, 2 * column), (-1, column), (1, column))):
            sources[place] = (source, first + index * rows)
    total = own[...].astype(F32)
    for place, (source, start) in sources.items():
        weight = 0.0
        for near_row, near_column in offsets:
            here = jnp.logical_and(near_row == place[0], near_column == place[1])
            weight = weight + jnp.where(here, 1.0 / (1.0 + (place[0] ** 2 + place[1] ** 2) / 2.0), 0.0)
        total = total + weight * source[start : start + rows, :].astype(F32)
    identity = (
        lax.broadcasted_iota(jnp.int32, (ensemble, ensemble), 0)
        == lax.broadcasted_iota(jnp.int32, (ensemble, ensemble), 1)
    ).astype(F32)
    full = functools.partial(jnp.dot, precision=FULL_PRECISION, preferred_element_type=F32)
    system = identity + total[:ensemble] / (ensemble - 1)
    squares = jnp.sum(jnp.sum(system * system, axis=1, keepdims=True), axis=0, keepdims=True)
    scaling = jnp.sqrt(squares)
    iterate = system / scaling
    correction = 1.5 * identity - 0.5 * iterate
    inverse = correction
    for _ in range(ITERS_NS - 1):
        iterate = full(iterate, correction)
        correction = 1.5 * identity - 0.5 * full(inverse, iterate)
        inverse = full(correction, inverse)
    tail = total[ensemble:]
    forcing = jnp.broadcast_to(tail[0:1] + tail[1:2], (8, ensemble))
    mean_weights = full(full(forcing, inverse), inverse)[0:1] / (scaling * (ensemble - 1))
    transform = inverse / jnp.sqrt(scaling) + mean_weights
    rest = (1.0 - jnp.sum(transform, axis=1, keepdims=True)) / ensemble
    members = ensemble // row_count
    to_rows = lax.broadcasted_iota(jnp.int32, (ensemble, ensemble), 0)
    to_columns = lax.broadcasted_iota(jnp.int32, (ensemble, ensemble), 1)
    wanted_rows, wanted_columns = to_rows % members, to_columns % members
    for index in range(row_count):
        target, origin = partners[index] * members, partners[row_count + index] * members
        wanted_rows = wanted_rows + jnp.where(to_rows // members == index, target, 0)
        wanted_columns = wanted_columns + jnp.where(to_columns // members == index, origin, 0)
    by_row = (to_columns == wanted_rows).astype(F32).astype(BF16)
    by_column = (to_rows == wanted_columns).astype(F32).astype(BF16)
    for index, part in enumerate(split(transform + rest)):
        moved = dot(dot(by_row, part).astype(BF16), by_column)
        out[:, index * ensemble : (index + 1) * ensemble] = moved.astype(BF16)


def analysis_kernel(weights, *refs):
    count = len(refs) // 2
    pieces, outs = refs[:count], refs[count:]
    members, width = pieces[0].shape
    step_width = 512
    for start in range(0, width, step_width):
        columns = [piece[:, start : start + step_width] for piece in pieces]
        analysed = dot(weights[...], jnp.concatenate(columns * 2, axis=0)).astype(BF16)
        for index, out in enumerate(outs):
            out[:, start : start + step_width] = analysed[index * members : (index + 1) * members]


def output_kernel(partners, *refs):
    *pieces, out, held, scratch = refs
    count = len(pieces)
    members, channels, nodes = out.shape
    half = members // 2
    low = lax.broadcasted_iota(jnp.int32, (half, 2 * channels), 1) < channels
    chunk = nodes // count
    for index, piece in enumerate(pieces):
        held[partners[count + index]] = piece[...]
    for region in range(count):
        for pair in range(chunk // 2):
            block = held[region, :, pair * 2 * channels : (pair + 1) * 2 * channels].astype(F32)
            first, second = block[:half], block[half:]
            row = (region * chunk + 2 * pair) * half
            scratch[row : row + half, :] = jnp.where(low, first, pltpu.roll(second, channels, 1))
            scratch[row + half : row + 2 * half, :] = jnp.where(low, pltpu.roll(first, channels, 1), second)
    for pair in range(half):
        block = scratch[pl.ds(pair, nodes, stride=half), :].T.astype(BF16)
        out[pair] = block[:channels]
        out[pair + half] = block[channels:]


def ring(value, axis, shift):
    count = lax.axis_size(axis)
    return lax.ppermute(value, axis, [(i, (i + shift) % count) for i in range(count)])


def partner_exchange(axis):
    count = lax.axis_size(axis)
    own = lax.axis_index(axis)
    steps = jnp.arange(count, dtype=jnp.int32)
    paired_up = count & (count - 1) == 0
    if paired_up:
        targets = origins = own ^ steps
    else:
        targets, origins = (own + steps) % count, (own - steps) % count

    def exchange(pieces):
        return [pieces[0]] + [
            lax.ppermute(
                piece, axis, [(i, i ^ step if paired_up else (i + step) % count) for i in range(count)]
            )
            for step, piece in enumerate(pieces)
            if step
        ]

    place = jnp.stack([lax.axis_index("space"), jnp.int32(lax.axis_size("space"))])
    return jnp.concatenate([targets, origins, place]), exchange


def body(
    initial_fields,
    encode_weight,
    send_weight,
    receive_weight,
    update_weight,
    norm_gain,
    decode_weight,
    edge_senders,
    halo_nodes,
    observed_perturbation,
    observed_values,
    region_neighbours,
):
    members, channels, nodes = initial_fields.shape
    hidden = encode_weight.shape[1]
    half = members // 2
    halo_count = halo_nodes.shape[1]
    ensemble = observed_perturbation.shape[1]
    groups = lax.axis_size("member")
    rows = ensemble + TAIL
    struct = jax.ShapeDtypeStruct
    own = call(
        gram_kernel,
        struct((rows, ensemble), BF16),
        placed_in(pltpu.HBM, observed_perturbation, observed_values, halo_nodes),
        specs=[HBM] * 3,
        scratch=[
            pltpu.VMEM(observed_perturbation.shape, BF16),
            pltpu.VMEM(observed_values.shape, BF16),
            pltpu.VMEM(halo_nodes.shape, jnp.int32),
            pltpu.SemaphoreType.DMA((3,)),
        ],
        flops=1 << 24,
    )
    before = ring(own, "space", 1)
    after = ring(own, "space", -1)
    up = ring(own, "member", 1)
    down = ring(own, "member", -1)
    partners, exchange = partner_exchange("member")
    columns, rearranged, sent, received = call(
        own_kernel,
        (
            struct((half, nodes, 2 * channels), BF16),
            struct((nodes * half, 2 * channels), BF16),
            pltpu.VMEM((nodes + 1, members, hidden), BF16),
            pltpu.VMEM((nodes, members, hidden), F32),
        ),
        (partners, *placed_in(pltpu.HBM, initial_fields, encode_weight, send_weight, receive_weight)),
        specs=[SMEM] + [HBM] * 4,
        scratch=[
            pltpu.VMEM(initial_fields.shape, BF16),
            pltpu.VMEM(encode_weight.shape, BF16),
            pltpu.VMEM(send_weight.shape, BF16),
            pltpu.VMEM(receive_weight.shape, BF16),
            pltpu.VMEM((nodes * half, 2 * channels), F32),
            pltpu.SemaphoreType.DMA((4,)),
        ],
        flops=1 << 30,
    )
    size = halo_count * half
    to_before, to_after = call(
        functools.partial(pick_kernel, halo_count),
        (struct((size + 3 * rows, 2 * channels), BF16),) * 2,
        (columns, before, after, up, down),
        scratch=[pltpu.VMEM((2 * size, 2 * channels), F32)],
        flops=1 << 27,
    )
    from_before = ring(to_after, "space", 1)
    from_after = ring(to_before, "space", -1)
    edges = edge_senders.T
    started, halo_edges, halo_edge_count = call(
        functools.partial(own_message_kernel, 2 * halo_count),
        (
            pltpu.VMEM((nodes + 1, members, hidden), F32),
            struct((edges.size + BATCH,), jnp.int32),
            struct((1,), jnp.int32),
        ),
        (edges, *placed_in(pltpu.VMEM, sent, received)),
        specs=[SMEM, VMEM, VMEM],
        outs=(VMEM, SMEM, SMEM),
        flops=1 << 31,
    )
    width = nodes // groups * channels
    piece = struct((members, width), BF16)
    *predicted, _ = call(
        functools.partial(message_kernel, halo_count),
        (piece,) * groups + (struct(started.shape, F32),),
        (
            partners,
            halo_edges,
            halo_edge_count,
            rearranged,
            *placed_in(pltpu.VMEM, received, started),
            from_before,
            from_after,
            encode_weight,
            send_weight,
            update_weight,
            norm_gain,
            decode_weight.T,
        ),
        specs=[SMEM] * 3 + [VMEM] * 10,
        scratch=[pltpu.VMEM((2 * halo_count, members, hidden), BF16)],
        flops=1 << 32,
        aliases={5: groups},
    )
    states = exchange(predicted)
    weights = call(
        weights_kernel,
        struct((ensemble, 2 * ensemble), BF16),
        (partners, region_neighbours, own, before, after, up, down, from_before, from_after),
        specs=[SMEM] * 2 + [VMEM] * 7,
        flops=1 << 30,
    )
    analysed = call(
        analysis_kernel,
        (piece,) * groups,
        (weights, *states),
        flops=1 << 28,
    )
    returned = exchange(analysed)
    return call(
        output_kernel,
        struct((members, channels, nodes), BF16),
        (partners, *returned),
        specs=[SMEM] + [VMEM] * groups,
        scratch=[
            pltpu.VMEM((groups, members, width), BF16),
            pltpu.VMEM((nodes * half, 2 * channels), F32),
        ],
        flops=1 << 20,
    )


def solution(mesh):
    placed = (
        P("member", None, "space"),
        P(),
        P(),
        P(),
        P(),
        P(),
        P(),
        P("space", None),
        P(None, "space"),
        P(("member", "space"), None, None),
        P(("member", "space"), None, None),
        P(("member", "space"), None),
    )
    return jax.shard_map(
        body, mesh=mesh, in_specs=placed, out_specs=P("member", None, "space"), check_vma=False
    )
```

time: 73.2 us -> 49.6 us (0.68)
  the two profiles are of different devices: /device:TPU:25 before, /device:TPU:0 now
where the time goes in v2:
time: 49.6 us
  Pallas kernels  23 us (46%)
  starting transfers between devices  17.4 us (35%)
  waiting for transfers between devices  8.89 us (18%)
    pallas_call x8, Pallas kernels, call(): pl.pallas_call(kernel, out_shape=shapes, in_specs=specs or [VMEM] * len(i...  23 us
    ppermute x6, starting transfers between devices, ring(): lax.ppermute(value, axis, [(i, (i + shift) % count) for i in range(count)])  10.3 us
    ppermute x6, starting transfers between devices, exchange(): lax.ppermute(piece, axis, [(i, i ^ step if paired_up else (i + step) % co...  7.11 us
    ppermute x6, waiting for transfers between devices, exchange(): lax.ppermute(piece, axis, [(i, i ^ step if paired_up else (i + step) % co...  6.51 us
    ppermute x6, waiting for transfers between devices, ring(): lax.ppermute(value, axis, [(i, (i + shift) % count) for i in range(count)])  2.38 us
  transfers between devices with their start and end apart: 12, of which 6 were waited for; matrix products, arithmetic and copies ran while one was open for 0% of the time, Pallas kernels for 25%

profile of v2, /device:TPU:0, one launch (start us, length us, event | category | flops | bytes accessed | tf_op | source)
XLA Modules:
  0.0 49.6 jit_solution(12314216878943499886)
XLA Ops:
  0.0 0.0 copy-start.4
  0.0 1.1 %shard_map.118.own = bf16[144,128]{1,0:T(8,128)(2,1)S(1)} custom-call(bf16[1,128,256]{2,1,0:T(8,128)(2,1)} %perturbation.1, bf16[1,2,256]{2,1,0:T(2,128)(2,1)} %values.1, s32[2,32]{1,0:T(2,128)} %halo_nodes.1), custom_call_target="tpu_custom_call" | custom-call | flops 16777216 | bytes 1048576 | tf_op jit(solution)/shard_map/pallas_call | solution.py:41
  1.1 3.9 %collective-permute-start.3 = (bf16[144,128]{1,0:T(8,128)(2,1)S(1)}, bf16[144,128]{1,0:T(8,128)(2,1)S(1)}, u32[]{:S(2)}, u32[]{:S(2)}) collective-permute-start(bf16[144,128]{1,0:T(8,128)(2,1)S(1)} %shard_map.118.own), channel_id=1, source_target_pairs={{0,24},{8,0},{16,8},{24,16},{1,25},{9,1},{17,9},{25,17},{2,26},{10... | collective-permute-start | bytes 110600 | tf_op jit(solution)/shard_map/ppermute | solution.py:357
  5.1 0.0 collective-permute-start.2
  5.1 2.8 %collective-permute-start.1 = (bf16[144,128]{1,0:T(8,128)(2,1)S(1)}, bf16[144,128]{1,0:T(8,128)(2,1)S(1)}, u32[]{:S(2)}, u32[]{:S(2)}) collective-permute-start(bf16[144,128]{1,0:T(8,128)(2,1)S(1)} %shard_map.118.own), channel_id=1, source_target_pairs={{0,7},{1,0},{2,1},{3,2},{4,3},{5,4},{6,5},{7,6},{8,15},{9,8},{10,9... | collective-permute-start | bytes 110600 | tf_op jit(solution)/shard_map/ppermute | solution.py:357
  7.8 0.0 collective-permute-start
  7.8 0.1 pad_add_fusion.partners
  7.9 3.9 %shard_map.119 = (bf16[16,128,128]{2,1,0:T(8,128)(2,1)S(1)}, bf16[2048,128]{1,0:T(8,128)(2,1)S(1)}, bf16[129,32,256]{2,1,0:T(8,128)(2,1)S(1)}, f32[128,32,256]{2,1,0:T(8,128)S(1)}) custom-call(s32[10]{0:T(128)S(1)} %pad_add_fusion.partners, bf16[32,64,128]{2,1,0:T(8,128)(2,1)} %fields.1, bf16[64,256]{1,0:T(8,128)(2,1)} %encode.3, bf16[1,256,256]{2,1,0:T(8,128)(2,1)} %send.3, ...), custom_call_target="tpu_custom_call" | custom-call | flops 1073741824 | bytes 1048576 | tf_op jit(solution)/shard_map/pallas_call | solution.py:41
  11.8 0.0 collective-permute-done.3.down
  11.8 0.0 collective-permute-done.2.up
  11.8 0.0 collective-permute-done.1.after
  11.8 1.2 %collective-permute-done.before = bf16[144,128]{1,0:T(8,128)(2,1)S(1)} collective-permute-done((bf16[144,128]{1,0:T(8,128)(2,1)S(1)}, bf16[144,128]{1,0:T(8,128)(2,1)S(1)}, u32[]{:S(2)}, u32[]{:S(2)}) %collective-permute-start) | collective-permute-done | bytes 36896 | tf_op jit(solution)/shard_map/ppermute | solution.py:357
  13.0 0.0 copy-start
  13.0 0.0 copy-start.1
  13.0 0.0 copy-start.2
  13.0 0.0 copy-start.3
  13.0 0.0 copy-start.5
  13.0 0.4 shard_map.120
  13.5 0.1 collective-permute-start.4
  13.5 3.5 %collective-permute-start.5 = (bf16[944,128]{1,0:T(8,128)(2,1)S(1)}, bf16[944,128]{1,0:T(8,128)(2,1)S(1)}, u32[]{:S(2)}, u32[]{:S(2)}) collective-permute-start(bf16[944,128]{1,0:T(8,128)(2,1)S(1)} %get-tuple-element.24), channel_id=1, source_target_pairs={{0,7},{1,0},{2,1},{3,2},{4,3},{5,4},{6,5},{7,6},{8,15},{9,8},{10,9... | collective-permute-start | bytes 725000 | tf_op jit(solution)/shard_map/ppermute | solution.py:357
  17.1 0.0 copy-done.4
  17.1 4.8 %shard_map.122 = (f32[129,32,256]{2,1,0:T(8,128)S(1)}, s32[520]{0:T(1024)S(1)}, s32[1]{0:T(128)}) custom-call(s32[4,128]{1,0:T(4,128)S(1)} %bitcast.4, bf16[129,32,256]{2,1,0:T(8,128)(2,1)S(1)} %get-tuple-element.25.sent, f32[128,32,256]{2,1,0:T(8,128)S(1)} %get-tuple-element.26.received), custom_call_target="tpu_custom_call" | custom-call | flops 2147483648 | bytes 1048576 | tf_op jit(solution)/shard_map/pallas_call | solution.py:41
  21.8 1.2 %collective-permute-done.4.from_before = bf16[944,128]{1,0:T(8,128)(2,1)S(1)} collective-permute-done((bf16[944,128]{1,0:T(8,128)(2,1)S(1)}, bf16[944,128]{1,0:T(8,128)(2,1)S(1)}, u32[]{:S(2)}, u32[]{:S(2)}) %collective-permute-start.4) | collective-permute-done | bytes 241696 | tf_op jit(solution)/shard_map/ppermute | solution.py:357
  23.0 0.0 collective-permute-done.5.from_after
  23.0 0.0 copy-done
  23.0 0.0 copy-done.1
  23.1 0.0 copy-done.2
  23.1 0.0 copy-done.3
  23.1 0.0 copy-done.5
  23.1 0.0 copy-start.6
  23.1 6.9 %shard_map.123 = (bf16[32,2048]{1,0:T(8,128)(2,1)S(1)}, bf16[32,2048]{1,0:T(8,128)(2,1)S(1)}, bf16[32,2048]{1,0:T(8,128)(2,1)S(1)}, bf16[32,2048]{1,0:T(8,128)(2,1)S(1)}, f32[129,32,256]{2,1,0:T(8,128)S(1)}) custom-call(s32[10]{0:T(128)S(1)} %pad_add_fusion.partners, s32[520]{0:T(1024)S(1)} %get-tuple-element.27.halo_edges, ...), custom_call_target="tpu_custom_call", output_to_operand_aliasing={{4}: (5, {})} | custom-call | flops 4294967296 | bytes 1048576 | tf_op jit(solution)/shard_map/pallas_call | solution.py:41
  30.0 1.7 %collective-permute-start.6 = (bf16[32,2048]{1,0:T(8,128)(2,1)S(1)}, bf16[32,2048]{1,0:T(8,128)(2,1)S(1)}, u32[]{:S(2)}, u32[]{:S(2)}) collective-permute-start(bf16[32,2048]{1,0:T(8,128)(2,1)S(1)} %get-tuple-element.32), channel_id=1, source_target_pairs={{0,8},{8,0},{16,24},{24,16},{1,9},{9,1},{17,25},{25,17},{2,10},{10... | collective-permute-start | bytes 393224 | tf_op jit(solution)/shard_map/ppermute | solution.py:372
  31.7 1.5 %collective-permute-start.7 = (bf16[32,2048]{1,0:T(8,128)(2,1)S(1)}, bf16[32,2048]{1,0:T(8,128)(2,1)S(1)}, u32[]{:S(2)}, u32[]{:S(2)}) collective-permute-start(bf16[32,2048]{1,0:T(8,128)(2,1)S(1)} %get-tuple-element.33), channel_id=1, source_target_pairs={{0,16},{8,24},{16,0},{24,8},{1,17},{9,25},{17,1},{25,9},{2,18},{10... | collective-permute-start | bytes 393224 | tf_op jit(solution)/shard_map/ppermute | solution.py:372
  33.2 0.3 collective-permute-start.8
  33.5 0.0 copy-done.6
  33.5 3.8 %shard_map.121.weights = bf16[128,256]{1,0:T(8,128)(2,1)S(1)} custom-call(s32[10]{0:T(128)S(1)} %pad_add_fusion.partners, s32[1,8]{1,0:T(1,128)S(1)} %copy-done.6, bf16[144,128]{1,0:T(8,128)(2,1)S(1)} %shard_map.118.own, bf16[144,128]{1,0:T(8,128)(2,1)S(1)} %collective-permute-done.before, bf16[144,128]{1,0:T(8,128)(2,1)S(1)} %collective-permute-done.1.after, ...), custom_call_target="tpu_custom_call" | custom-call | flops 1073741824 | bytes 1048576 | tf_op jit(solution)/shard_map/pallas_call | solution.py:41
  37.3 0.0 collective-permute-done.6.refs_1_
  37.3 0.0 collective-permute-done.7.refs_2_
  37.3 2.4 %collective-permute-done.8.refs_3_ = bf16[32,2048]{1,0:T(8,128)(2,1)S(1)} collective-permute-done((bf16[32,2048]{1,0:T(8,128)(2,1)S(1)}, bf16[32,2048]{1,0:T(8,128)(2,1)S(1)}, u32[]{:S(2)}, u32[]{:S(2)}) %collective-permute-start.8) | collective-permute-done | bytes 131104 | tf_op jit(solution)/shard_map/ppermute | solution.py:372
  39.7 0.3 shard_map.124
  40.0 0.9 %collective-permute-start.9 = (bf16[32,2048]{1,0:T(8,128)(2,1)S(1)}, bf16[32,2048]{1,0:T(8,128)(2,1)S(1)}, u32[]{:S(2)}, u32[]{:S(2)}) collective-permute-start(bf16[32,2048]{1,0:T(8,128)(2,1)S(1)} %get-tuple-element.36), channel_id=1, source_target_pairs={{0,8},{8,0},{16,24},{24,16},{1,9},{9,1},{17,25},{25,17},{2,10},{10... | collective-permute-start | bytes 393224 | tf_op jit(solution)/shard_map/ppermute | solution.py:372
  40.8 1.0 %collective-permute-start.10 = (bf16[32,2048]{1,0:T(8,128)(2,1)S(1)}, bf16[32,2048]{1,0:T(8,128)(2,1)S(1)}, u32[]{:S(2)}, u32[]{:S(2)}) collective-permute-start(bf16[32,2048]{1,0:T(8,128)(2,1)S(1)} %get-tuple-element.37), channel_id=1, source_target_pairs={{0,16},{8,24},{16,0},{24,8},{1,17},{9,25},{17,1},{25,9},{2,18},{10... | collective-permute-start | bytes 393224 | tf_op jit(solution)/shard_map/ppermute | solution.py:372
  41.8 1.7 %collective-permute-start.11 = (bf16[32,2048]{1,0:T(8,128)(2,1)S(1)}, bf16[32,2048]{1,0:T(8,128)(2,1)S(1)}, u32[]{:S(2)}, u32[]{:S(2)}) collective-permute-start(bf16[32,2048]{1,0:T(8,128)(2,1)S(1)} %get-tuple-element.38), channel_id=1, source_target_pairs={{0,24},{8,16},{16,8},{24,0},{1,25},{9,17},{17,9},{25,1},{2,26},{10... | collective-permute-start | bytes 393224 | tf_op jit(solution)/shard_map/ppermute | solution.py:372
  43.6 1.5 %collective-permute-done.9.refs_1_ = bf16[32,2048]{1,0:T(8,128)(2,1)S(1)} collective-permute-done((bf16[32,2048]{1,0:T(8,128)(2,1)S(1)}, bf16[32,2048]{1,0:T(8,128)(2,1)S(1)}, u32[]{:S(2)}, u32[]{:S(2)}) %collective-permute-start.9) | collective-permute-done | bytes 131104 | tf_op jit(solution)/shard_map/ppermute | solution.py:372
  45.0 0.8 %collective-permute-done.10.refs_2_ = bf16[32,2048]{1,0:T(8,128)(2,1)S(1)} collective-permute-done((bf16[32,2048]{1,0:T(8,128)(2,1)S(1)}, bf16[32,2048]{1,0:T(8,128)(2,1)S(1)}, u32[]{:S(2)}, u32[]{:S(2)}) %collective-permute-start.10) | collective-permute-done | bytes 131104 | tf_op jit(solution)/shard_map/ppermute | solution.py:372
  45.8 1.9 %collective-permute-done.11.refs_3_ = bf16[32,2048]{1,0:T(8,128)(2,1)S(1)} collective-permute-done((bf16[32,2048]{1,0:T(8,128)(2,1)S(1)}, bf16[32,2048]{1,0:T(8,128)(2,1)S(1)}, u32[]{:S(2)}, u32[]{:S(2)}) %collective-permute-start.11) | collective-permute-done | bytes 131104 | tf_op jit(solution)/shard_map/ppermute | solution.py:372
  47.7 1.9 %shard_map.125 = bf16[32,64,128]{2,1,0:T(8,128)(2,1)} custom-call(s32[10]{0:T(128)S(1)} %pad_add_fusion.partners, bf16[32,2048]{1,0:T(8,128)(2,1)S(1)} %get-tuple-element.35.refs_0_, bf16[32,2048]{1,0:T(8,128)(2,1)S(1)} %collective-permute-done.9.refs_1_, bf16[32,2048]{1,0:T(8,128)(2,1)S(1)} %collective-permute-done.10.refs_2_, ...), custom_call_target="tpu_custom_call" | custom-call | flops 1048576 | bytes 1048576 | tf_op jit(solution)/shard_map/pallas_call | solution.py:41
  (1 shorter events, 0.0 us)
Async XLA Ops:
  0.0 17.1 %copy-start.4 = (s32[128,4]{0,1:T(4,128)S(1)}, s32[128,4]{0,1:T(4,128)}, u32[]{:S(2)}) copy-start(s32[128,4]{0,1:T(4,128)} %param.19) | copy-start | bytes 6148
  1.1 10.7 %collective-permute-start.3 = (bf16[144,128]{1,0:T(8,128)(2,1)S(1)}, bf16[144,128]{1,0:T(8,128)(2,1)S(1)}, u32[]{:S(2)}, u32[]{:S(2)}) collective-permute-start(bf16[144,128]{1,0:T(8,128)(2,1)S(1)} %shard_map.118.own), channel_id=1, source_target_pairs={{0,24},{8,0},{16,8},{24,16},{1,25},{9,1},{17,9},{25,17},{2,26},{10... | collective-permute-start | bytes 110600 | tf_op jit(solution)/shard_map/ppermute | solution.py:357
  5.1 6.8 %collective-permute-start.2 = (bf16[144,128]{1,0:T(8,128)(2,1)S(1)}, bf16[144,128]{1,0:T(8,128)(2,1)S(1)}, u32[]{:S(2)}, u32[]{:S(2)}) collective-permute-start(bf16[144,128]{1,0:T(8,128)(2,1)S(1)} %shard_map.118.own), channel_id=1, source_target_pairs={{0,8},{8,16},{16,24},{24,0},{1,9},{9,17},{17,25},{25,1},{2,10},{10... | collective-permute-start | bytes 110600 | tf_op jit(solution)/shard_map/ppermute | solution.py:357
  5.1 6.8 %collective-permute-start.1 = (bf16[144,128]{1,0:T(8,128)(2,1)S(1)}, bf16[144,128]{1,0:T(8,128)(2,1)S(1)}, u32[]{:S(2)}, u32[]{:S(2)}) collective-permute-start(bf16[144,128]{1,0:T(8,128)(2,1)S(1)} %shard_map.118.own), channel_id=1, source_target_pairs={{0,7},{1,0},{2,1},{3,2},{4,3},{5,4},{6,5},{7,6},{8,15},{9,8},{10,9... | collective-permute-start | bytes 110600 | tf_op jit(solution)/shard_map/ppermute | solution.py:357
  7.8 5.2 %collective-permute-start = (bf16[144,128]{1,0:T(8,128)(2,1)S(1)}, bf16[144,128]{1,0:T(8,128)(2,1)S(1)}, u32[]{:S(2)}, u32[]{:S(2)}) collective-permute-start(bf16[144,128]{1,0:T(8,128)(2,1)S(1)} %shard_map.118.own), channel_id=1, source_target_pairs={{0,1},{1,2},{2,3},{3,4},{4,5},{5,6},{6,7},{7,0},{8,9},{9,10},{10,1... | collective-permute-start | bytes 110600 | tf_op jit(solution)/shard_map/ppermute | solution.py:357
  13.0 10.0 %copy-start = (bf16[1,256,256]{2,1,0:T(8,128)(2,1)S(1)}, bf16[1,256,256]{2,1,0:T(8,128)(2,1)}, u32[]{:S(2)}) copy-start(bf16[1,256,256]{2,1,0:T(8,128)(2,1)} %send.3) | copy-start | bytes 393220
  13.0 10.0 %copy-start.1 = (bf16[1,256,256]{2,1,0:T(8,128)(2,1)S(1)}, bf16[1,256,256]{2,1,0:T(8,128)(2,1)}, u32[]{:S(2)}) copy-start(bf16[1,256,256]{2,1,0:T(8,128)(2,1)} %update.1) | copy-start | bytes 393220
  13.0 10.0 %copy-start.2 = (bf16[64,256]{1,0:T(8,128)(2,1)S(1)}, bf16[64,256]{1,0:T(8,128)(2,1)}, u32[]{:S(2)}) copy-start(bf16[64,256]{1,0:T(8,128)(2,1)} %encode.3) | copy-start | bytes 98308
  13.0 10.0 %copy-start.3 = (bf16[256,64]{0,1:T(8,128)(2,1)S(1)}, bf16[256,64]{0,1:T(8,128)(2,1)}, u32[]{:S(2)}) copy-start(bf16[256,64]{0,1:T(8,128)(2,1)} %param.18) | copy-start | bytes 98308
  13.0 10.1 %copy-start.5 = (bf16[1,256]{1,0:T(2,128)(2,1)S(1)}, bf16[1,256]{1,0:T(2,128)(2,1)}, u32[]{:S(2)}) copy-start(bf16[1,256]{1,0:T(2,128)(2,1)} %gain.1) | copy-start | bytes 1540
  13.5 9.6 %collective-permute-start.4 = (bf16[944,128]{1,0:T(8,128)(2,1)S(1)}, bf16[944,128]{1,0:T(8,128)(2,1)S(1)}, u32[]{:S(2)}, u32[]{:S(2)}) collective-permute-start(bf16[944,128]{1,0:T(8,128)(2,1)S(1)} %get-tuple-element.23), channel_id=1, source_target_pairs={{0,1},{1,2},{2,3},{3,4},{4,5},{5,6},{6,7},{7,0},{8,9},{9,10},{10,1... | collective-permute-start | bytes 725000 | tf_op jit(solution)/shard_map/ppermute | solution.py:357
  13.5 9.5 %collective-permute-start.5 = (bf16[944,128]{1,0:T(8,128)(2,1)S(1)}, bf16[944,128]{1,0:T(8,128)(2,1)S(1)}, u32[]{:S(2)}, u32[]{:S(2)}) collective-permute-start(bf16[944,128]{1,0:T(8,128)(2,1)S(1)} %get-tuple-element.24), channel_id=1, source_target_pairs={{0,7},{1,0},{2,1},{3,2},{4,3},{5,4},{6,5},{7,6},{8,15},{9,8},{10,9... | collective-permute-start | bytes 725000 | tf_op jit(solution)/shard_map/ppermute | solution.py:357
  23.1 10.4 %copy-start.6 = (s32[1,8]{1,0:T(1,128)S(1)}, s32[1,8]{1,0:T(1,128)}, u32[]{:S(2)}) copy-start(s32[1,8]{1,0:T(1,128)} %neighbours.1) | copy-start | bytes 100
  30.0 7.3 %collective-permute-start.6 = (bf16[32,2048]{1,0:T(8,128)(2,1)S(1)}, bf16[32,2048]{1,0:T(8,128)(2,1)S(1)}, u32[]{:S(2)}, u32[]{:S(2)}) collective-permute-start(bf16[32,2048]{1,0:T(8,128)(2,1)S(1)} %get-tuple-element.32), channel_id=1, source_target_pairs={{0,8},{8,0},{16,24},{24,16},{1,9},{9,1},{17,25},{25,17},{2,10},{10... | collective-permute-start | bytes 393224 | tf_op jit(solution)/shard_map/ppermute | solution.py:372
  31.7 5.6 %collective-permute-start.7 = (bf16[32,2048]{1,0:T(8,128)(2,1)S(1)}, bf16[32,2048]{1,0:T(8,128)(2,1)S(1)}, u32[]{:S(2)}, u32[]{:S(2)}) collective-permute-start(bf16[32,2048]{1,0:T(8,128)(2,1)S(1)} %get-tuple-element.33), channel_id=1, source_target_pairs={{0,16},{8,24},{16,0},{24,8},{1,17},{9,25},{17,1},{25,9},{2,18},{10... | collective-permute-start | bytes 393224 | tf_op jit(solution)/shard_map/ppermute | solution.py:372
  33.2 6.4 %collective-permute-start.8 = (bf16[32,2048]{1,0:T(8,128)(2,1)S(1)}, bf16[32,2048]{1,0:T(8,128)(2,1)S(1)}, u32[]{:S(2)}, u32[]{:S(2)}) collective-permute-start(bf16[32,2048]{1,0:T(8,128)(2,1)S(1)} %get-tuple-element.34), channel_id=1, source_target_pairs={{0,24},{8,16},{16,8},{24,0},{1,25},{9,17},{17,9},{25,1},{2,26},{10... | collective-permute-start | bytes 393224 | tf_op jit(solution)/shard_map/ppermute | solution.py:372
  40.0 5.0 %collective-permute-start.9 = (bf16[32,2048]{1,0:T(8,128)(2,1)S(1)}, bf16[32,2048]{1,0:T(8,128)(2,1)S(1)}, u32[]{:S(2)}, u32[]{:S(2)}) collective-permute-start(bf16[32,2048]{1,0:T(8,128)(2,1)S(1)} %get-tuple-element.36), channel_id=1, source_target_pairs={{0,8},{8,0},{16,24},{24,16},{1,9},{9,1},{17,25},{25,17},{2,10},{10... | collective-permute-start | bytes 393224 | tf_op jit(solution)/shard_map/ppermute | solution.py:372
  40.8 5.0 %collective-permute-start.10 = (bf16[32,2048]{1,0:T(8,128)(2,1)S(1)}, bf16[32,2048]{1,0:T(8,128)(2,1)S(1)}, u32[]{:S(2)}, u32[]{:S(2)}) collective-permute-start(bf16[32,2048]{1,0:T(8,128)(2,1)S(1)} %get-tuple-element.37), channel_id=1, source_target_pairs={{0,16},{8,24},{16,0},{24,8},{1,17},{9,25},{17,1},{25,9},{2,18},{10... | collective-permute-start | bytes 393224 | tf_op jit(solution)/shard_map/ppermute | solution.py:372
  41.8 5.9 %collective-permute-start.11 = (bf16[32,2048]{1,0:T(8,128)(2,1)S(1)}, bf16[32,2048]{1,0:T(8,128)(2,1)S(1)}, u32[]{:S(2)}, u32[]{:S(2)}) collective-permute-start(bf16[32,2048]{1,0:T(8,128)(2,1)S(1)} %get-tuple-element.38), channel_id=1, source_target_pairs={{0,24},{8,16},{16,8},{24,0},{1,25},{9,17},{17,9},{25,1},{2,26},{10... | collective-permute-start | bytes 393224 | tf_op jit(solution)/shard_map/ppermute | solution.py:372

commit v3 on v2

v3 whole, which is shorter than its diff:
```python
import functools

import jax
import jax.numpy as jnp
from jax import lax
from jax.experimental import pallas as pl
from jax.experimental.pallas import tpu as pltpu
from jax.sharding import PartitionSpec as P

ITERS_NS = 5
EPSILON = 1e-05
F32 = jnp.float32
BF16 = jnp.bfloat16
FULL_PRECISION = lax.Precision.HIGHEST
VMEM = pl.BlockSpec(memory_space=pltpu.VMEM)
SMEM = pl.BlockSpec(memory_space=pltpu.SMEM)
TAIL = 16
NOWHERE = -1048576.0
OUTPUT_STEP = 4
BATCH = 16
HBM = pl.BlockSpec(memory_space=pltpu.HBM)
ANY = pl.BlockSpec(memory_space=pl.ANY)


def dot(left, right):
    return jnp.dot(left, right, preferred_element_type=F32)


def dot_t(left, right):
    return lax.dot_general(left, right, (((1,), (1,)), ((), ())), preferred_element_type=F32)


def split(value):
    high = value.astype(BF16)
    return high, (value - high.astype(F32)).astype(BF16)


def placed_in(space, *values):
    return tuple(pltpu.with_memory_space_constraint(value, space) for value in values)


def call(kernel, shapes, inputs, specs=None, outs=None, scratch=(), flops=0, aliases=None):
    return pl.pallas_call(
        kernel,
        out_shape=shapes,
        in_specs=specs or [VMEM] * len(inputs),
        out_specs=outs or jax.tree.map(lambda _: VMEM, shapes),
        scratch_shapes=list(scratch),
        input_output_aliases=aliases or {},
        compiler_params=pltpu.CompilerParams(vmem_limit_bytes=16 * 1024 * 1024),
        cost_estimate=pl.CostEstimate(flops=flops, bytes_accessed=1 << 20, transcendentals=0),
    )(*inputs)


def start_copies(sems, *ends):
    copies = [
        pltpu.make_async_copy(source, target, sems.at[index]) for index, (source, target) in enumerate(ends)
    ]
    for copy in copies:
        copy.start()
    return copies


def gram_kernel(perturbation, values, halo_nodes, fields, encode, send, receive, out, *refs):
    *near, held, held_values, held_lists, sems = refs
    copies = start_copies(
        sems,
        (perturbation, held),
        (values, held_values),
        (halo_nodes, held_lists),
        *zip((fields, encode, send, receive), near),
    )
    for copy in copies[:3]:
        copy.wait()
    ensemble = held.shape[1]
    members = held[0]
    wide = held_values[0].astype(F32)
    high, low = split(members.astype(F32) * wide[0:1])
    gram = dot_t(high, members) + dot_t(low, members)
    high, low = split(jnp.broadcast_to(wide[0:1] * wide[1:2], (TAIL, wide.shape[1])))
    forcing = dot_t(high, members) + dot_t(low, members)
    high, low = split(forcing)
    lists = held_lists[...].astype(F32)
    lists = jnp.concatenate([lists, jnp.zeros((2, ensemble - lists.shape[1]), F32)], axis=1)
    row = lax.broadcasted_iota(jnp.int32, forcing.shape, 0)
    tail = jnp.where(row == 0, high.astype(F32), low.astype(F32))
    tail = jnp.where(row == 2, lists[0:1], jnp.where(row == 3, lists[1:2], tail))
    out[:ensemble, :] = gram.astype(BF16)
    out[ensemble:, :] = tail.astype(BF16)
    for copy in copies[3:]:
        copy.wait()


def paired(fields, pair):
    half = fields.shape[0] // 2
    return jnp.concatenate([fields[pair], fields[pair + half]], axis=0)


def pick_kernel(halo_count, columns, own, before, after, to_before, to_after, column, scratch):
    half, nodes, _ = columns.shape
    rows = before.shape[0]
    ensemble = rows - TAIL
    wanted_before = before[ensemble:, :].astype(F32)[3:4]
    wanted_after = after[ensemble:, :].astype(F32)[2:3]
    node = lax.broadcasted_iota(jnp.int32, (nodes, wanted_before.shape[1]), 0).astype(F32)
    chosen = jnp.concatenate(
        [(node == wanted).astype(F32).T[:halo_count].astype(BF16) for wanted in (wanted_before, wanted_after)],
        axis=0,
    )
    for pair in range(half):
        picked = dot(chosen, columns[pair])
        scratch[pl.ds(pair, 2 * halo_count, stride=half), :] = picked
    size = halo_count * half
    to_before[:size, :] = scratch[:size, :].astype(BF16)
    to_after[:size, :] = scratch[size:, :].astype(BF16)
    to_before[size:, :] = after[...]
    to_after[size:, :] = before[...]
    for index, source in enumerate((before, own, after)):
        column[index * rows : (index + 1) * rows, :] = source[...]


def block_diagonal(weight):
    zero = jnp.zeros_like(weight)
    return jnp.concatenate(
        [jnp.concatenate([weight, zero], axis=1), jnp.concatenate([zero, weight], axis=1)], axis=0
    )


def halves(wide, nodes, half, hidden):
    return jnp.concatenate(
        [wide[:, :hidden].reshape(nodes, half, hidden), wide[:, hidden:].reshape(nodes, half, hidden)], axis=1
    )


def columns_kernel(fields, columns, rearranged, scratch):
    half = fields.shape[0] // 2
    nodes = fields.shape[2]
    for pair in range(half):
        column = paired(fields, pair).astype(F32).T
        scratch[pl.ds(pair, nodes, stride=half), :] = column
        columns[pair] = column.astype(BF16)
    rearranged[...] = scratch[...].astype(BF16)


def own_kernel(rearranged, encode, send, receive, sent, received):
    nodes, members, hidden = received.shape
    half = members // 2
    both = block_diagonal(encode[...])
    send_half = send[0] * 0.5
    receive_half = receive[0] * 0.5
    sent[nodes] = jnp.full(sent.shape[1:], NOWHERE, F32)
    step_nodes = 32
    size = step_nodes * half
    for index in range(nodes // step_nodes):
        rows = rearranged[index * size : (index + 1) * size, :]
        stream = halves(dot(rows, both), step_nodes, half, hidden)
        rounded = stream.astype(BF16).reshape(step_nodes * 2 * half, hidden)
        shape = (step_nodes, 2 * half, hidden)
        at = slice(index * step_nodes, (index + 1) * step_nodes)
        sent[at] = dot(rounded, send_half).astype(BF16).astype(F32).reshape(shape)
        received[at] = dot(rounded, receive_half).reshape(shape)


def activated(sender, here):
    moved = sender + here
    return moved + moved * jnp.tanh(moved)


def own_message_kernel(halo_total, edges, sent, received, messages, halo_edges):
    nodes, members, hidden = received.shape
    degree = edges.shape[0]
    group = 8

    def step(index, count):
        for offset in range(group):
            node = index * group + offset
            here = received[node]
            total = None
            for slot in range(degree):
                sender = edges[slot, node]
                value = activated(sent[jnp.minimum(sender, nodes)], here)
                total = value if total is None else total + value
                halo_edges[count] = node * halo_total + sender - nodes
                count = count + jnp.where(sender < nodes, 0, 1)
            messages[node] = total
        return count

    count = lax.fori_loop(0, nodes // group, step, 0)
    for index in range(BATCH):
        halo_edges[count + index] = nodes * halo_total
    halo_edges[halo_edges.shape[0] - 1] = count
    messages[nodes] = jnp.zeros((members, hidden), F32)


def message_kernel(
    halo_count,
    halo_edges_far,
    rearranged,
    received,
    started,
    from_before,
    from_after,
    encode,
    send,
    update,
    gain,
    decode,
    *outputs,
):
    *outs, messages, extended, halo_edges, sems = outputs
    (listed,) = start_copies(sems, (halo_edges_far, halo_edges))
    targets, _ = partners("member")
    nodes, members, hidden = received.shape
    half = members // 2
    regions = len(outs)
    channels = decode.shape[0]
    both = block_diagonal(encode[...])
    send_half = send[0] * 0.5
    for side, source in enumerate((from_before, from_after)):
        stream = halves(dot(source[: halo_count * half, :], both), halo_count, half, hidden)
        rounded = stream.astype(BF16).reshape(halo_count * members, hidden)
        extended[side * halo_count : (side + 1) * halo_count] = (
            dot(rounded, send_half).astype(BF16).astype(F32).reshape(halo_count, members, hidden)
        )

    listed.wait()

    def batch(index, carry):
        found = []
        for offset in range(BATCH):
            code = halo_edges[index * BATCH + offset]
            node = code // (2 * halo_count)
            here = received[jnp.minimum(node, nodes - 1)]
            found.append((node, activated(extended[code % (2 * halo_count)], here)))
        for node, value in found:
            messages[node] = messages[node] + value
        return carry

    lax.fori_loop(0, (halo_edges[halo_edges.shape[0] - 1] + BATCH - 1) // BATCH, batch, 0)
    zero = jnp.zeros_like(decode[...])
    decode_even = jnp.concatenate([decode[...], zero], axis=0)
    decode_odd = jnp.concatenate([zero, decode[...]], axis=0)
    gains = gain[...].astype(F32)
    chunk = nodes // regions
    pairs = chunk // 2
    width = 2 * channels
    average = jnp.full((hidden, width), 1.0 / hidden, BF16)
    low = lax.broadcasted_iota(jnp.int32, (nodes // 2, half, width), 2) < channels
    bases = [target * chunk for target in targets]
    fields = jnp.concatenate(
        [rearranged[pl.ds(pl.multiple_of(base * half, chunk * half), chunk * half), :] for base in bases], axis=0
    )
    stream = halves(dot(fields, both), nodes, half, hidden).reshape(nodes * members, hidden)
    message = jnp.concatenate([messages[pl.ds(base, chunk)] for base in bases], axis=0).reshape(nodes * members, hidden)
    mean_square = dot((message * message).astype(BF16), average)
    scale = lax.rsqrt(mean_square + EPSILON)
    scaled = message * jnp.concatenate([scale] * (hidden // width), axis=1) * gains
    stream = stream + dot(scaled.astype(BF16), update[0])
    final = stream.astype(BF16).reshape(nodes // 2, 2, members, hidden)
    rows = nodes // 2 * members
    change = dot_t(final[:, 0].reshape(rows, hidden), decode_even) + dot_t(
        final[:, 1].reshape(rows, hidden), decode_odd
    )
    wide = fields.astype(F32).reshape(nodes // 2, 2, half, width)
    even, odd = wide[:, 0], wide[:, 1]
    first = jnp.where(low, even, pltpu.roll(odd, channels, 2))
    second = jnp.where(low, pltpu.roll(even, channels, 2), odd)
    initial = jnp.concatenate([first, second], axis=1)
    forecast = (initial + change.reshape(initial.shape)).astype(BF16)
    for index, out in enumerate(outs):
        for pair in range(pairs):
            out[:, pair * width : (pair + 1) * width] = forecast[index * pairs + pair]


def weights_kernel(neighbours, own, before, after, up, down, from_before, from_after, out):
    rows, ensemble = own.shape
    first = from_before.shape[0] - rows
    row_count, column_count = lax.axis_size("member"), lax.axis_size("space")
    own_row, own_column = lax.axis_index("member"), lax.axis_index("space")
    targets, origins = partners("member")
    offsets = []
    for index in range(neighbours.shape[1]):
        region = neighbours[0, index]
        near_row = (region // column_count - own_row + 1 + row_count) % row_count - 1
        near_column = (region % column_count - own_column + 2 + column_count) % column_count - 2
        offsets.append((near_row, near_column))
    sources = {(0, -1): (before, 0), (0, 1): (after, 0), (0, -2): (from_before, first), (0, 2): (from_after, first)}
    for row, source in ((-1, up), (1, down)):
        for index in range(3):
            sources[row, index - 1] = (source, index * rows)
    total = own[...].astype(F32)
    for place, (source, start) in sources.items():
        weight = 0.0
        for near_row, near_column in offsets:
            here = jnp.logical_and(near_row == place[0], near_column == place[1])
            weight = weight + jnp.where(here, 1.0 / (1.0 + (place[0] ** 2 + place[1] ** 2) / 2.0), 0.0)
        total = total + weight * source[start : start + rows, :].astype(F32)
    identity = (
        lax.broadcasted_iota(jnp.int32, (ensemble, ensemble), 0)
        == lax.broadcasted_iota(jnp.int32, (ensemble, ensemble), 1)
    ).astype(F32)
    full = functools.partial(jnp.dot, precision=FULL_PRECISION, preferred_element_type=F32)
    system = identity + total[:ensemble] / (ensemble - 1)
    squares = jnp.sum(jnp.sum(system * system, axis=1, keepdims=True), axis=0, keepdims=True)
    scaling = jnp.sqrt(squares)
    iterate = system / scaling
    correction = 1.5 * identity - 0.5 * iterate
    inverse = correction
    for _ in range(ITERS_NS - 1):
        iterate = full(iterate, correction)
        correction = 1.5 * identity - 0.5 * full(inverse, iterate)
        inverse = full(correction, inverse)
    tail = total[ensemble:]
    forcing = jnp.broadcast_to(tail[0:1] + tail[1:2], (8, ensemble))
    mean_weights = full(full(forcing, inverse), inverse)[0:1] / (scaling * (ensemble - 1))
    transform = inverse / jnp.sqrt(scaling) + mean_weights
    rest = (1.0 - jnp.sum(transform, axis=1, keepdims=True)) / ensemble
    members = ensemble // row_count
    to_rows = lax.broadcasted_iota(jnp.int32, (ensemble, ensemble), 0)
    to_columns = lax.broadcasted_iota(jnp.int32, (ensemble, ensemble), 1)
    wanted_rows, wanted_columns = to_rows % members, to_columns % members
    for index in range(row_count):
        target, origin = targets[index] * members, origins[index] * members
        wanted_rows = wanted_rows + jnp.where(to_rows // members == index, target, 0)
        wanted_columns = wanted_columns + jnp.where(to_columns // members == index, origin, 0)
    by_row = (to_columns == wanted_rows).astype(F32).astype(BF16)
    by_column = (to_rows == wanted_columns).astype(F32).astype(BF16)
    for index, part in enumerate(split(transform + rest)):
        moved = dot(dot(by_row, part).astype(BF16), by_column)
        out[:, index * ensemble : (index + 1) * ensemble] = moved.astype(BF16)


def analysis_kernel(weights, *refs):
    count = len(refs) // 2
    pieces, outs = refs[:count], refs[count:]
    members, width = pieces[0].shape
    step_width = 512
    for start in range(0, width, step_width):
        columns = [piece[:, start : start + step_width] for piece in pieces]
        analysed = dot(weights[...], jnp.concatenate(columns * 2, axis=0)).astype(BF16)
        for index, out in enumerate(outs):
            out[:, start : start + step_width] = analysed[index * members : (index + 1) * members]


def output_kernel(*refs):
    *pieces, far, out, held, scratch, sems = refs
    count = len(pieces)
    members, channels, nodes = out.shape
    half = members // 2
    low = lax.broadcasted_iota(jnp.int32, (half, 2 * channels), 1) < channels
    chunk = nodes // count
    for index, piece in enumerate(pieces):
        held[partners("member")[1][index]] = piece[...]
    for region in range(count):
        for pair in range(chunk // 2):
            block = held[region, :, pair * 2 * channels : (pair + 1) * 2 * channels].astype(F32)
            first, second = block[:half], block[half:]
            row = (region * chunk + 2 * pair) * half
            scratch[row : row + half, :] = jnp.where(low, first, pltpu.roll(second, channels, 1))
            scratch[row + half : row + 2 * half, :] = jnp.where(low, pltpu.roll(first, channels, 1), second)
    copies = []
    for pair in range(half):
        block = scratch[pl.ds(pair, nodes, stride=half), :].T.astype(BF16)
        out[pair] = block[:channels]
        out[pair + half] = block[channels:]
        if (pair + 1) % OUTPUT_STEP == 0:
            step = pair // OUTPUT_STEP
            parts = [slice(start, start + OUTPUT_STEP) for start in (pair + 1 - OUTPUT_STEP, pair + 1 - OUTPUT_STEP + half)]
            copies += start_copies(sems.at[step], *((out.at[part], far.at[part]) for part in parts))
    for copy in copies:
        copy.wait()


def ring(value, axis, shift):
    count = lax.axis_size(axis)
    return lax.ppermute(value, axis, [(i, (i + shift) % count) for i in range(count)])


def partners(axis):
    count = lax.axis_size(axis)
    own = lax.axis_index(axis)
    if count & (count - 1) == 0:
        targets = origins = [own ^ step for step in range(count)]
    else:
        targets = [lax.rem(own + step, count) for step in range(count)]
        origins = [lax.rem(own + count - step, count) for step in range(count)]
    return targets, origins


def exchange(pieces, axis):
    count = lax.axis_size(axis)
    paired_up = count & (count - 1) == 0
    return [pieces[0]] + [
        lax.ppermute(piece, axis, [(i, i ^ step if paired_up else (i + step) % count) for i in range(count)])
        for step, piece in enumerate(pieces)
        if step
    ]


def body(
    initial_fields,
    encode_weight,
    send_weight,
    receive_weight,
    update_weight,
    norm_gain,
    decode_weight,
    edge_senders,
    halo_nodes,
    observed_perturbation,
    observed_values,
    region_neighbours,
):
    members, channels, nodes = initial_fields.shape
    hidden = encode_weight.shape[1]
    half = members // 2
    halo_count = halo_nodes.shape[1]
    ensemble = observed_perturbation.shape[1]
    groups = lax.axis_size("member")
    rows = ensemble + TAIL
    struct = jax.ShapeDtypeStruct
    raw = (initial_fields, encode_weight, send_weight, receive_weight)
    own, *near = call(
        gram_kernel,
        (struct((rows, ensemble), BF16),) + tuple(pltpu.VMEM(value.shape, BF16) for value in raw),
        placed_in(pltpu.HBM, observed_perturbation, observed_values, halo_nodes, *raw),
        specs=[HBM] * 7,
        scratch=[
            pltpu.VMEM(observed_perturbation.shape, BF16),
            pltpu.VMEM(observed_values.shape, BF16),
            pltpu.VMEM(halo_nodes.shape, jnp.int32),
            pltpu.SemaphoreType.DMA((7,)),
        ],
        flops=1 << 24,
    )
    before = ring(own, "space", 1)
    after = ring(own, "space", -1)
    fields, *weights = placed_in(pltpu.VMEM, *near)
    columns, rearranged = call(
        columns_kernel,
        (struct((half, nodes, 2 * channels), BF16), struct((nodes * half, 2 * channels), BF16)),
        (fields,),
        scratch=[pltpu.VMEM((nodes * half, 2 * channels), F32)],
        flops=1 << 28,
    )
    sent, received = call(
        own_kernel,
        (pltpu.VMEM((nodes + 1, members, hidden), F32), pltpu.VMEM((nodes, members, hidden), F32)),
        (rearranged, *weights),
        flops=1 << 30,
    )
    size = halo_count * half
    columns, sent, received = lax.optimization_barrier((columns, sent, received))
    to_before, to_after, column = call(
        functools.partial(pick_kernel, halo_count),
        (struct((size + rows, 2 * channels), BF16),) * 2 + (struct((3 * rows, ensemble), BF16),),
        (columns, own, before, after),
        scratch=[pltpu.VMEM((2 * size, 2 * channels), F32)],
        flops=1 << 27,
    )
    from_before = ring(to_after, "space", 1)
    from_after = ring(to_before, "space", -1)
    edges = edge_senders.T
    started, halo_edges = call(
        functools.partial(own_message_kernel, 2 * halo_count),
        (
            pltpu.VMEM((nodes + 1, members, hidden), F32),
            struct((edges.size + BATCH + 1,), jnp.int32),
        ),
        (edges, *placed_in(pltpu.VMEM, sent, received)),
        specs=[SMEM, VMEM, VMEM],
        outs=(VMEM, SMEM),
        flops=1 << 31,
    )
    column, started = lax.optimization_barrier((column, started))
    up = ring(column, "member", 1)
    down = ring(column, "member", -1)
    width = nodes // groups * channels
    piece = struct((members, width), BF16)
    *predicted, _ = call(
        functools.partial(message_kernel, halo_count),
        (piece,) * groups + (struct(started.shape, F32),),
        (
            halo_edges,
            rearranged,
            *placed_in(pltpu.VMEM, received, started),
            from_before,
            from_after,
            encode_weight,
            send_weight,
            update_weight,
            norm_gain,
            decode_weight.T,
        ),
        specs=[ANY] + [VMEM] * 10,
        scratch=[
            pltpu.VMEM((2 * halo_count, members, hidden), F32),
            pltpu.SMEM(halo_edges.shape, jnp.int32),
            pltpu.SemaphoreType.DMA((1,)),
        ],
        flops=1 << 32,
        aliases={3: groups},
    )
    states = exchange(predicted, "member")
    weights = call(
        weights_kernel,
        struct((ensemble, 2 * ensemble), BF16),
        (region_neighbours, own, before, after, up, down, from_before, from_after),
        specs=[SMEM] + [VMEM] * 7,
        flops=1 << 30,
    )
    analysed = call(
        analysis_kernel,
        (piece,) * groups,
        (weights, *states),
        flops=1 << 28,
    )
    returned = exchange(analysed, "member")
    return call(
        output_kernel,
        struct((members, channels, nodes), BF16),
        tuple(returned),
        outs=HBM,
        scratch=[
            pltpu.VMEM((members, channels, nodes), BF16),
            pltpu.VMEM((groups, members, width), BF16),
            pltpu.VMEM((nodes * half, 2 * channels), F32),
            pltpu.SemaphoreType.DMA((half // OUTPUT_STEP, 2)),
        ],
        flops=1 << 20,
    )


def solution(mesh):
    placed = (
        P("member", None, "space"),
        P(),
        P(),
        P(),
        P(),
        P(),
        P(),
        P("space", None),
        P(None, "space"),
        P(("member", "space"), None, None),
        P(("member", "space"), None, None),
        P(("member", "space"), None),
    )
    return jax.shard_map(
        body, mesh=mesh, in_specs=placed, out_specs=P("member", None, "space"), check_vma=False
    )
```

time: 49.6 us -> 44 us (0.89)
  Pallas kernels: 23 us -> 18.2 us
  waiting for transfers between devices: 8.89 us -> 7.04 us
  starting transfers between devices: 17.4 us -> 18.3 us
    pallas_call x8 -> x9, Pallas kernels: 23 us -> 18.2 us  [call(): pl.pallas_call(kernel, out_shape=shapes, in_specs=specs or [VMEM] * len(i...]
    ppermute x6, waiting for transfers between devices: 2.38 us -> 0.02 us  [ring(): lax.ppermute(value, axis, [(i, (i + shift) % count) for i in range(count)])]
    ppermute x6, starting transfers between devices: 10.3 us -> 11.2 us  [ring(): lax.ppermute(value, axis, [(i, (i + shift) % count) for i in range(count)])]
    ppermute x6, waiting for transfers between devices: 6.51 us -> 7.03 us  [exchange(): lax.ppermute(piece, axis, [(i, i ^ step if paired_up else (i + step) % co...]
  transfers between devices with their start and end apart: 12 -> 12, of which waited for: 6 -> 3; matrix products, arithmetic and copies ran while one was open for 0% -> 0% of each run, Pallas kernels for 25% -> 34%
where the time goes in v3:
time: 44 us; the launch traced here: 43.8 us
  starting transfers between devices  18.3 us (42%)
  Pallas kernels  18.2 us (41%)
  waiting for transfers between devices  7.04 us (16%)
    pallas_call x9, Pallas kernels, call(): pl.pallas_call(kernel, out_shape=shapes, in_specs=specs or [VMEM] * len(i...  18.2 us
    ppermute x6, starting transfers between devices, ring(): lax.ppermute(value, axis, [(i, (i + shift) % count) for i in range(count)])  11.2 us
    ppermute x6, starting transfers between devices, exchange(): lax.ppermute(piece, axis, [(i, i ^ step if paired_up else (i + step) % co...  7.11 us
    ppermute x6, waiting for transfers between devices, exchange(): lax.ppermute(piece, axis, [(i, i ^ step if paired_up else (i + step) % co...  7.03 us
  transfers between devices with their start and end apart: 12, of which 3 were waited for; matrix products, arithmetic and copies ran while one was open for 0% of the time, Pallas kernels for 34%

profile of v3, /device:TPU:0, one launch (start us, length us, event | category | flops | bytes accessed | tf_op | source)
XLA Modules:
  0.0 43.8 jit_solution(11419670287920245021)
XLA Ops:
  0.0 0.0 copy-start.2
  0.0 1.3 %shard_map.118 = (bf16[144,128]{1,0:T(8,128)(2,1)S(1)}, bf16[32,64,128]{2,1,0:T(8,128)(2,1)S(1)}, bf16[64,256]{1,0:T(8,128)(2,1)S(1)}, bf16[1,256,256]{2,1,0:T(8,128)(2,1)S(1)}, bf16[1,256,256]{2,1,0:T(8,128)(2,1)S(1)}) custom-call(bf16[1,128,256]{2,1,0:T(8,128)(2,1)} %perturbation.1, bf16[1,2,256]{2,1,0:T(2,128)(2,1)} %values.1, s32[2,32]{1,0:T(2,128)} %halo_nodes.1, ...), custom_call_target="tpu_custom_call" | custom-call | flops 16777216 | bytes 1048576 | tf_op jit(solution)/shard_map/pallas_call | solution.py:43
  1.3 0.5 %collective-permute-start = (bf16[144,128]{1,0:T(8,128)(2,1)S(1)}, bf16[144,128]{1,0:T(8,128)(2,1)S(1)}, u32[]{:S(2)}, u32[]{:S(2)}) collective-permute-start(bf16[144,128]{1,0:T(8,128)(2,1)S(1)} %get-tuple-element.32.own), channel_id=1, source_target_pairs={{0,1},{1,2},{2,3},{3,4},{4,5},{5,6},{6,7},{7,0},{8,9},{9,10},{10,1... | collective-permute-start | bytes 110600 | tf_op jit(solution)/shard_map/ppermute | solution.py:376
  1.8 4.1 %collective-permute-start.1 = (bf16[144,128]{1,0:T(8,128)(2,1)S(1)}, bf16[144,128]{1,0:T(8,128)(2,1)S(1)}, u32[]{:S(2)}, u32[]{:S(2)}) collective-permute-start(bf16[144,128]{1,0:T(8,128)(2,1)S(1)} %get-tuple-element.32.own), channel_id=1, source_target_pairs={{0,7},{1,0},{2,1},{3,2},{4,3},{5,4},{6,5},{7,6},{8,15},{9,8},{10,9... | collective-permute-start | bytes 110600 | tf_op jit(solution)/shard_map/ppermute | solution.py:376
  5.9 0.4 shard_map.119
  6.3 1.8 %shard_map.120 = (f32[129,32,256]{2,1,0:T(8,128)S(1)}, f32[128,32,256]{2,1,0:T(8,128)S(1)}) custom-call(bf16[2048,128]{1,0:T(8,128)(2,1)S(1)} %get-tuple-element.35.rearranged, bf16[64,256]{1,0:T(8,128)(2,1)S(1)} %get-tuple-element.36.encode, bf16[1,256,256]{2,1,0:T(8,128)(2,1)S(1)} %get-tuple-element.37.send, bf16[1,256,256]{2,1,0:T(8,128)(2,1)S(1)} %get-tuple-element.38.receive), custom_call_target="tpu_custom_call" | custom-call | flops 1073741824 | bytes 1048576 | tf_op jit(solution)/shard_map/pallas_call | solution.py:43
  8.1 0.0 collective-permute-done.before
  8.1 0.0 collective-permute-done.1.after
  8.1 0.4 shard_map.121
  8.5 0.0 copy-start
  8.6 0.0 copy-start.1
  8.6 0.0 copy-start.3
  8.6 0.0 copy-start.4
  8.6 0.0 copy-start.5
  8.6 0.1 collective-permute-start.4
  8.7 3.5 %collective-permute-start.5 = (bf16[656,128]{1,0:T(8,128)(2,1)S(1)}, bf16[656,128]{1,0:T(8,128)(2,1)S(1)}, u32[]{:S(2)}, u32[]{:S(2)}) collective-permute-start(bf16[656,128]{1,0:T(8,128)(2,1)S(1)} %get-tuple-element.48), channel_id=1, source_target_pairs={{0,7},{1,0},{2,1},{3,2},{4,3},{5,4},{6,5},{7,6},{8,15},{9,8},{10,9... | collective-permute-start | bytes 503816 | tf_op jit(solution)/shard_map/ppermute | solution.py:376
  12.2 0.0 copy-done.2
  12.2 4.0 %shard_map.122 = (f32[129,32,256]{2,1,0:T(8,128)S(1)}, s32[529]{0:T(1024)S(1)}) custom-call(s32[4,128]{1,0:T(4,128)S(1)} %bitcast.2, f32[129,32,256]{2,1,0:T(8,128)S(1)} %get-tuple-element.43.sent, f32[128,32,256]{2,1,0:T(8,128)S(1)} %get-tuple-element.44.received), custom_call_target="tpu_custom_call" | custom-call | flops 2147483648 | bytes 1048576 | tf_op jit(solution)/shard_map/pallas_call | solution.py:43
  16.2 2.0 %collective-permute-start.2 = (bf16[432,128]{1,0:T(8,128)(2,1)S(1)}, bf16[432,128]{1,0:T(8,128)(2,1)S(1)}, u32[]{:S(2)}, u32[]{:S(2)}) collective-permute-start(bf16[432,128]{1,0:T(8,128)(2,1)S(1)} %get-tuple-element.46), channel_id=1, source_target_pairs={{0,8},{8,16},{16,24},{24,0},{1,9},{9,17},{17,25},{25,1},{2,10},{10... | collective-permute-start | bytes 331784 | tf_op jit(solution)/shard_map/ppermute | solution.py:376
  18.2 1.0 %collective-permute-start.3 = (bf16[432,128]{1,0:T(8,128)(2,1)S(1)}, bf16[432,128]{1,0:T(8,128)(2,1)S(1)}, u32[]{:S(2)}, u32[]{:S(2)}) collective-permute-start(bf16[432,128]{1,0:T(8,128)(2,1)S(1)} %get-tuple-element.46), channel_id=1, source_target_pairs={{0,24},{8,0},{16,8},{24,16},{1,25},{9,1},{17,9},{25,17},{2,26},{10... | collective-permute-start | bytes 331784 | tf_op jit(solution)/shard_map/ppermute | solution.py:376
  19.2 0.0 collective-permute-done.4.from_before
  19.2 0.0 collective-permute-done.5.from_after
  19.3 0.0 copy-done
  19.3 0.0 copy-done.1
  19.3 0.0 copy-done.3
  19.3 0.0 copy-done.4
  19.3 0.0 copy-done.5
  19.3 0.0 copy-start.6
  19.3 5.0 %shard_map.124 = (bf16[32,2048]{1,0:T(8,128)(2,1)S(1)}, bf16[32,2048]{1,0:T(8,128)(2,1)S(1)}, bf16[32,2048]{1,0:T(8,128)(2,1)S(1)}, bf16[32,2048]{1,0:T(8,128)(2,1)S(1)}, f32[129,32,256]{2,1,0:T(8,128)S(1)}) custom-call(s32[529]{0:T(1024)S(1)} %get-tuple-element.49.halo_edges_far, ...), custom_call_target="tpu_custom_call", output_to_operand_aliasing={{4}: (3, {})} | custom-call | flops 4294967296 | bytes 1048576 | tf_op jit(solution)/shard_map/pallas_call | solution.py:43
  24.3 1.1 %collective-permute-start.6 = (bf16[32,2048]{1,0:T(8,128)(2,1)S(1)}, bf16[32,2048]{1,0:T(8,128)(2,1)S(1)}, u32[]{:S(2)}, u32[]{:S(2)}) collective-permute-start(bf16[32,2048]{1,0:T(8,128)(2,1)S(1)} %get-tuple-element.52), channel_id=1, source_target_pairs={{0,8},{8,0},{16,24},{24,16},{1,9},{9,1},{17,25},{25,17},{2,10},{10... | collective-permute-start | bytes 393224 | tf_op jit(solution)/shard_map/ppermute | solution.py:394
  25.4 1.5 %collective-permute-start.7 = (bf16[32,2048]{1,0:T(8,128)(2,1)S(1)}, bf16[32,2048]{1,0:T(8,128)(2,1)S(1)}, u32[]{:S(2)}, u32[]{:S(2)}) collective-permute-start(bf16[32,2048]{1,0:T(8,128)(2,1)S(1)} %get-tuple-element.53), channel_id=1, source_target_pairs={{0,16},{8,24},{16,0},{24,8},{1,17},{9,25},{17,1},{25,9},{2,18},{10... | collective-permute-start | bytes 393224 | tf_op jit(solution)/shard_map/ppermute | solution.py:394
  26.9 1.0 %collective-permute-start.8 = (bf16[32,2048]{1,0:T(8,128)(2,1)S(1)}, bf16[32,2048]{1,0:T(8,128)(2,1)S(1)}, u32[]{:S(2)}, u32[]{:S(2)}) collective-permute-start(bf16[32,2048]{1,0:T(8,128)(2,1)S(1)} %get-tuple-element.54), channel_id=1, source_target_pairs={{0,24},{8,16},{16,8},{24,0},{1,25},{9,17},{17,9},{25,1},{2,26},{10... | collective-permute-start | bytes 393224 | tf_op jit(solution)/shard_map/ppermute | solution.py:394
  27.9 0.0 collective-permute-done.2.up
  27.9 0.0 collective-permute-done.3.down
  27.9 0.0 copy-done.6
  27.9 3.6 %shard_map.123.weights = bf16[128,256]{1,0:T(8,128)(2,1)S(1)} custom-call(s32[1,8]{1,0:T(1,128)S(1)} %copy-done.6, bf16[144,128]{1,0:T(8,128)(2,1)S(1)} %get-tuple-element.32.own, bf16[144,128]{1,0:T(8,128)(2,1)S(1)} %collective-permute-done.before, bf16[144,128]{1,0:T(8,128)(2,1)S(1)} %collective-permute-done.1.after, ...), custom_call_target="tpu_custom_call" | custom-call | flops 1073741824 | bytes 1048576 | tf_op jit(solution)/shard_map/pallas_call | solution.py:43
  31.6 0.0 collective-permute-done.6.refs_1_
  31.6 0.0 collective-permute-done.7.refs_2_
  31.6 2.2 %collective-permute-done.8.refs_3_ = bf16[32,2048]{1,0:T(8,128)(2,1)S(1)} collective-permute-done((bf16[32,2048]{1,0:T(8,128)(2,1)S(1)}, bf16[32,2048]{1,0:T(8,128)(2,1)S(1)}, u32[]{:S(2)}, u32[]{:S(2)}) %collective-permute-start.8) | collective-permute-done | bytes 131104 | tf_op jit(solution)/shard_map/ppermute | solution.py:394
  33.8 0.3 shard_map.125
  34.1 2.0 %collective-permute-start.9 = (bf16[32,2048]{1,0:T(8,128)(2,1)S(1)}, bf16[32,2048]{1,0:T(8,128)(2,1)S(1)}, u32[]{:S(2)}, u32[]{:S(2)}) collective-permute-start(bf16[32,2048]{1,0:T(8,128)(2,1)S(1)} %get-tuple-element.56), channel_id=1, source_target_pairs={{0,8},{8,0},{16,24},{24,16},{1,9},{9,1},{17,25},{25,17},{2,10},{10... | collective-permute-start | bytes 393224 | tf_op jit(solution)/shard_map/ppermute | solution.py:394
  36.1 0.0 collective-permute-start.10
  36.1 1.5 %collective-permute-start.11 = (bf16[32,2048]{1,0:T(8,128)(2,1)S(1)}, bf16[32,2048]{1,0:T(8,128)(2,1)S(1)}, u32[]{:S(2)}, u32[]{:S(2)}) collective-permute-start(bf16[32,2048]{1,0:T(8,128)(2,1)S(1)} %get-tuple-element.58), channel_id=1, source_target_pairs={{0,24},{8,16},{16,8},{24,0},{1,25},{9,17},{17,9},{25,1},{2,26},{10... | collective-permute-start | bytes 393224 | tf_op jit(solution)/shard_map/ppermute | solution.py:394
  37.6 1.5 %collective-permute-done.9.refs_1_ = bf16[32,2048]{1,0:T(8,128)(2,1)S(1)} collective-permute-done((bf16[32,2048]{1,0:T(8,128)(2,1)S(1)}, bf16[32,2048]{1,0:T(8,128)(2,1)S(1)}, u32[]{:S(2)}, u32[]{:S(2)}) %collective-permute-start.9) | collective-permute-done | bytes 131104 | tf_op jit(solution)/shard_map/ppermute | solution.py:394
  39.1 3.4 %collective-permute-done.10.refs_2_ = bf16[32,2048]{1,0:T(8,128)(2,1)S(1)} collective-permute-done((bf16[32,2048]{1,0:T(8,128)(2,1)S(1)}, bf16[32,2048]{1,0:T(8,128)(2,1)S(1)}, u32[]{:S(2)}, u32[]{:S(2)}) %collective-permute-start.10) | collective-permute-done | bytes 131104 | tf_op jit(solution)/shard_map/ppermute | solution.py:394
  42.5 0.0 collective-permute-done.11.refs_3_
  42.5 1.3 %shard_map.126 = bf16[32,64,128]{2,1,0:T(8,128)(2,1)} custom-call(bf16[32,2048]{1,0:T(8,128)(2,1)S(1)} %get-tuple-element.55.refs_0_, bf16[32,2048]{1,0:T(8,128)(2,1)S(1)} %collective-permute-done.9.refs_1_, bf16[32,2048]{1,0:T(8,128)(2,1)S(1)} %collective-permute-done.10.refs_2_, bf16[32,2048]{1,0:T(8,128)(2,1)S(1)} %collective-permute-done.11.refs_3_), custom_call_target="tpu_custom_call" | custom-call | flops 1048576 | bytes 1048576 | tf_op jit(solution)/shard_map/pallas_call | solution.py:43
Async XLA Ops:
  0.0 12.2 %copy-start.2 = (s32[128,4]{0,1:T(4,128)S(1)}, s32[128,4]{0,1:T(4,128)}, u32[]{:S(2)}) copy-start(s32[128,4]{0,1:T(4,128)} %param.19) | copy-start | bytes 6148
  1.3 6.8 %collective-permute-start = (bf16[144,128]{1,0:T(8,128)(2,1)S(1)}, bf16[144,128]{1,0:T(8,128)(2,1)S(1)}, u32[]{:S(2)}, u32[]{:S(2)}) collective-permute-start(bf16[144,128]{1,0:T(8,128)(2,1)S(1)} %get-tuple-element.32.own), channel_id=1, source_target_pairs={{0,1},{1,2},{2,3},{3,4},{4,5},{5,6},{6,7},{7,0},{8,9},{9,10},{10,1... | collective-permute-start | bytes 110600 | tf_op jit(solution)/shard_map/ppermute | solution.py:376
  1.8 6.3 %collective-permute-start.1 = (bf16[144,128]{1,0:T(8,128)(2,1)S(1)}, bf16[144,128]{1,0:T(8,128)(2,1)S(1)}, u32[]{:S(2)}, u32[]{:S(2)}) collective-permute-start(bf16[144,128]{1,0:T(8,128)(2,1)S(1)} %get-tuple-element.32.own), channel_id=1, source_target_pairs={{0,7},{1,0},{2,1},{3,2},{4,3},{5,4},{6,5},{7,6},{8,15},{9,8},{10,9... | collective-permute-start | bytes 110600 | tf_op jit(solution)/shard_map/ppermute | solution.py:376
  8.5 10.7 %copy-start = (bf16[1,256,256]{2,1,0:T(8,128)(2,1)S(1)}, bf16[1,256,256]{2,1,0:T(8,128)(2,1)}, u32[]{:S(2)}) copy-start(bf16[1,256,256]{2,1,0:T(8,128)(2,1)} %send.3) | copy-start | bytes 393220
  8.6 10.7 %copy-start.1 = (bf16[64,256]{1,0:T(8,128)(2,1)S(1)}, bf16[64,256]{1,0:T(8,128)(2,1)}, u32[]{:S(2)}) copy-start(bf16[64,256]{1,0:T(8,128)(2,1)} %encode.3) | copy-start | bytes 98308
  8.6 10.7 %copy-start.3 = (bf16[1,256,256]{2,1,0:T(8,128)(2,1)S(1)}, bf16[1,256,256]{2,1,0:T(8,128)(2,1)}, u32[]{:S(2)}) copy-start(bf16[1,256,256]{2,1,0:T(8,128)(2,1)} %update.1) | copy-start | bytes 393220
  8.6 10.7 %copy-start.4 = (bf16[256,64]{0,1:T(8,128)(2,1)S(1)}, bf16[256,64]{0,1:T(8,128)(2,1)}, u32[]{:S(2)}) copy-start(bf16[256,64]{0,1:T(8,128)(2,1)} %param.18) | copy-start | bytes 98308
  8.6 10.7 %copy-start.5 = (bf16[1,256]{1,0:T(2,128)(2,1)S(1)}, bf16[1,256]{1,0:T(2,128)(2,1)}, u32[]{:S(2)}) copy-start(bf16[1,256]{1,0:T(2,128)(2,1)} %gain.1) | copy-start | bytes 1540
  8.6 10.6 %collective-permute-start.4 = (bf16[656,128]{1,0:T(8,128)(2,1)S(1)}, bf16[656,128]{1,0:T(8,128)(2,1)S(1)}, u32[]{:S(2)}, u32[]{:S(2)}) collective-permute-start(bf16[656,128]{1,0:T(8,128)(2,1)S(1)} %get-tuple-element.47), channel_id=1, source_target_pairs={{0,1},{1,2},{2,3},{3,4},{4,5},{5,6},{6,7},{7,0},{8,9},{9,10},{10,1... | collective-permute-start | bytes 503816 | tf_op jit(solution)/shard_map/ppermute | solution.py:376
  8.7 10.6 %collective-permute-start.5 = (bf16[656,128]{1,0:T(8,128)(2,1)S(1)}, bf16[656,128]{1,0:T(8,128)(2,1)S(1)}, u32[]{:S(2)}, u32[]{:S(2)}) collective-permute-start(bf16[656,128]{1,0:T(8,128)(2,1)S(1)} %get-tuple-element.48), channel_id=1, source_target_pairs={{0,7},{1,0},{2,1},{3,2},{4,3},{5,4},{6,5},{7,6},{8,15},{9,8},{10,9... | collective-permute-start | bytes 503816 | tf_op jit(solution)/shard_map/ppermute | solution.py:376
  16.2 11.7 %collective-permute-start.2 = (bf16[432,128]{1,0:T(8,128)(2,1)S(1)}, bf16[432,128]{1,0:T(8,128)(2,1)S(1)}, u32[]{:S(2)}, u32[]{:S(2)}) collective-permute-start(bf16[432,128]{1,0:T(8,128)(2,1)S(1)} %get-tuple-element.46), channel_id=1, source_target_pairs={{0,8},{8,16},{16,24},{24,0},{1,9},{9,17},{17,25},{25,1},{2,10},{10... | collective-permute-start | bytes 331784 | tf_op jit(solution)/shard_map/ppermute | solution.py:376
  18.2 9.7 %collective-permute-start.3 = (bf16[432,128]{1,0:T(8,128)(2,1)S(1)}, bf16[432,128]{1,0:T(8,128)(2,1)S(1)}, u32[]{:S(2)}, u32[]{:S(2)}) collective-permute-start(bf16[432,128]{1,0:T(8,128)(2,1)S(1)} %get-tuple-element.46), channel_id=1, source_target_pairs={{0,24},{8,0},{16,8},{24,16},{1,25},{9,1},{17,9},{25,17},{2,26},{10... | collective-permute-start | bytes 331784 | tf_op jit(solution)/shard_map/ppermute | solution.py:376
  19.3 8.6 %copy-start.6 = (s32[1,8]{1,0:T(1,128)S(1)}, s32[1,8]{1,0:T(1,128)}, u32[]{:S(2)}) copy-start(s32[1,8]{1,0:T(1,128)} %neighbours.1) | copy-start | bytes 100
  24.3 7.2 %collective-permute-start.6 = (bf16[32,2048]{1,0:T(8,128)(2,1)S(1)}, bf16[32,2048]{1,0:T(8,128)(2,1)S(1)}, u32[]{:S(2)}, u32[]{:S(2)}) collective-permute-start(bf16[32,2048]{1,0:T(8,128)(2,1)S(1)} %get-tuple-element.52), channel_id=1, source_target_pairs={{0,8},{8,0},{16,24},{24,16},{1,9},{9,1},{17,25},{25,17},{2,10},{10... | collective-permute-start | bytes 393224 | tf_op jit(solution)/shard_map/ppermute | solution.py:394
  25.4 6.2 %collective-permute-start.7 = (bf16[32,2048]{1,0:T(8,128)(2,1)S(1)}, bf16[32,2048]{1,0:T(8,128)(2,1)S(1)}, u32[]{:S(2)}, u32[]{:S(2)}) collective-permute-start(bf16[32,2048]{1,0:T(8,128)(2,1)S(1)} %get-tuple-element.53), channel_id=1, source_target_pairs={{0,16},{8,24},{16,0},{24,8},{1,17},{9,25},{17,1},{25,9},{2,18},{10... | collective-permute-start | bytes 393224 | tf_op jit(solution)/shard_map/ppermute | solution.py:394
  26.9 6.8 %collective-permute-start.8 = (bf16[32,2048]{1,0:T(8,128)(2,1)S(1)}, bf16[32,2048]{1,0:T(8,128)(2,1)S(1)}, u32[]{:S(2)}, u32[]{:S(2)}) collective-permute-start(bf16[32,2048]{1,0:T(8,128)(2,1)S(1)} %get-tuple-element.54), channel_id=1, source_target_pairs={{0,24},{8,16},{16,8},{24,0},{1,25},{9,17},{17,9},{25,1},{2,26},{10... | collective-permute-start | bytes 393224 | tf_op jit(solution)/shard_map/ppermute | solution.py:394
  34.1 5.0 %collective-permute-start.9 = (bf16[32,2048]{1,0:T(8,128)(2,1)S(1)}, bf16[32,2048]{1,0:T(8,128)(2,1)S(1)}, u32[]{:S(2)}, u32[]{:S(2)}) collective-permute-start(bf16[32,2048]{1,0:T(8,128)(2,1)S(1)} %get-tuple-element.56), channel_id=1, source_target_pairs={{0,8},{8,0},{16,24},{24,16},{1,9},{9,1},{17,25},{25,17},{2,10},{10... | collective-permute-start | bytes 393224 | tf_op jit(solution)/shard_map/ppermute | solution.py:394
  36.1 6.4 %collective-permute-start.10 = (bf16[32,2048]{1,0:T(8,128)(2,1)S(1)}, bf16[32,2048]{1,0:T(8,128)(2,1)S(1)}, u32[]{:S(2)}, u32[]{:S(2)}) collective-permute-start(bf16[32,2048]{1,0:T(8,128)(2,1)S(1)} %get-tuple-element.57), channel_id=1, source_target_pairs={{0,16},{8,24},{16,0},{24,8},{1,17},{9,25},{17,1},{25,9},{2,18},{10... | collective-permute-start | bytes 393224 | tf_op jit(solution)/shard_map/ppermute | solution.py:394
  36.1 6.4 %collective-permute-start.11 = (bf16[32,2048]{1,0:T(8,128)(2,1)S(1)}, bf16[32,2048]{1,0:T(8,128)(2,1)S(1)}, u32[]{:S(2)}, u32[]{:S(2)}) collective-permute-start(bf16[32,2048]{1,0:T(8,128)(2,1)S(1)} %get-tuple-element.58), channel_id=1, source_target_pairs={{0,24},{8,16},{16,8},{24,0},{1,25},{9,17},{17,9},{25,1},{2,26},{10... | collective-permute-start | bytes 393224 | tf_op jit(solution)/shard_map/ppermute | solution.py:394

commit v4 on v3

--- a/solution.py
+++ b/solution.py
@@ -209,11 +209,8 @@
 ):
     *outs, messages, extended, halo_edges, sems = outputs
     (listed,) = start_copies(sems, (halo_edges_far, halo_edges))
-    targets, _ = partners("member")
     nodes, members, hidden = received.shape
     half = members // 2
-    regions = len(outs)
-    channels = decode.shape[0]
     both = block_diagonal(encode[...])
     send_half = send[0] * 0.5
     for side, source in enumerate((from_before, from_after)):
@@ -237,16 +234,26 @@
         return carry
 
     lax.fori_loop(0, (halo_edges[halo_edges.shape[0] - 1] + BATCH - 1) // BATCH, batch, 0)
+    forecast_kernel(range(1, len(outs) + 1), messages, rearranged, encode, update, gain, decode, *outs)
+
+
+def forecast_kernel(pieces, messages, rearranged, encode, update, gain, decode, *outs):
+    members, hidden = messages.shape[1:]
+    half = members // 2
+    channels = decode.shape[0]
+    targets, _ = partners("member")
+    chunk = rearranged.shape[0] // half // len(targets)
+    nodes = chunk * len(outs)
+    both = block_diagonal(encode[...])
     zero = jnp.zeros_like(decode[...])
     decode_even = jnp.concatenate([decode[...], zero], axis=0)
     decode_odd = jnp.concatenate([zero, decode[...]], axis=0)
     gains = gain[...].astype(F32)
-    chunk = nodes // regions
     pairs = chunk // 2
     width = 2 * channels
     average = jnp.full((hidden, width), 1.0 / hidden, BF16)
     low = lax.broadcasted_iota(jnp.int32, (nodes // 2, half, width), 2) < channels
-    bases = [target * chunk for target in targets]
+    bases = [target * chunk for target in [targets[piece] for piece in pieces]]
     fields = jnp.concatenate(
         [rearranged[pl.ds(pl.multiple_of(base * half, chunk * half), chunk * half), :] for base in bases], axis=0
     )
@@ -272,7 +279,9 @@
             out[:, pair * width : (pair + 1) * width] = forecast[index * pairs + pair]
 
 
-def weights_kernel(neighbours, own, before, after, up, down, from_before, from_after, out):
+def weights_kernel(neighbours, own, before, after, up, down, from_before, from_after, *refs):
+    *forecast, out, piece = refs
+    forecast_kernel([0], *forecast, piece)
     rows, ensemble = own.shape
     first = from_before.shape[0] - rows
     row_count, column_count = lax.axis_size("member"), lax.axis_size("space")
@@ -342,31 +351,43 @@
             out[:, start : start + step_width] = analysed[index * members : (index + 1) * members]
 
 
-def output_kernel(*refs):
-    *pieces, far, out, held, scratch, sems = refs
-    count = len(pieces)
+def stage(piece, region, staged):
+    members, width = piece.shape
+    half = members // 2
+    lanes = staged.shape[2]
+    low = lax.broadcasted_iota(jnp.int32, (half, lanes), 1) < lanes // 2
+    for pair in range(width // lanes):
+        block = piece[:, pair * lanes : (pair + 1) * lanes].astype(F32)
+        first, second = block[:half], block[half:]
+        row = 2 * pair * half
+        staged[region, row : row + half, :] = jnp.where(low, first, pltpu.roll(second, lanes // 2, 1))
+        staged[region, row + half : row + 2 * half, :] = jnp.where(low, pltpu.roll(first, lanes // 2, 1), second)
+
+
+def stage_kernel(*refs):
+    *pieces, staged = refs
+    _, origins = partners("member")
+    for index, piece in enumerate(pieces):
+        stage(piece, origins[index], staged)
+
+
+def output_kernel(piece, _, far, staged, out, sems):
+    _, origins = partners("member")
+    stage(piece, origins[len(origins) - 1], staged)
     members, channels, nodes = out.shape
     half = members // 2
-    low = lax.broadcasted_iota(jnp.int32, (half, 2 * channels), 1) < channels
-    chunk = nodes // count
-    for index, piece in enumerate(pieces):
-        held[partners("member")[1][index]] = piece[...]
-    for region in range(count):
-        for pair in range(chunk // 2):
-            block = held[region, :, pair * 2 * channels : (pair + 1) * 2 * channels].astype(F32)
-            first, second = block[:half], block[half:]
-            row = (region * chunk + 2 * pair) * half
-            scratch[row : row + half, :] = jnp.where(low, first, pltpu.roll(second, channels, 1))
-            scratch[row + half : row + 2 * half, :] = jnp.where(low, pltpu.roll(first, channels, 1), second)
+    chunk = nodes // len(origins)
     copies = []
     for pair in range(half):
-        block = scratch[pl.ds(pair, nodes, stride=half), :].T.astype(BF16)
+        block = jnp.concatenate(
+            [staged[region, pl.ds(pair, chunk, stride=half), :] for region in range(len(origins))], axis=0
+        ).T.astype(BF16)
         out[pair] = block[:channels]
         out[pair + half] = block[channels:]
         if (pair + 1) % OUTPUT_STEP == 0:
-            step = pair // OUTPUT_STEP
-            parts = [slice(start, start + OUTPUT_STEP) for start in (pair + 1 - OUTPUT_STEP, pair + 1 - OUTPUT_STEP + half)]
-            copies += start_copies(sems.at[step], *((out.at[part], far.at[part]) for part in parts))
+            start = pair + 1 - OUTPUT_STEP
+            parts = [slice(first, first + OUTPUT_STEP) for first in (start, start + half)]
+            copies += start_copies(sems.at[pair // OUTPUT_STEP], *((out.at[part], far.at[part]) for part in parts))
     for copy in copies:
         copy.wait()
 
@@ -434,7 +455,6 @@
         flops=1 << 24,
     )
     before = ring(own, "space", 1)
-    after = ring(own, "space", -1)
     fields, *weights = placed_in(pltpu.VMEM, *near)
     columns, rearranged = call(
         columns_kernel,
@@ -443,6 +463,8 @@
         scratch=[pltpu.VMEM((nodes * half, 2 * channels), F32)],
         flops=1 << 28,
     )
+    own_again, _ = lax.optimization_barrier((own, columns))
+    after = ring(own_again, "space", -1)
     sent, received = call(
         own_kernel,
         (pltpu.VMEM((nodes + 1, members, hidden), F32), pltpu.VMEM((nodes, members, hidden), F32)),
@@ -477,9 +499,10 @@
     down = ring(column, "member", -1)
     width = nodes // groups * channels
     piece = struct((members, width), BF16)
-    *predicted, _ = call(
+    shared = (rearranged, encode_weight, update_weight, norm_gain, decode_weight.T)
+    *predicted, messages = call(
         functools.partial(message_kernel, halo_count),
-        (piece,) * groups + (struct(started.shape, F32),),
+        (piece,) * (groups - 1) + (pltpu.VMEM(started.shape, F32),),
         (
             halo_edges,
             rearranged,
@@ -499,36 +522,54 @@
             pltpu.SemaphoreType.DMA((1,)),
         ],
         flops=1 << 32,
-        aliases={3: groups},
-    )
-    states = exchange(predicted, "member")
-    weights = call(
+        aliases={3: groups - 1},
+    )
+    predicted = exchange([None, *predicted], "member")
+    weights, kept = call(
         weights_kernel,
-        struct((ensemble, 2 * ensemble), BF16),
-        (region_neighbours, own, before, after, up, down, from_before, from_after),
-        specs=[SMEM] + [VMEM] * 7,
+        (struct((ensemble, 2 * ensemble), BF16), piece),
+        (
+            region_neighbours,
+            own,
+            before,
+            after,
+            up,
+            down,
+            from_before,
+            from_after,
+            *placed_in(pltpu.VMEM, messages),
+            *shared,
+        ),
+        specs=[SMEM] + [VMEM] * (8 + len(shared)),
         flops=1 << 30,
     )
+    states = (kept, *predicted[1:])
     analysed = call(
         analysis_kernel,
         (piece,) * groups,
         (weights, *states),
         flops=1 << 28,
     )
-    returned = exchange(analysed, "member")
-    return call(
+    *early_pieces, last_piece = exchange(analysed, "member")
+    staged = call(
+        stage_kernel,
+        pltpu.VMEM((groups, nodes // groups * half, 2 * channels), F32),
+        tuple(early_pieces),
+        flops=1 << 24,
+    )
+    analysis, _ = call(
         output_kernel,
-        struct((members, channels, nodes), BF16),
-        tuple(returned),
-        outs=HBM,
+        (struct((members, channels, nodes), BF16), pltpu.VMEM(staged.shape, F32)),
+        (last_piece, *placed_in(pltpu.VMEM, staged)),
+        outs=(HBM, VMEM),
         scratch=[
             pltpu.VMEM((members, channels, nodes), BF16),
-            pltpu.VMEM((groups, members, width), BF16),
-            pltpu.VMEM((nodes * half, 2 * channels), F32),
             pltpu.SemaphoreType.DMA((half // OUTPUT_STEP, 2)),
         ],
-        flops=1 << 20,
-    )
+        flops=1 << 24,
+        aliases={1: 1},
+    )
+    return analysis
 
 
 def solution(mesh):

time: 44 us -> 43.3 us (0.984)
  waiting for transfers between devices: 7.04 us -> 6.01 us
    ppermute x6, waiting for transfers between devices: 7.03 us -> 6 us  [exchange(): lax.ppermute(piece, axis, [(i, i ^ step if paired_up else (i + step) % co...]
    pallas_call x9 -> x10, Pallas kernels: 18.2 us -> 18.6 us  [call(): pl.pallas_call(kernel, out_shape=shapes, in_specs=specs or [VMEM] * len(i...]
  transfers between devices with their start and end apart: 12 -> 12, of which waited for: 3 -> 4; matrix products, arithmetic and copies ran while one was open for 0% -> 0% of each run, Pallas kernels for 34% -> 36%
where the time goes in v4:
time: 43.3 us; the launch traced here: 43.2 us
  Pallas kernels  18.6 us (43%)
  starting transfers between devices  18.3 us (42%)
  waiting for transfers between devices  6.01 us (14%)
    pallas_call x10, Pallas kernels, call(): pl.pallas_call(kernel, out_shape=shapes, in_specs=specs or [VMEM] * len(i...  18.6 us
    ppermute x6, starting transfers between devices, ring(): lax.ppermute(value, axis, [(i, (i + shift) % count) for i in range(count)])  11.2 us
    ppermute x6, starting transfers between devices, exchange(): lax.ppermute(piece, axis, [(i, i ^ step if paired_up else (i + step) % co...  7.11 us
    ppermute x6, waiting for transfers between devices, exchange(): lax.ppermute(piece, axis, [(i, i ^ step if paired_up else (i + step) % co...  6 us
  transfers between devices with their start and end apart: 12, of which 4 were waited for; matrix products, arithmetic and copies ran while one was open for 0% of the time, Pallas kernels for 36%

profile of v4, /device:TPU:0, one launch (start us, length us, event | category | flops | bytes accessed | tf_op | source)
XLA Modules:
  0.0 43.2 jit_solution(10790579472109195845)
XLA Ops:
  0.0 0.0 copy-start.4
  0.0 1.3 %shard_map.118 = (bf16[144,128]{1,0:T(8,128)(2,1)S(1)}, bf16[32,64,128]{2,1,0:T(8,128)(2,1)S(1)}, bf16[64,256]{1,0:T(8,128)(2,1)S(1)}, bf16[1,256,256]{2,1,0:T(8,128)(2,1)S(1)}, bf16[1,256,256]{2,1,0:T(8,128)(2,1)S(1)}) custom-call(bf16[1,128,256]{2,1,0:T(8,128)(2,1)} %perturbation.1, bf16[1,2,256]{2,1,0:T(2,128)(2,1)} %values.1, s32[2,32]{1,0:T(2,128)} %halo_nodes.1, ...), custom_call_target="tpu_custom_call" | custom-call | flops 16777216 | bytes 1048576 | tf_op jit(solution)/shard_map/pallas_call | solution.py:43
  1.3 0.5 %collective-permute-start = (bf16[144,128]{1,0:T(8,128)(2,1)S(1)}, bf16[144,128]{1,0:T(8,128)(2,1)S(1)}, u32[]{:S(2)}, u32[]{:S(2)}) collective-permute-start(bf16[144,128]{1,0:T(8,128)(2,1)S(1)} %get-tuple-element.39.own), channel_id=1, source_target_pairs={{0,1},{1,2},{2,3},{3,4},{4,5},{5,6},{6,7},{7,0},{8,9},{9,10},{10,1... | collective-permute-start | bytes 110600 | tf_op jit(solution)/shard_map/ppermute | solution.py:397
  1.8 0.4 shard_map.119
  2.2 4.1 %collective-permute-start.1 = (bf16[144,128]{1,0:T(8,128)(2,1)S(1)}, bf16[144,128]{1,0:T(8,128)(2,1)S(1)}, u32[]{:S(2)}, u32[]{:S(2)}) collective-permute-start(bf16[144,128]{1,0:T(8,128)(2,1)S(1)} %get-tuple-element.39.own), channel_id=1, source_target_pairs={{0,7},{1,0},{2,1},{3,2},{4,3},{5,4},{6,5},{7,6},{8,15},{9,8},{10,9... | collective-permute-start | bytes 110600 | tf_op jit(solution)/shard_map/ppermute | solution.py:397
  6.3 1.8 %shard_map.120 = (f32[129,32,256]{2,1,0:T(8,128)S(1)}, f32[128,32,256]{2,1,0:T(8,128)S(1)}) custom-call(bf16[2048,128]{1,0:T(8,128)(2,1)S(1)} %get-tuple-element.40.rearranged.refs_1_, bf16[64,256]{1,0:T(8,128)(2,1)S(1)} %get-tuple-element.41.encode, bf16[1,256,256]{2,1,0:T(8,128)(2,1)S(1)} %get-tuple-element.42.send, ...), custom_call_target="tpu_custom_call" | custom-call | flops 1073741824 | bytes 1048576 | tf_op jit(solution)/shard_map/pallas_call | solution.py:43
  8.1 0.0 collective-permute-done.before
  8.1 0.0 collective-permute-done.1.after
  8.1 0.4 shard_map.121
  8.5 0.0 copy-start
  8.6 0.0 copy-start.1
  8.6 0.0 copy-start.2
  8.6 0.0 copy-start.3
  8.6 0.0 copy-start.5
  8.6 0.3 collective-permute-start.4
  8.9 3.3 %collective-permute-start.5 = (bf16[656,128]{1,0:T(8,128)(2,1)S(1)}, bf16[656,128]{1,0:T(8,128)(2,1)S(1)}, u32[]{:S(2)}, u32[]{:S(2)}) collective-permute-start(bf16[656,128]{1,0:T(8,128)(2,1)S(1)} %get-tuple-element.53), channel_id=1, source_target_pairs={{0,7},{1,0},{2,1},{3,2},{4,3},{5,4},{6,5},{7,6},{8,15},{9,8},{10,9... | collective-permute-start | bytes 503816 | tf_op jit(solution)/shard_map/ppermute | solution.py:397
  12.2 0.0 copy-done.4
  12.2 4.0 %shard_map.122 = (f32[129,32,256]{2,1,0:T(8,128)S(1)}, s32[529]{0:T(1024)S(1)}) custom-call(s32[4,128]{1,0:T(4,128)S(1)} %bitcast.4, f32[129,32,256]{2,1,0:T(8,128)S(1)} %get-tuple-element.48.sent, f32[128,32,256]{2,1,0:T(8,128)S(1)} %get-tuple-element.49.received), custom_call_target="tpu_custom_call" | custom-call | flops 2147483648 | bytes 1048576 | tf_op jit(solution)/shard_map/pallas_call | solution.py:43
  16.2 3.0 %collective-permute-start.3 = (bf16[432,128]{1,0:T(8,128)(2,1)S(1)}, bf16[432,128]{1,0:T(8,128)(2,1)S(1)}, u32[]{:S(2)}, u32[]{:S(2)}) collective-permute-start(bf16[432,128]{1,0:T(8,128)(2,1)S(1)} %get-tuple-element.51), channel_id=1, source_target_pairs={{0,24},{8,0},{16,8},{24,16},{1,25},{9,1},{17,9},{25,17},{2,26},{10... | collective-permute-start | bytes 331784 | tf_op jit(solution)/shard_map/ppermute | solution.py:397
  19.2 0.0 collective-permute-start.2
  19.2 0.0 collective-permute-done.4.from_before
  19.2 0.0 collective-permute-done.5.from_after
  19.2 0.0 copy-done
  19.3 0.0 copy-done.1
  19.3 0.0 copy-done.2
  19.3 0.0 copy-done.3
  19.3 0.0 copy-done.5
  19.3 0.0 copy-start.6
  19.3 4.9 %shard_map.123 = (bf16[32,2048]{1,0:T(8,128)(2,1)S(1)}, bf16[32,2048]{1,0:T(8,128)(2,1)S(1)}, bf16[32,2048]{1,0:T(8,128)(2,1)S(1)}, f32[129,32,256]{2,1,0:T(8,128)S(1)}) custom-call(s32[529]{0:T(1024)S(1)} %get-tuple-element.54.halo_edges_far, bf16[2048,128]{1,0:T(8,128)(2,1)S(1)} %get-tuple-element.40.rearranged.refs_1_, ...), custom_call_target="tpu_custom_call", output_to_operand_aliasing={{3}: (3, {})} | custom-call | flops 4294967296 | bytes 1048576 | tf_op jit(solution)/shard_map/pallas_call | solution.py:43
  24.2 2.0 %collective-permute-start.6 = (bf16[32,2048]{1,0:T(8,128)(2,1)S(1)}, bf16[32,2048]{1,0:T(8,128)(2,1)S(1)}, u32[]{:S(2)}, u32[]{:S(2)}) collective-permute-start(bf16[32,2048]{1,0:T(8,128)(2,1)S(1)} %get-tuple-element.59), channel_id=1, source_target_pairs={{0,8},{8,0},{16,24},{24,16},{1,9},{9,1},{17,25},{25,17},{2,10},{10... | collective-permute-start | bytes 393224 | tf_op jit(solution)/shard_map/ppermute | solution.py:415
  26.2 1.5 %collective-permute-start.7 = (bf16[32,2048]{1,0:T(8,128)(2,1)S(1)}, bf16[32,2048]{1,0:T(8,128)(2,1)S(1)}, u32[]{:S(2)}, u32[]{:S(2)}) collective-permute-start(bf16[32,2048]{1,0:T(8,128)(2,1)S(1)} %get-tuple-element.60), channel_id=1, source_target_pairs={{0,16},{8,24},{16,0},{24,8},{1,17},{9,25},{17,1},{25,9},{2,18},{10... | collective-permute-start | bytes 393224 | tf_op jit(solution)/shard_map/ppermute | solution.py:415
  27.8 0.0 collective-permute-start.8
  27.8 0.0 collective-permute-done.3.down
  27.8 0.0 collective-permute-done.2.up
  27.8 0.0 copy-done.6
  27.8 4.1 %shard_map.124 = (bf16[128,256]{1,0:T(8,128)(2,1)S(1)}, bf16[32,2048]{1,0:T(8,128)(2,1)S(1)}) custom-call(s32[1,8]{1,0:T(1,128)S(1)} %copy-done.6, bf16[144,128]{1,0:T(8,128)(2,1)S(1)} %get-tuple-element.39.own, bf16[144,128]{1,0:T(8,128)(2,1)S(1)} %collective-permute-done.before, bf16[144,128]{1,0:T(8,128)(2,1)S(1)} %collective-permute-done.1.after, ...), custom_call_target="tpu_custom_call" | custom-call | flops 1073741824 | bytes 1048576 | tf_op jit(solution)/shard_map/pallas_call | solution.py:43
  31.9 0.0 collective-permute-done.6.refs_1_
  31.9 0.0 collective-permute-done.7.refs_2_
  31.9 3.2 %collective-permute-done.8.refs_3_ = bf16[32,2048]{1,0:T(8,128)(2,1)S(1)} collective-permute-done((bf16[32,2048]{1,0:T(8,128)(2,1)S(1)}, bf16[32,2048]{1,0:T(8,128)(2,1)S(1)}, u32[]{:S(2)}, u32[]{:S(2)}) %collective-permute-start.8) | collective-permute-done | bytes 131104 | tf_op jit(solution)/shard_map/ppermute | solution.py:415
  35.1 0.3 shard_map.125
  35.5 0.1 collective-permute-start.10
  35.5 0.2 collective-permute-start.11
  35.8 3.2 %collective-permute-start.9 = (bf16[32,2048]{1,0:T(8,128)(2,1)S(1)}, bf16[32,2048]{1,0:T(8,128)(2,1)S(1)}, u32[]{:S(2)}, u32[]{:S(2)}) collective-permute-start(bf16[32,2048]{1,0:T(8,128)(2,1)S(1)} %get-tuple-element.62), channel_id=1, source_target_pairs={{0,24},{8,16},{16,8},{24,0},{1,25},{9,17},{17,9},{25,1},{2,26},{10... | collective-permute-start | bytes 393224 | tf_op jit(solution)/shard_map/ppermute | solution.py:415
  39.0 1.5 %collective-permute-done.10.refs_1_ = bf16[32,2048]{1,0:T(8,128)(2,1)S(1)} collective-permute-done((bf16[32,2048]{1,0:T(8,128)(2,1)S(1)}, bf16[32,2048]{1,0:T(8,128)(2,1)S(1)}, u32[]{:S(2)}, u32[]{:S(2)}) %collective-permute-start.10) | collective-permute-done | bytes 131104 | tf_op jit(solution)/shard_map/ppermute | solution.py:415
  40.5 0.1 collective-permute-done.11.refs_2_
  40.6 0.2 shard_map.126._
  40.8 1.2 %collective-permute-done.9.piece = bf16[32,2048]{1,0:T(8,128)(2,1)S(1)} collective-permute-done((bf16[32,2048]{1,0:T(8,128)(2,1)S(1)}, bf16[32,2048]{1,0:T(8,128)(2,1)S(1)}, u32[]{:S(2)}, u32[]{:S(2)}) %collective-permute-start.9) | collective-permute-done | bytes 131104 | tf_op jit(solution)/shard_map/ppermute | solution.py:415
  42.0 1.2 %shard_map.127 = (bf16[32,64,128]{2,1,0:T(8,128)(2,1)}, f32[4,512,128]{2,1,0:T(8,128)S(1)}) custom-call(bf16[32,2048]{1,0:T(8,128)(2,1)S(1)} %collective-permute-done.9.piece, f32[4,512,128]{2,1,0:T(8,128)S(1)} %shard_map.126._), custom_call_target="tpu_custom_call", output_to_operand_aliasing={{1}: (1, {})} | custom-call | flops 16777216 | bytes 1048576 | tf_op jit(solution)/shard_map/pallas_call | solution.py:43
Async XLA Ops:
  0.0 12.2 %copy-start.4 = (s32[128,4]{0,1:T(4,128)S(1)}, s32[128,4]{0,1:T(4,128)}, u32[]{:S(2)}) copy-start(s32[128,4]{0,1:T(4,128)} %param.19) | copy-start | bytes 6148
  1.3 6.8 %collective-permute-start = (bf16[144,128]{1,0:T(8,128)(2,1)S(1)}, bf16[144,128]{1,0:T(8,128)(2,1)S(1)}, u32[]{:S(2)}, u32[]{:S(2)}) collective-permute-start(bf16[144,128]{1,0:T(8,128)(2,1)S(1)} %get-tuple-element.39.own), channel_id=1, source_target_pairs={{0,1},{1,2},{2,3},{3,4},{4,5},{5,6},{6,7},{7,0},{8,9},{9,10},{10,1... | collective-permute-start | bytes 110600 | tf_op jit(solution)/shard_map/ppermute | solution.py:397
  2.2 5.9 %collective-permute-start.1 = (bf16[144,128]{1,0:T(8,128)(2,1)S(1)}, bf16[144,128]{1,0:T(8,128)(2,1)S(1)}, u32[]{:S(2)}, u32[]{:S(2)}) collective-permute-start(bf16[144,128]{1,0:T(8,128)(2,1)S(1)} %get-tuple-element.39.own), channel_id=1, source_target_pairs={{0,7},{1,0},{2,1},{3,2},{4,3},{5,4},{6,5},{7,6},{8,15},{9,8},{10,9... | collective-permute-start | bytes 110600 | tf_op jit(solution)/shard_map/ppermute | solution.py:397
  8.5 10.7 %copy-start = (bf16[64,256]{1,0:T(8,128)(2,1)S(1)}, bf16[64,256]{1,0:T(8,128)(2,1)}, u32[]{:S(2)}) copy-start(bf16[64,256]{1,0:T(8,128)(2,1)} %refs_2_.1) | copy-start | bytes 98308
  8.6 10.7 %copy-start.1 = (bf16[1,256,256]{2,1,0:T(8,128)(2,1)S(1)}, bf16[1,256,256]{2,1,0:T(8,128)(2,1)}, u32[]{:S(2)}) copy-start(bf16[1,256,256]{2,1,0:T(8,128)(2,1)} %send.3) | copy-start | bytes 393220
  8.6 10.7 %copy-start.2 = (bf16[1,256,256]{2,1,0:T(8,128)(2,1)S(1)}, bf16[1,256,256]{2,1,0:T(8,128)(2,1)}, u32[]{:S(2)}) copy-start(bf16[1,256,256]{2,1,0:T(8,128)(2,1)} %refs_3_.1) | copy-start | bytes 393220
  8.6 10.7 %copy-start.3 = (bf16[256,64]{0,1:T(8,128)(2,1)S(1)}, bf16[256,64]{0,1:T(8,128)(2,1)}, u32[]{:S(2)}) copy-start(bf16[256,64]{0,1:T(8,128)(2,1)} %param.18) | copy-start | bytes 98308
  8.6 10.7 %copy-start.5 = (bf16[1,256]{1,0:T(2,128)(2,1)S(1)}, bf16[1,256]{1,0:T(2,128)(2,1)}, u32[]{:S(2)}) copy-start(bf16[1,256]{1,0:T(2,128)(2,1)} %refs_4_.1) | copy-start | bytes 1540
  8.6 10.6 %collective-permute-start.4 = (bf16[656,128]{1,0:T(8,128)(2,1)S(1)}, bf16[656,128]{1,0:T(8,128)(2,1)S(1)}, u32[]{:S(2)}, u32[]{:S(2)}) collective-permute-start(bf16[656,128]{1,0:T(8,128)(2,1)S(1)} %get-tuple-element.52), channel_id=1, source_target_pairs={{0,1},{1,2},{2,3},{3,4},{4,5},{5,6},{6,7},{7,0},{8,9},{9,10},{10,1... | collective-permute-start | bytes 503816 | tf_op jit(solution)/shard_map/ppermute | solution.py:397
  8.9 10.4 %collective-permute-start.5 = (bf16[656,128]{1,0:T(8,128)(2,1)S(1)}, bf16[656,128]{1,0:T(8,128)(2,1)S(1)}, u32[]{:S(2)}, u32[]{:S(2)}) collective-permute-start(bf16[656,128]{1,0:T(8,128)(2,1)S(1)} %get-tuple-element.53), channel_id=1, source_target_pairs={{0,7},{1,0},{2,1},{3,2},{4,3},{5,4},{6,5},{7,6},{8,15},{9,8},{10,9... | collective-permute-start | bytes 503816 | tf_op jit(solution)/shard_map/ppermute | solution.py:397
  16.2 11.5 %collective-permute-start.3 = (bf16[432,128]{1,0:T(8,128)(2,1)S(1)}, bf16[432,128]{1,0:T(8,128)(2,1)S(1)}, u32[]{:S(2)}, u32[]{:S(2)}) collective-permute-start(bf16[432,128]{1,0:T(8,128)(2,1)S(1)} %get-tuple-element.51), channel_id=1, source_target_pairs={{0,24},{8,0},{16,8},{24,16},{1,25},{9,1},{17,9},{25,17},{2,26},{10... | collective-permute-start | bytes 331784 | tf_op jit(solution)/shard_map/ppermute | solution.py:397
  19.2 8.6 %collective-permute-start.2 = (bf16[432,128]{1,0:T(8,128)(2,1)S(1)}, bf16[432,128]{1,0:T(8,128)(2,1)S(1)}, u32[]{:S(2)}, u32[]{:S(2)}) collective-permute-start(bf16[432,128]{1,0:T(8,128)(2,1)S(1)} %get-tuple-element.51), channel_id=1, source_target_pairs={{0,8},{8,16},{16,24},{24,0},{1,9},{9,17},{17,25},{25,1},{2,10},{10... | collective-permute-start | bytes 331784 | tf_op jit(solution)/shard_map/ppermute | solution.py:397
  19.3 8.5 %copy-start.6 = (s32[1,8]{1,0:T(1,128)S(1)}, s32[1,8]{1,0:T(1,128)}, u32[]{:S(2)}) copy-start(s32[1,8]{1,0:T(1,128)} %neighbours.1) | copy-start | bytes 100
  24.2 7.7 %collective-permute-start.6 = (bf16[32,2048]{1,0:T(8,128)(2,1)S(1)}, bf16[32,2048]{1,0:T(8,128)(2,1)S(1)}, u32[]{:S(2)}, u32[]{:S(2)}) collective-permute-start(bf16[32,2048]{1,0:T(8,128)(2,1)S(1)} %get-tuple-element.59), channel_id=1, source_target_pairs={{0,8},{8,0},{16,24},{24,16},{1,9},{9,1},{17,25},{25,17},{2,10},{10... | collective-permute-start | bytes 393224 | tf_op jit(solution)/shard_map/ppermute | solution.py:415
  26.2 5.7 %collective-permute-start.7 = (bf16[32,2048]{1,0:T(8,128)(2,1)S(1)}, bf16[32,2048]{1,0:T(8,128)(2,1)S(1)}, u32[]{:S(2)}, u32[]{:S(2)}) collective-permute-start(bf16[32,2048]{1,0:T(8,128)(2,1)S(1)} %get-tuple-element.60), channel_id=1, source_target_pairs={{0,16},{8,24},{16,0},{24,8},{1,17},{9,25},{17,1},{25,9},{2,18},{10... | collective-permute-start | bytes 393224 | tf_op jit(solution)/shard_map/ppermute | solution.py:415
  27.8 7.4 %collective-permute-start.8 = (bf16[32,2048]{1,0:T(8,128)(2,1)S(1)}, bf16[32,2048]{1,0:T(8,128)(2,1)S(1)}, u32[]{:S(2)}, u32[]{:S(2)}) collective-permute-start(bf16[32,2048]{1,0:T(8,128)(2,1)S(1)} %get-tuple-element.61), channel_id=1, source_target_pairs={{0,24},{8,16},{16,8},{24,0},{1,25},{9,17},{17,9},{25,1},{2,26},{10... | collective-permute-start | bytes 393224 | tf_op jit(solution)/shard_map/ppermute | solution.py:415
  35.5 5.0 %collective-permute-start.10 = (bf16[32,2048]{1,0:T(8,128)(2,1)S(1)}, bf16[32,2048]{1,0:T(8,128)(2,1)S(1)}, u32[]{:S(2)}, u32[]{:S(2)}) collective-permute-start(bf16[32,2048]{1,0:T(8,128)(2,1)S(1)} %get-tuple-element.64), channel_id=1, source_target_pairs={{0,8},{8,0},{16,24},{24,16},{1,9},{9,1},{17,25},{25,17},{2,10},{10... | collective-permute-start | bytes 393224 | tf_op jit(solution)/shard_map/ppermute | solution.py:415
  35.5 5.0 %collective-permute-start.11 = (bf16[32,2048]{1,0:T(8,128)(2,1)S(1)}, bf16[32,2048]{1,0:T(8,128)(2,1)S(1)}, u32[]{:S(2)}, u32[]{:S(2)}) collective-permute-start(bf16[32,2048]{1,0:T(8,128)(2,1)S(1)} %get-tuple-element.65), channel_id=1, source_target_pairs={{0,16},{8,24},{16,0},{24,8},{1,17},{9,25},{17,1},{25,9},{2,18},{10... | collective-permute-start | bytes 393224 | tf_op jit(solution)/shard_map/ppermute | solution.py:415
  35.8 6.2 %collective-permute-start.9 = (bf16[32,2048]{1,0:T(8,128)(2,1)S(1)}, bf16[32,2048]{1,0:T(8,128)(2,1)S(1)}, u32[]{:S(2)}, u32[]{:S(2)}) collective-permute-start(bf16[32,2048]{1,0:T(8,128)(2,1)S(1)} %get-tuple-element.62), channel_id=1, source_target_pairs={{0,24},{8,16},{16,8},{24,0},{1,25},{9,17},{17,9},{25,1},{2,26},{10... | collective-permute-start | bytes 393224 | tf_op jit(solution)/shard_map/ppermute | solution.py:415

commit v5 on v4

--- a/solution.py
+++ b/solution.py
@@ -279,7 +279,7 @@
             out[:, pair * width : (pair + 1) * width] = forecast[index * pairs + pair]
 
 
-def weights_kernel(neighbours, own, before, after, up, down, from_before, from_after, *refs):
+def weights_kernel(neighbours, own, before, after, down, up, from_before, from_after, *refs):
     *forecast, out, piece = refs
     forecast_kernel([0], *forecast, piece)
     rows, ensemble = own.shape
@@ -341,7 +341,7 @@
 
 def analysis_kernel(weights, *refs):
     count = len(refs) // 2
-    pieces, outs = refs[:count], refs[count:]
+    pieces, outs = refs[:count][::-1], refs[count:]
     members, width = pieces[0].shape
     step_width = 512
     for start in range(0, width, step_width):
@@ -364,16 +364,16 @@
         staged[region, row + half : row + 2 * half, :] = jnp.where(low, pltpu.roll(first, lanes // 2, 1), second)
 
 
-def stage_kernel(*refs):
+def stage_kernel(order, *refs):
     *pieces, staged = refs
     _, origins = partners("member")
-    for index, piece in enumerate(pieces):
+    for index, piece in zip(order, pieces):
         stage(piece, origins[index], staged)
 
 
-def output_kernel(piece, _, far, staged, out, sems):
+def output_kernel(last, piece, _, far, staged, out, sems):
     _, origins = partners("member")
-    stage(piece, origins[len(origins) - 1], staged)
+    stage(piece, origins[last], staged)
     members, channels, nodes = out.shape
     half = members // 2
     chunk = nodes // len(origins)
@@ -495,8 +495,8 @@
         flops=1 << 31,
     )
     column, started = lax.optimization_barrier((column, started))
+    down = ring(column, "member", -1)
     up = ring(column, "member", 1)
-    down = ring(column, "member", -1)
     width = nodes // groups * channels
     piece = struct((members, width), BF16)
     shared = (rearranged, encode_weight, update_weight, norm_gain, decode_weight.T)
@@ -533,8 +533,8 @@
             own,
             before,
             after,
+            down,
             up,
-            down,
             from_before,
             from_after,
             *placed_in(pltpu.VMEM, messages),
@@ -547,20 +547,22 @@
     analysed = call(
         analysis_kernel,
         (piece,) * groups,
-        (weights, *states),
+        (weights, *states[::-1]),
         flops=1 << 28,
     )
-    *early_pieces, last_piece = exchange(analysed, "member")
+    returned = exchange(analysed, "member")
+    *order, last = [*range(1, groups)][::-1]
+    order = [*order, 0]
     staged = call(
-        stage_kernel,
+        functools.partial(stage_kernel, order),
         pltpu.VMEM((groups, nodes // groups * half, 2 * channels), F32),
-        tuple(early_pieces),
+        tuple(returned[index] for index in order),
         flops=1 << 24,
     )
     analysis, _ = call(
-        output_kernel,
+        functools.partial(output_kernel, last),
         (struct((members, channels, nodes), BF16), pltpu.VMEM(staged.shape, F32)),
-        (last_piece, *placed_in(pltpu.VMEM, staged)),
+        (returned[last], *placed_in(pltpu.VMEM, staged)),
         outs=(HBM, VMEM),
         scratch=[
             pltpu.VMEM((members, channels, nodes), BF16),

time: 43.3 us -> 42.6 us (0.984)
  waiting for transfers between devices: 6.01 us -> 4.53 us
  starting transfers between devices: 18.3 us -> 19 us
    ppermute x6, waiting for transfers between devices: 6 us -> 4.51 us  [exchange(): lax.ppermute(piece, axis, [(i, i ^ step if paired_up else (i + step) % co...]
    ppermute x6, starting transfers between devices: 7.11 us -> 7.7 us  [exchange(): lax.ppermute(piece, axis, [(i, i ^ step if paired_up else (i + step) % co...]
  transfers between devices with their start and end apart: 12 -> 12, of which waited for: 4 -> 3; matrix products, arithmetic and copies ran while one was open for 0% -> 0% of each run, Pallas kernels for 36% -> 36%
where the time goes in v5:
time: 42.6 us; the launch traced here: 42.3 us
  starting transfers between devices  19 us (45%)
  Pallas kernels  18.6 us (44%)
  waiting for transfers between devices  4.53 us (11%)
    pallas_call x10, Pallas kernels, call(): pl.pallas_call(kernel, out_shape=shapes, in_specs=specs or [VMEM] * len(i...  18.6 us
    ppermute x6, starting transfers between devices, ring(): lax.ppermute(value, axis, [(i, (i + shift) % count) for i in range(count)])  11.3 us
    ppermute x6, starting transfers between devices, exchange(): lax.ppermute(piece, axis, [(i, i ^ step if paired_up else (i + step) % co...  7.7 us
    ppermute x6, waiting for transfers between devices, exchange(): lax.ppermute(piece, axis, [(i, i ^ step if paired_up else (i + step) % co...  4.51 us
  transfers between devices with their start and end apart: 12, of which 3 were waited for; matrix products, arithmetic and copies ran while one was open for 0% of the time, Pallas kernels for 36%

profile of v5, /device:TPU:0, one launch (start us, length us, event | category | flops | bytes accessed | tf_op | source)
XLA Modules:
  0.0 42.3 jit_solution(9845176076054855921)
XLA Ops:
  0.0 0.0 copy-start.4
  0.0 1.3 %shard_map.118 = (bf16[144,128]{1,0:T(8,128)(2,1)S(1)}, bf16[32,64,128]{2,1,0:T(8,128)(2,1)S(1)}, bf16[64,256]{1,0:T(8,128)(2,1)S(1)}, bf16[1,256,256]{2,1,0:T(8,128)(2,1)S(1)}, bf16[1,256,256]{2,1,0:T(8,128)(2,1)S(1)}) custom-call(bf16[1,128,256]{2,1,0:T(8,128)(2,1)} %perturbation.1, bf16[1,2,256]{2,1,0:T(2,128)(2,1)} %values.1, s32[2,32]{1,0:T(2,128)} %halo_nodes.1, ...), custom_call_target="tpu_custom_call" | custom-call | flops 16777216 | bytes 1048576 | tf_op jit(solution)/shard_map/pallas_call | solution.py:43
  1.3 0.5 %collective-permute-start = (bf16[144,128]{1,0:T(8,128)(2,1)S(1)}, bf16[144,128]{1,0:T(8,128)(2,1)S(1)}, u32[]{:S(2)}, u32[]{:S(2)}) collective-permute-start(bf16[144,128]{1,0:T(8,128)(2,1)S(1)} %get-tuple-element.39.own), channel_id=1, source_target_pairs={{0,1},{1,2},{2,3},{3,4},{4,5},{5,6},{6,7},{7,0},{8,9},{9,10},{10,1... | collective-permute-start | bytes 110600 | tf_op jit(solution)/shard_map/ppermute | solution.py:397
  1.8 0.4 shard_map.119
  2.2 4.1 %collective-permute-start.1 = (bf16[144,128]{1,0:T(8,128)(2,1)S(1)}, bf16[144,128]{1,0:T(8,128)(2,1)S(1)}, u32[]{:S(2)}, u32[]{:S(2)}) collective-permute-start(bf16[144,128]{1,0:T(8,128)(2,1)S(1)} %get-tuple-element.39.own), channel_id=1, source_target_pairs={{0,7},{1,0},{2,1},{3,2},{4,3},{5,4},{6,5},{7,6},{8,15},{9,8},{10,9... | collective-permute-start | bytes 110600 | tf_op jit(solution)/shard_map/ppermute | solution.py:397
  6.3 1.8 %shard_map.120 = (f32[129,32,256]{2,1,0:T(8,128)S(1)}, f32[128,32,256]{2,1,0:T(8,128)S(1)}) custom-call(bf16[2048,128]{1,0:T(8,128)(2,1)S(1)} %get-tuple-element.40.rearranged.refs_1_, bf16[64,256]{1,0:T(8,128)(2,1)S(1)} %get-tuple-element.41.encode, bf16[1,256,256]{2,1,0:T(8,128)(2,1)S(1)} %get-tuple-element.42.send, ...), custom_call_target="tpu_custom_call" | custom-call | flops 1073741824 | bytes 1048576 | tf_op jit(solution)/shard_map/pallas_call | solution.py:43
  8.1 0.0 collective-permute-done.before
  8.1 0.0 collective-permute-done.1.after
  8.1 0.4 shard_map.121
  8.5 0.0 copy-start
  8.6 0.0 copy-start.1
  8.6 0.0 copy-start.2
  8.6 0.0 copy-start.3
  8.6 0.0 copy-start.5
  8.6 0.3 collective-permute-start.4
  8.9 3.3 %collective-permute-start.5 = (bf16[656,128]{1,0:T(8,128)(2,1)S(1)}, bf16[656,128]{1,0:T(8,128)(2,1)S(1)}, u32[]{:S(2)}, u32[]{:S(2)}) collective-permute-start(bf16[656,128]{1,0:T(8,128)(2,1)S(1)} %get-tuple-element.53), channel_id=1, source_target_pairs={{0,7},{1,0},{2,1},{3,2},{4,3},{5,4},{6,5},{7,6},{8,15},{9,8},{10,9... | collective-permute-start | bytes 503816 | tf_op jit(solution)/shard_map/ppermute | solution.py:397
  12.2 0.0 copy-done.4
  12.2 4.0 %shard_map.122 = (f32[129,32,256]{2,1,0:T(8,128)S(1)}, s32[529]{0:T(1024)S(1)}) custom-call(s32[4,128]{1,0:T(4,128)S(1)} %bitcast.4, f32[129,32,256]{2,1,0:T(8,128)S(1)} %get-tuple-element.48.sent, f32[128,32,256]{2,1,0:T(8,128)S(1)} %get-tuple-element.49.received), custom_call_target="tpu_custom_call" | custom-call | flops 2147483648 | bytes 1048576 | tf_op jit(solution)/shard_map/pallas_call | solution.py:43
  16.2 2.0 %collective-permute-start.3 = (bf16[432,128]{1,0:T(8,128)(2,1)S(1)}, bf16[432,128]{1,0:T(8,128)(2,1)S(1)}, u32[]{:S(2)}, u32[]{:S(2)}) collective-permute-start(bf16[432,128]{1,0:T(8,128)(2,1)S(1)} %get-tuple-element.51), channel_id=1, source_target_pairs={{0,8},{8,16},{16,24},{24,0},{1,9},{9,17},{17,25},{25,1},{2,10},{10... | collective-permute-start | bytes 331784 | tf_op jit(solution)/shard_map/ppermute | solution.py:397
  18.3 1.0 %collective-permute-start.2 = (bf16[432,128]{1,0:T(8,128)(2,1)S(1)}, bf16[432,128]{1,0:T(8,128)(2,1)S(1)}, u32[]{:S(2)}, u32[]{:S(2)}) collective-permute-start(bf16[432,128]{1,0:T(8,128)(2,1)S(1)} %get-tuple-element.51), channel_id=1, source_target_pairs={{0,24},{8,0},{16,8},{24,16},{1,25},{9,1},{17,9},{25,17},{2,26},{10... | collective-permute-start | bytes 331784 | tf_op jit(solution)/shard_map/ppermute | solution.py:397
  19.3 0.0 collective-permute-done.4.from_before
  19.3 0.0 collective-permute-done.5.from_after
  19.3 0.0 copy-done
  19.3 0.0 copy-done.1
  19.3 0.0 copy-done.2
  19.3 0.0 copy-done.3
  19.3 0.0 copy-done.5
  19.3 0.0 copy-start.6
  19.4 4.9 %shard_map.123 = (bf16[32,2048]{1,0:T(8,128)(2,1)S(1)}, bf16[32,2048]{1,0:T(8,128)(2,1)S(1)}, bf16[32,2048]{1,0:T(8,128)(2,1)S(1)}, f32[129,32,256]{2,1,0:T(8,128)S(1)}) custom-call(s32[529]{0:T(1024)S(1)} %get-tuple-element.54.halo_edges_far, bf16[2048,128]{1,0:T(8,128)(2,1)S(1)} %get-tuple-element.40.rearranged.refs_1_, ...), custom_call_target="tpu_custom_call", output_to_operand_aliasing={{3}: (3, {})} | custom-call | flops 4294967296 | bytes 1048576 | tf_op jit(solution)/shard_map/pallas_call | solution.py:43
  24.3 2.0 %collective-permute-start.6 = (bf16[32,2048]{1,0:T(8,128)(2,1)S(1)}, bf16[32,2048]{1,0:T(8,128)(2,1)S(1)}, u32[]{:S(2)}, u32[]{:S(2)}) collective-permute-start(bf16[32,2048]{1,0:T(8,128)(2,1)S(1)} %get-tuple-element.58), channel_id=1, source_target_pairs={{0,24},{8,16},{16,8},{24,0},{1,25},{9,17},{17,9},{25,1},{2,26},{10... | collective-permute-start | bytes 393224 | tf_op jit(solution)/shard_map/ppermute | solution.py:415
  26.3 0.5 %collective-permute-start.7 = (bf16[32,2048]{1,0:T(8,128)(2,1)S(1)}, bf16[32,2048]{1,0:T(8,128)(2,1)S(1)}, u32[]{:S(2)}, u32[]{:S(2)}) collective-permute-start(bf16[32,2048]{1,0:T(8,128)(2,1)S(1)} %get-tuple-element.59), channel_id=1, source_target_pairs={{0,16},{8,24},{16,0},{24,8},{1,17},{9,25},{17,1},{25,9},{2,18},{10... | collective-permute-start | bytes 393224 | tf_op jit(solution)/shard_map/ppermute | solution.py:415
  26.8 1.0 %collective-permute-start.8 = (bf16[32,2048]{1,0:T(8,128)(2,1)S(1)}, bf16[32,2048]{1,0:T(8,128)(2,1)S(1)}, u32[]{:S(2)}, u32[]{:S(2)}) collective-permute-start(bf16[32,2048]{1,0:T(8,128)(2,1)S(1)} %get-tuple-element.60), channel_id=1, source_target_pairs={{0,8},{8,0},{16,24},{24,16},{1,9},{9,1},{17,25},{25,17},{2,10},{10... | collective-permute-start | bytes 393224 | tf_op jit(solution)/shard_map/ppermute | solution.py:415
  27.8 0.0 collective-permute-done.3.up
  27.8 0.0 collective-permute-done.2.down
  27.8 0.0 copy-done.6
  27.8 4.1 %shard_map.124 = (bf16[128,256]{1,0:T(8,128)(2,1)S(1)}, bf16[32,2048]{1,0:T(8,128)(2,1)S(1)}) custom-call(s32[1,8]{1,0:T(1,128)S(1)} %copy-done.6, bf16[144,128]{1,0:T(8,128)(2,1)S(1)} %get-tuple-element.39.own, bf16[144,128]{1,0:T(8,128)(2,1)S(1)} %collective-permute-done.before, bf16[144,128]{1,0:T(8,128)(2,1)S(1)} %collective-permute-done.1.after, ...), custom_call_target="tpu_custom_call" | custom-call | flops 1073741824 | bytes 1048576 | tf_op jit(solution)/shard_map/pallas_call | solution.py:43
  31.9 0.0 collective-permute-done.6.refs_0_
  31.9 0.0 collective-permute-done.7.refs_1_
  31.9 0.2 collective-permute-done.8.refs_2_
  32.1 0.3 shard_map.125
  32.5 3.5 %collective-permute-start.10 = (bf16[32,2048]{1,0:T(8,128)(2,1)S(1)}, bf16[32,2048]{1,0:T(8,128)(2,1)S(1)}, u32[]{:S(2)}, u32[]{:S(2)}) collective-permute-start(bf16[32,2048]{1,0:T(8,128)(2,1)S(1)} %get-tuple-element.63), channel_id=1, source_target_pairs={{0,24},{8,16},{16,8},{24,0},{1,25},{9,17},{17,9},{25,1},{2,26},{10... | collective-permute-start | bytes 393224 | tf_op jit(solution)/shard_map/ppermute | solution.py:415
  36.0 0.0 collective-permute-start.11
  36.0 0.6 %collective-permute-start.9 = (bf16[32,2048]{1,0:T(8,128)(2,1)S(1)}, bf16[32,2048]{1,0:T(8,128)(2,1)S(1)}, u32[]{:S(2)}, u32[]{:S(2)}) collective-permute-start(bf16[32,2048]{1,0:T(8,128)(2,1)S(1)} %get-tuple-element.62), channel_id=1, source_target_pairs={{0,8},{8,0},{16,24},{24,16},{1,9},{9,1},{17,25},{25,17},{2,10},{10... | collective-permute-start | bytes 393224 | tf_op jit(solution)/shard_map/ppermute | solution.py:415
  36.6 2.3 %collective-permute-done.10.refs_0_ = bf16[32,2048]{1,0:T(8,128)(2,1)S(1)} collective-permute-done((bf16[32,2048]{1,0:T(8,128)(2,1)S(1)}, bf16[32,2048]{1,0:T(8,128)(2,1)S(1)}, u32[]{:S(2)}, u32[]{:S(2)}) %collective-permute-start.10) | collective-permute-done | bytes 131104 | tf_op jit(solution)/shard_map/ppermute | solution.py:415
  38.9 2.0 %collective-permute-done.11.refs_1_ = bf16[32,2048]{1,0:T(8,128)(2,1)S(1)} collective-permute-done((bf16[32,2048]{1,0:T(8,128)(2,1)S(1)}, bf16[32,2048]{1,0:T(8,128)(2,1)S(1)}, u32[]{:S(2)}, u32[]{:S(2)}) %collective-permute-start.11) | collective-permute-done | bytes 131104 | tf_op jit(solution)/shard_map/ppermute | solution.py:415
  40.9 0.2 shard_map.126._
  41.1 0.0 collective-permute-done.9.piece
  41.1 1.2 %shard_map.127 = (bf16[32,64,128]{2,1,0:T(8,128)(2,1)}, f32[4,512,128]{2,1,0:T(8,128)S(1)}) custom-call(bf16[32,2048]{1,0:T(8,128)(2,1)S(1)} %collective-permute-done.9.piece, f32[4,512,128]{2,1,0:T(8,128)S(1)} %shard_map.126._), custom_call_target="tpu_custom_call", output_to_operand_aliasing={{1}: (1, {})} | custom-call | flops 16777216 | bytes 1048576 | tf_op jit(solution)/shard_map/pallas_call | solution.py:43
Async XLA Ops:
  0.0 12.2 %copy-start.4 = (s32[128,4]{0,1:T(4,128)S(1)}, s32[128,4]{0,1:T(4,128)}, u32[]{:S(2)}) copy-start(s32[128,4]{0,1:T(4,128)} %param.19) | copy-start | bytes 6148
  1.3 6.8 %collective-permute-start = (bf16[144,128]{1,0:T(8,128)(2,1)S(1)}, bf16[144,128]{1,0:T(8,128)(2,1)S(1)}, u32[]{:S(2)}, u32[]{:S(2)}) collective-permute-start(bf16[144,128]{1,0:T(8,128)(2,1)S(1)} %get-tuple-element.39.own), channel_id=1, source_target_pairs={{0,1},{1,2},{2,3},{3,4},{4,5},{5,6},{6,7},{7,0},{8,9},{9,10},{10,1... | collective-permute-start | bytes 110600 | tf_op jit(solution)/shard_map/ppermute | solution.py:397
  2.2 5.9 %collective-permute-start.1 = (bf16[144,128]{1,0:T(8,128)(2,1)S(1)}, bf16[144,128]{1,0:T(8,128)(2,1)S(1)}, u32[]{:S(2)}, u32[]{:S(2)}) collective-permute-start(bf16[144,128]{1,0:T(8,128)(2,1)S(1)} %get-tuple-element.39.own), channel_id=1, source_target_pairs={{0,7},{1,0},{2,1},{3,2},{4,3},{5,4},{6,5},{7,6},{8,15},{9,8},{10,9... | collective-permute-start | bytes 110600 | tf_op jit(solution)/shard_map/ppermute | solution.py:397
  8.5 10.8 %copy-start = (bf16[64,256]{1,0:T(8,128)(2,1)S(1)}, bf16[64,256]{1,0:T(8,128)(2,1)}, u32[]{:S(2)}) copy-start(bf16[64,256]{1,0:T(8,128)(2,1)} %refs_2_.1) | copy-start | bytes 98308
  8.6 10.8 %copy-start.1 = (bf16[1,256,256]{2,1,0:T(8,128)(2,1)S(1)}, bf16[1,256,256]{2,1,0:T(8,128)(2,1)}, u32[]{:S(2)}) copy-start(bf16[1,256,256]{2,1,0:T(8,128)(2,1)} %send.3) | copy-start | bytes 393220
  8.6 10.8 %copy-start.2 = (bf16[1,256,256]{2,1,0:T(8,128)(2,1)S(1)}, bf16[1,256,256]{2,1,0:T(8,128)(2,1)}, u32[]{:S(2)}) copy-start(bf16[1,256,256]{2,1,0:T(8,128)(2,1)} %refs_3_.1) | copy-start | bytes 393220
  8.6 10.7 %copy-start.3 = (bf16[256,64]{0,1:T(8,128)(2,1)S(1)}, bf16[256,64]{0,1:T(8,128)(2,1)}, u32[]{:S(2)}) copy-start(bf16[256,64]{0,1:T(8,128)(2,1)} %param.18) | copy-start | bytes 98308
  8.6 10.7 %copy-start.5 = (bf16[1,256]{1,0:T(2,128)(2,1)S(1)}, bf16[1,256]{1,0:T(2,128)(2,1)}, u32[]{:S(2)}) copy-start(bf16[1,256]{1,0:T(2,128)(2,1)} %refs_4_.1) | copy-start | bytes 1540
  8.6 10.7 %collective-permute-start.4 = (bf16[656,128]{1,0:T(8,128)(2,1)S(1)}, bf16[656,128]{1,0:T(8,128)(2,1)S(1)}, u32[]{:S(2)}, u32[]{:S(2)}) collective-permute-start(bf16[656,128]{1,0:T(8,128)(2,1)S(1)} %get-tuple-element.52), channel_id=1, source_target_pairs={{0,1},{1,2},{2,3},{3,4},{4,5},{5,6},{6,7},{7,0},{8,9},{9,10},{10,1... | collective-permute-start | bytes 503816 | tf_op jit(solution)/shard_map/ppermute | solution.py:397
  8.9 10.4 %collective-permute-start.5 = (bf16[656,128]{1,0:T(8,128)(2,1)S(1)}, bf16[656,128]{1,0:T(8,128)(2,1)S(1)}, u32[]{:S(2)}, u32[]{:S(2)}) collective-permute-start(bf16[656,128]{1,0:T(8,128)(2,1)S(1)} %get-tuple-element.53), channel_id=1, source_target_pairs={{0,7},{1,0},{2,1},{3,2},{4,3},{5,4},{6,5},{7,6},{8,15},{9,8},{10,9... | collective-permute-start | bytes 503816 | tf_op jit(solution)/shard_map/ppermute | solution.py:397
  16.2 11.6 %collective-permute-start.3 = (bf16[432,128]{1,0:T(8,128)(2,1)S(1)}, bf16[432,128]{1,0:T(8,128)(2,1)S(1)}, u32[]{:S(2)}, u32[]{:S(2)}) collective-permute-start(bf16[432,128]{1,0:T(8,128)(2,1)S(1)} %get-tuple-element.51), channel_id=1, source_target_pairs={{0,8},{8,16},{16,24},{24,0},{1,9},{9,17},{17,25},{25,1},{2,10},{10... | collective-permute-start | bytes 331784 | tf_op jit(solution)/shard_map/ppermute | solution.py:397
  18.3 9.6 %collective-permute-start.2 = (bf16[432,128]{1,0:T(8,128)(2,1)S(1)}, bf16[432,128]{1,0:T(8,128)(2,1)S(1)}, u32[]{:S(2)}, u32[]{:S(2)}) collective-permute-start(bf16[432,128]{1,0:T(8,128)(2,1)S(1)} %get-tuple-element.51), channel_id=1, source_target_pairs={{0,24},{8,0},{16,8},{24,16},{1,25},{9,1},{17,9},{25,17},{2,26},{10... | collective-permute-start | bytes 331784 | tf_op jit(solution)/shard_map/ppermute | solution.py:397
  19.3 8.5 %copy-start.6 = (s32[1,8]{1,0:T(1,128)S(1)}, s32[1,8]{1,0:T(1,128)}, u32[]{:S(2)}) copy-start(s32[1,8]{1,0:T(1,128)} %neighbours.1) | copy-start | bytes 100
  24.3 7.7 %collective-permute-start.6 = (bf16[32,2048]{1,0:T(8,128)(2,1)S(1)}, bf16[32,2048]{1,0:T(8,128)(2,1)S(1)}, u32[]{:S(2)}, u32[]{:S(2)}) collective-permute-start(bf16[32,2048]{1,0:T(8,128)(2,1)S(1)} %get-tuple-element.58), channel_id=1, source_target_pairs={{0,24},{8,16},{16,8},{24,0},{1,25},{9,17},{17,9},{25,1},{2,26},{10... | collective-permute-start | bytes 393224 | tf_op jit(solution)/shard_map/ppermute | solution.py:415
  26.3 5.6 %collective-permute-start.7 = (bf16[32,2048]{1,0:T(8,128)(2,1)S(1)}, bf16[32,2048]{1,0:T(8,128)(2,1)S(1)}, u32[]{:S(2)}, u32[]{:S(2)}) collective-permute-start(bf16[32,2048]{1,0:T(8,128)(2,1)S(1)} %get-tuple-element.59), channel_id=1, source_target_pairs={{0,16},{8,24},{16,0},{24,8},{1,17},{9,25},{17,1},{25,9},{2,18},{10... | collective-permute-start | bytes 393224 | tf_op jit(solution)/shard_map/ppermute | solution.py:415
  26.8 5.3 %collective-permute-start.8 = (bf16[32,2048]{1,0:T(8,128)(2,1)S(1)}, bf16[32,2048]{1,0:T(8,128)(2,1)S(1)}, u32[]{:S(2)}, u32[]{:S(2)}) collective-permute-start(bf16[32,2048]{1,0:T(8,128)(2,1)S(1)} %get-tuple-element.60), channel_id=1, source_target_pairs={{0,8},{8,0},{16,24},{24,16},{1,9},{9,1},{17,25},{25,17},{2,10},{10... | collective-permute-start | bytes 393224 | tf_op jit(solution)/shard_map/ppermute | solution.py:415
  32.5 6.5 %collective-permute-start.10 = (bf16[32,2048]{1,0:T(8,128)(2,1)S(1)}, bf16[32,2048]{1,0:T(8,128)(2,1)S(1)}, u32[]{:S(2)}, u32[]{:S(2)}) collective-permute-start(bf16[32,2048]{1,0:T(8,128)(2,1)S(1)} %get-tuple-element.63), channel_id=1, source_target_pairs={{0,24},{8,16},{16,8},{24,0},{1,25},{9,17},{17,9},{25,1},{2,26},{10... | collective-permute-start | bytes 393224 | tf_op jit(solution)/shard_map/ppermute | solution.py:415
  36.0 5.0 %collective-permute-start.11 = (bf16[32,2048]{1,0:T(8,128)(2,1)S(1)}, bf16[32,2048]{1,0:T(8,128)(2,1)S(1)}, u32[]{:S(2)}, u32[]{:S(2)}) collective-permute-start(bf16[32,2048]{1,0:T(8,128)(2,1)S(1)} %get-tuple-element.64), channel_id=1, source_target_pairs={{0,16},{8,24},{16,0},{24,8},{1,17},{9,25},{17,1},{25,9},{2,18},{10... | collective-permute-start | bytes 393224 | tf_op jit(solution)/shard_map/ppermute | solution.py:415
  36.0 5.2 %collective-permute-start.9 = (bf16[32,2048]{1,0:T(8,128)(2,1)S(1)}, bf16[32,2048]{1,0:T(8,128)(2,1)S(1)}, u32[]{:S(2)}, u32[]{:S(2)}) collective-permute-start(bf16[32,2048]{1,0:T(8,128)(2,1)S(1)} %get-tuple-element.62), channel_id=1, source_target_pairs={{0,8},{8,0},{16,24},{24,16},{1,9},{9,1},{17,25},{25,17},{2,10},{10... | collective-permute-start | bytes 393224 | tf_op jit(solution)/shard_map/ppermute | solution.py:415

commit v6 on v5

--- a/solution.py
+++ b/solution.py
@@ -198,8 +198,8 @@
     rearranged,
     received,
     started,
+    from_after,
     from_before,
-    from_after,
     encode,
     send,
     update,
@@ -279,7 +279,7 @@
             out[:, pair * width : (pair + 1) * width] = forecast[index * pairs + pair]
 
 
-def weights_kernel(neighbours, own, before, after, down, up, from_before, from_after, *refs):
+def weights_kernel(neighbours, own, before, after, down, up, from_after, from_before, *refs):
     *forecast, out, piece = refs
     forecast_kernel([0], *forecast, piece)
     rows, ensemble = own.shape
@@ -480,8 +480,8 @@
         scratch=[pltpu.VMEM((2 * size, 2 * channels), F32)],
         flops=1 << 27,
     )
+    from_after = ring(to_before, "space", -1)
     from_before = ring(to_after, "space", 1)
-    from_after = ring(to_before, "space", -1)
     edges = edge_senders.T
     started, halo_edges = call(
         functools.partial(own_message_kernel, 2 * halo_count),
@@ -507,8 +507,8 @@
             halo_edges,
             rearranged,
             *placed_in(pltpu.VMEM, received, started),
+            from_after,
             from_before,
-            from_after,
             encode_weight,
             send_weight,
             update_weight,
@@ -535,8 +535,8 @@
             after,
             down,
             up,
+            from_after,
             from_before,
-            from_after,
             *placed_in(pltpu.VMEM, messages),
             *shared,
         ),

time: 42.6 us -> 41.5 us (0.974)
  starting transfers between devices: 19 us -> 18.2 us
    ppermute x6, starting transfers between devices: 7.7 us -> 7.11 us  [exchange(): lax.ppermute(piece, axis, [(i, i ^ step if paired_up else (i + step) % co...]
  transfers between devices with their start and end apart: 12 -> 12, of which waited for: 3 -> 4; matrix products, arithmetic and copies ran while one was open for 0% -> 0% of each run, Pallas kernels for 36% -> 37%
where the time goes in v6:
time: 41.5 us; the launch traced here: 41.3 us
  Pallas kernels  18.6 us (45%)
  starting transfers between devices  18.2 us (44%)
  waiting for transfers between devices  4.25 us (10%)
    pallas_call x10, Pallas kernels, call(): pl.pallas_call(kernel, out_shape=shapes, in_specs=specs or [VMEM] * len(i...  18.6 us
    ppermute x6, starting transfers between devices, ring(): lax.ppermute(value, axis, [(i, (i + shift) % count) for i in range(count)])  11.1 us
    ppermute x6, starting transfers between devices, exchange(): lax.ppermute(piece, axis, [(i, i ^ step if paired_up else (i + step) % co...  7.11 us
    ppermute x6, waiting for transfers between devices, exchange(): lax.ppermute(piece, axis, [(i, i ^ step if paired_up else (i + step) % co...  4.23 us
  transfers between devices with their start and end apart: 12, of which 4 were waited for; matrix products, arithmetic and copies ran while one was open for 0% of the time, Pallas kernels for 37%

profile of v6, /device:TPU:0, one launch (start us, length us, event | category | flops | bytes accessed | tf_op | source)
XLA Modules:
  0.0 41.3 jit_solution(15620972751658022349)
XLA Ops:
  0.0 0.0 copy-start.4
  0.0 1.3 %shard_map.118 = (bf16[144,128]{1,0:T(8,128)(2,1)S(1)}, bf16[32,64,128]{2,1,0:T(8,128)(2,1)S(1)}, bf16[64,256]{1,0:T(8,128)(2,1)S(1)}, bf16[1,256,256]{2,1,0:T(8,128)(2,1)S(1)}, bf16[1,256,256]{2,1,0:T(8,128)(2,1)S(1)}) custom-call(bf16[1,128,256]{2,1,0:T(8,128)(2,1)} %perturbation.1, bf16[1,2,256]{2,1,0:T(2,128)(2,1)} %values.1, s32[2,32]{1,0:T(2,128)} %halo_nodes.1, ...), custom_call_target="tpu_custom_call" | custom-call | flops 16777216 | bytes 1048576 | tf_op jit(solution)/shard_map/pallas_call | solution.py:43
  1.3 0.5 %collective-permute-start = (bf16[144,128]{1,0:T(8,128)(2,1)S(1)}, bf16[144,128]{1,0:T(8,128)(2,1)S(1)}, u32[]{:S(2)}, u32[]{:S(2)}) collective-permute-start(bf16[144,128]{1,0:T(8,128)(2,1)S(1)} %get-tuple-element.39.own), channel_id=1, source_target_pairs={{0,1},{1,2},{2,3},{3,4},{4,5},{5,6},{6,7},{7,0},{8,9},{9,10},{10,1... | collective-permute-start | bytes 110600 | tf_op jit(solution)/shard_map/ppermute | solution.py:397
  1.8 0.4 shard_map.119
  2.2 4.1 %collective-permute-start.1 = (bf16[144,128]{1,0:T(8,128)(2,1)S(1)}, bf16[144,128]{1,0:T(8,128)(2,1)S(1)}, u32[]{:S(2)}, u32[]{:S(2)}) collective-permute-start(bf16[144,128]{1,0:T(8,128)(2,1)S(1)} %get-tuple-element.39.own), channel_id=1, source_target_pairs={{0,7},{1,0},{2,1},{3,2},{4,3},{5,4},{6,5},{7,6},{8,15},{9,8},{10,9... | collective-permute-start | bytes 110600 | tf_op jit(solution)/shard_map/ppermute | solution.py:397
  6.3 1.8 %shard_map.120 = (f32[129,32,256]{2,1,0:T(8,128)S(1)}, f32[128,32,256]{2,1,0:T(8,128)S(1)}) custom-call(bf16[2048,128]{1,0:T(8,128)(2,1)S(1)} %get-tuple-element.40.rearranged.refs_1_, bf16[64,256]{1,0:T(8,128)(2,1)S(1)} %get-tuple-element.41.encode, bf16[1,256,256]{2,1,0:T(8,128)(2,1)S(1)} %get-tuple-element.42.send, ...), custom_call_target="tpu_custom_call" | custom-call | flops 1073741824 | bytes 1048576 | tf_op jit(solution)/shard_map/pallas_call | solution.py:43
  8.1 0.0 collective-permute-done.before
  8.1 0.0 collective-permute-done.1.after
  8.1 0.4 %shard_map.121 = (bf16[656,128]{1,0:T(8,128)(2,1)S(1)}, bf16[656,128]{1,0:T(8,128)(2,1)S(1)}, bf16[432,128]{1,0:T(8,128)(2,1)S(1)}) custom-call(bf16[16,128,128]{2,1,0:T(8,128)(2,1)S(1)} %get-tuple-element.46.columns, bf16[144,128]{1,0:T(8,128)(2,1)S(1)} %get-tuple-element.39.own, bf16[144,128]{1,0:T(8,128)(2,1)S(1)} %collective-permute-done.before, ...), custom_call_target="tpu_custom_call" | custom-call | flops 134217728 | bytes 1048576 | tf_op jit(solution)/shard_map/pallas_call | solution.py:43
  8.5 0.0 copy-start
  8.6 0.0 copy-start.1
  8.6 0.0 copy-start.2
  8.6 0.0 copy-start.3
  8.6 0.0 copy-start.5
  8.6 3.4 %collective-permute-start.4 = (bf16[656,128]{1,0:T(8,128)(2,1)S(1)}, bf16[656,128]{1,0:T(8,128)(2,1)S(1)}, u32[]{:S(2)}, u32[]{:S(2)}) collective-permute-start(bf16[656,128]{1,0:T(8,128)(2,1)S(1)} %get-tuple-element.52), channel_id=1, source_target_pairs={{0,7},{1,0},{2,1},{3,2},{4,3},{5,4},{6,5},{7,6},{8,15},{9,8},{10,9... | collective-permute-start | bytes 503816 | tf_op jit(solution)/shard_map/ppermute | solution.py:397
  12.0 0.0 collective-permute-start.5
  12.0 0.0 copy-done.4
  12.0 4.0 %shard_map.122 = (f32[129,32,256]{2,1,0:T(8,128)S(1)}, s32[529]{0:T(1024)S(1)}) custom-call(s32[4,128]{1,0:T(4,128)S(1)} %bitcast.4, f32[129,32,256]{2,1,0:T(8,128)S(1)} %get-tuple-element.48.sent, f32[128,32,256]{2,1,0:T(8,128)S(1)} %get-tuple-element.49.received), custom_call_target="tpu_custom_call" | custom-call | flops 2147483648 | bytes 1048576 | tf_op jit(solution)/shard_map/pallas_call | solution.py:43
  16.1 2.0 %collective-permute-start.3 = (bf16[432,128]{1,0:T(8,128)(2,1)S(1)}, bf16[432,128]{1,0:T(8,128)(2,1)S(1)}, u32[]{:S(2)}, u32[]{:S(2)}) collective-permute-start(bf16[432,128]{1,0:T(8,128)(2,1)S(1)} %get-tuple-element.51), channel_id=1, source_target_pairs={{0,8},{8,16},{16,24},{24,0},{1,9},{9,17},{17,25},{25,1},{2,10},{10... | collective-permute-start | bytes 331784 | tf_op jit(solution)/shard_map/ppermute | solution.py:397
  18.1 1.0 %collective-permute-start.2 = (bf16[432,128]{1,0:T(8,128)(2,1)S(1)}, bf16[432,128]{1,0:T(8,128)(2,1)S(1)}, u32[]{:S(2)}, u32[]{:S(2)}) collective-permute-start(bf16[432,128]{1,0:T(8,128)(2,1)S(1)} %get-tuple-element.51), channel_id=1, source_target_pairs={{0,24},{8,0},{16,8},{24,16},{1,25},{9,1},{17,9},{25,17},{2,26},{10... | collective-permute-start | bytes 331784 | tf_op jit(solution)/shard_map/ppermute | solution.py:397
  19.1 0.0 collective-permute-done.4.from_after
  19.1 0.0 collective-permute-done.5.from_before
  19.1 0.0 copy-done
  19.1 0.0 copy-done.1
  19.1 0.0 copy-done.2
  19.2 0.0 copy-done.3
  19.2 0.0 copy-done.5
  19.2 0.0 copy-start.6
  19.2 4.9 %shard_map.123 = (bf16[32,2048]{1,0:T(8,128)(2,1)S(1)}, bf16[32,2048]{1,0:T(8,128)(2,1)S(1)}, bf16[32,2048]{1,0:T(8,128)(2,1)S(1)}, f32[129,32,256]{2,1,0:T(8,128)S(1)}) custom-call(s32[529]{0:T(1024)S(1)} %get-tuple-element.54.halo_edges_far, bf16[2048,128]{1,0:T(8,128)(2,1)S(1)} %get-tuple-element.40.rearranged.refs_1_, ...), custom_call_target="tpu_custom_call", output_to_operand_aliasing={{3}: (3, {})} | custom-call | flops 4294967296 | bytes 1048576 | tf_op jit(solution)/shard_map/pallas_call | solution.py:43
  24.1 2.5 %collective-permute-start.6 = (bf16[32,2048]{1,0:T(8,128)(2,1)S(1)}, bf16[32,2048]{1,0:T(8,128)(2,1)S(1)}, u32[]{:S(2)}, u32[]{:S(2)}) collective-permute-start(bf16[32,2048]{1,0:T(8,128)(2,1)S(1)} %get-tuple-element.58), channel_id=1, source_target_pairs={{0,24},{8,16},{16,8},{24,0},{1,25},{9,17},{17,9},{25,1},{2,26},{10... | collective-permute-start | bytes 393224 | tf_op jit(solution)/shard_map/ppermute | solution.py:415
  26.6 0.5 %collective-permute-start.7 = (bf16[32,2048]{1,0:T(8,128)(2,1)S(1)}, bf16[32,2048]{1,0:T(8,128)(2,1)S(1)}, u32[]{:S(2)}, u32[]{:S(2)}) collective-permute-start(bf16[32,2048]{1,0:T(8,128)(2,1)S(1)} %get-tuple-element.59), channel_id=1, source_target_pairs={{0,16},{8,24},{16,0},{24,8},{1,17},{9,25},{17,1},{25,9},{2,18},{10... | collective-permute-start | bytes 393224 | tf_op jit(solution)/shard_map/ppermute | solution.py:415
  27.1 0.6 %collective-permute-start.8 = (bf16[32,2048]{1,0:T(8,128)(2,1)S(1)}, bf16[32,2048]{1,0:T(8,128)(2,1)S(1)}, u32[]{:S(2)}, u32[]{:S(2)}) collective-permute-start(bf16[32,2048]{1,0:T(8,128)(2,1)S(1)} %get-tuple-element.60), channel_id=1, source_target_pairs={{0,8},{8,0},{16,24},{24,16},{1,9},{9,1},{17,25},{25,17},{2,10},{10... | collective-permute-start | bytes 393224 | tf_op jit(solution)/shard_map/ppermute | solution.py:415
  27.7 0.0 collective-permute-done.3.up
  27.7 0.0 collective-permute-done.2.down
  27.7 0.0 copy-done.6
  27.7 4.1 %shard_map.124 = (bf16[128,256]{1,0:T(8,128)(2,1)S(1)}, bf16[32,2048]{1,0:T(8,128)(2,1)S(1)}) custom-call(s32[1,8]{1,0:T(1,128)S(1)} %copy-done.6, bf16[144,128]{1,0:T(8,128)(2,1)S(1)} %get-tuple-element.39.own, bf16[144,128]{1,0:T(8,128)(2,1)S(1)} %collective-permute-done.before, bf16[144,128]{1,0:T(8,128)(2,1)S(1)} %collective-permute-done.1.after, ...), custom_call_target="tpu_custom_call" | custom-call | flops 1073741824 | bytes 1048576 | tf_op jit(solution)/shard_map/pallas_call | solution.py:43
  31.8 0.0 collective-permute-done.6.refs_0_
  31.8 0.0 collective-permute-done.7.refs_1_
  31.8 0.3 collective-permute-done.8.refs_2_
  32.1 0.3 shard_map.125
  32.4 2.5 %collective-permute-start.10 = (bf16[32,2048]{1,0:T(8,128)(2,1)S(1)}, bf16[32,2048]{1,0:T(8,128)(2,1)S(1)}, u32[]{:S(2)}, u32[]{:S(2)}) collective-permute-start(bf16[32,2048]{1,0:T(8,128)(2,1)S(1)} %get-tuple-element.63), channel_id=1, source_target_pairs={{0,24},{8,16},{16,8},{24,0},{1,25},{9,17},{17,9},{25,1},{2,26},{10... | collective-permute-start | bytes 393224 | tf_op jit(solution)/shard_map/ppermute | solution.py:415
  34.8 0.3 collective-permute-start.11
  35.1 0.8 %collective-permute-start.9 = (bf16[32,2048]{1,0:T(8,128)(2,1)S(1)}, bf16[32,2048]{1,0:T(8,128)(2,1)S(1)}, u32[]{:S(2)}, u32[]{:S(2)}) collective-permute-start(bf16[32,2048]{1,0:T(8,128)(2,1)S(1)} %get-tuple-element.62), channel_id=1, source_target_pairs={{0,8},{8,0},{16,24},{24,16},{1,9},{9,1},{17,25},{25,17},{2,10},{10... | collective-permute-start | bytes 393224 | tf_op jit(solution)/shard_map/ppermute | solution.py:415
  35.9 2.4 %collective-permute-done.10.refs_0_ = bf16[32,2048]{1,0:T(8,128)(2,1)S(1)} collective-permute-done((bf16[32,2048]{1,0:T(8,128)(2,1)S(1)}, bf16[32,2048]{1,0:T(8,128)(2,1)S(1)}, u32[]{:S(2)}, u32[]{:S(2)}) %collective-permute-start.10) | collective-permute-done | bytes 131104 | tf_op jit(solution)/shard_map/ppermute | solution.py:415
  38.3 1.5 %collective-permute-done.11.refs_1_ = bf16[32,2048]{1,0:T(8,128)(2,1)S(1)} collective-permute-done((bf16[32,2048]{1,0:T(8,128)(2,1)S(1)}, bf16[32,2048]{1,0:T(8,128)(2,1)S(1)}, u32[]{:S(2)}, u32[]{:S(2)}) %collective-permute-start.11) | collective-permute-done | bytes 131104 | tf_op jit(solution)/shard_map/ppermute | solution.py:415
  39.8 0.2 shard_map.126._
  40.0 0.1 collective-permute-done.9.piece
  40.1 1.2 %shard_map.127 = (bf16[32,64,128]{2,1,0:T(8,128)(2,1)}, f32[4,512,128]{2,1,0:T(8,128)S(1)}) custom-call(bf16[32,2048]{1,0:T(8,128)(2,1)S(1)} %collective-permute-done.9.piece, f32[4,512,128]{2,1,0:T(8,128)S(1)} %shard_map.126._), custom_call_target="tpu_custom_call", output_to_operand_aliasing={{1}: (1, {})} | custom-call | flops 16777216 | bytes 1048576 | tf_op jit(solution)/shard_map/pallas_call | solution.py:43
Async XLA Ops:
  0.0 12.0 %copy-start.4 = (s32[128,4]{0,1:T(4,128)S(1)}, s32[128,4]{0,1:T(4,128)}, u32[]{:S(2)}) copy-start(s32[128,4]{0,1:T(4,128)} %param.19) | copy-start | bytes 6148
  1.3 6.8 %collective-permute-start = (bf16[144,128]{1,0:T(8,128)(2,1)S(1)}, bf16[144,128]{1,0:T(8,128)(2,1)S(1)}, u32[]{:S(2)}, u32[]{:S(2)}) collective-permute-start(bf16[144,128]{1,0:T(8,128)(2,1)S(1)} %get-tuple-element.39.own), channel_id=1, source_target_pairs={{0,1},{1,2},{2,3},{3,4},{4,5},{5,6},{6,7},{7,0},{8,9},{9,10},{10,1... | collective-permute-start | bytes 110600 | tf_op jit(solution)/shard_map/ppermute | solution.py:397
  2.2 5.9 %collective-permute-start.1 = (bf16[144,128]{1,0:T(8,128)(2,1)S(1)}, bf16[144,128]{1,0:T(8,128)(2,1)S(1)}, u32[]{:S(2)}, u32[]{:S(2)}) collective-permute-start(bf16[144,128]{1,0:T(8,128)(2,1)S(1)} %get-tuple-element.39.own), channel_id=1, source_target_pairs={{0,7},{1,0},{2,1},{3,2},{4,3},{5,4},{6,5},{7,6},{8,15},{9,8},{10,9... | collective-permute-start | bytes 110600 | tf_op jit(solution)/shard_map/ppermute | solution.py:397
  8.5 10.6 %copy-start = (bf16[64,256]{1,0:T(8,128)(2,1)S(1)}, bf16[64,256]{1,0:T(8,128)(2,1)}, u32[]{:S(2)}) copy-start(bf16[64,256]{1,0:T(8,128)(2,1)} %refs_2_.1) | copy-start | bytes 98308
  8.6 10.6 %copy-start.1 = (bf16[1,256,256]{2,1,0:T(8,128)(2,1)S(1)}, bf16[1,256,256]{2,1,0:T(8,128)(2,1)}, u32[]{:S(2)}) copy-start(bf16[1,256,256]{2,1,0:T(8,128)(2,1)} %send.3) | copy-start | bytes 393220
  8.6 10.6 %copy-start.2 = (bf16[1,256,256]{2,1,0:T(8,128)(2,1)S(1)}, bf16[1,256,256]{2,1,0:T(8,128)(2,1)}, u32[]{:S(2)}) copy-start(bf16[1,256,256]{2,1,0:T(8,128)(2,1)} %refs_3_.1) | copy-start | bytes 393220
  8.6 10.6 %copy-start.3 = (bf16[256,64]{0,1:T(8,128)(2,1)S(1)}, bf16[256,64]{0,1:T(8,128)(2,1)}, u32[]{:S(2)}) copy-start(bf16[256,64]{0,1:T(8,128)(2,1)} %param.18) | copy-start | bytes 98308
  8.6 10.6 %copy-start.5 = (bf16[1,256]{1,0:T(2,128)(2,1)S(1)}, bf16[1,256]{1,0:T(2,128)(2,1)}, u32[]{:S(2)}) copy-start(bf16[1,256]{1,0:T(2,128)(2,1)} %refs_4_.1) | copy-start | bytes 1540
  8.6 10.5 %collective-permute-start.4 = (bf16[656,128]{1,0:T(8,128)(2,1)S(1)}, bf16[656,128]{1,0:T(8,128)(2,1)S(1)}, u32[]{:S(2)}, u32[]{:S(2)}) collective-permute-start(bf16[656,128]{1,0:T(8,128)(2,1)S(1)} %get-tuple-element.52), channel_id=1, source_target_pairs={{0,7},{1,0},{2,1},{3,2},{4,3},{5,4},{6,5},{7,6},{8,15},{9,8},{10,9... | collective-permute-start | bytes 503816 | tf_op jit(solution)/shard_map/ppermute | solution.py:397
  12.0 7.1 %collective-permute-start.5 = (bf16[656,128]{1,0:T(8,128)(2,1)S(1)}, bf16[656,128]{1,0:T(8,128)(2,1)S(1)}, u32[]{:S(2)}, u32[]{:S(2)}) collective-permute-start(bf16[656,128]{1,0:T(8,128)(2,1)S(1)} %get-tuple-element.53), channel_id=1, source_target_pairs={{0,1},{1,2},{2,3},{3,4},{4,5},{5,6},{6,7},{7,0},{8,9},{9,10},{10,1... | collective-permute-start | bytes 503816 | tf_op jit(solution)/shard_map/ppermute | solution.py:397
  16.1 11.6 %collective-permute-start.3 = (bf16[432,128]{1,0:T(8,128)(2,1)S(1)}, bf16[432,128]{1,0:T(8,128)(2,1)S(1)}, u32[]{:S(2)}, u32[]{:S(2)}) collective-permute-start(bf16[432,128]{1,0:T(8,128)(2,1)S(1)} %get-tuple-element.51), channel_id=1, source_target_pairs={{0,8},{8,16},{16,24},{24,0},{1,9},{9,17},{17,25},{25,1},{2,10},{10... | collective-permute-start | bytes 331784 | tf_op jit(solution)/shard_map/ppermute | solution.py:397
  18.1 9.6 %collective-permute-start.2 = (bf16[432,128]{1,0:T(8,128)(2,1)S(1)}, bf16[432,128]{1,0:T(8,128)(2,1)S(1)}, u32[]{:S(2)}, u32[]{:S(2)}) collective-permute-start(bf16[432,128]{1,0:T(8,128)(2,1)S(1)} %get-tuple-element.51), channel_id=1, source_target_pairs={{0,24},{8,0},{16,8},{24,16},{1,25},{9,1},{17,9},{25,17},{2,26},{10... | collective-permute-start | bytes 331784 | tf_op jit(solution)/shard_map/ppermute | solution.py:397
  19.2 8.5 %copy-start.6 = (s32[1,8]{1,0:T(1,128)S(1)}, s32[1,8]{1,0:T(1,128)}, u32[]{:S(2)}) copy-start(s32[1,8]{1,0:T(1,128)} %neighbours.1) | copy-start | bytes 100
  24.1 7.7 %collective-permute-start.6 = (bf16[32,2048]{1,0:T(8,128)(2,1)S(1)}, bf16[32,2048]{1,0:T(8,128)(2,1)S(1)}, u32[]{:S(2)}, u32[]{:S(2)}) collective-permute-start(bf16[32,2048]{1,0:T(8,128)(2,1)S(1)} %get-tuple-element.58), channel_id=1, source_target_pairs={{0,24},{8,16},{16,8},{24,0},{1,25},{9,17},{17,9},{25,1},{2,26},{10... | collective-permute-start | bytes 393224 | tf_op jit(solution)/shard_map/ppermute | solution.py:415
  26.6 5.2 %collective-permute-start.7 = (bf16[32,2048]{1,0:T(8,128)(2,1)S(1)}, bf16[32,2048]{1,0:T(8,128)(2,1)S(1)}, u32[]{:S(2)}, u32[]{:S(2)}) collective-permute-start(bf16[32,2048]{1,0:T(8,128)(2,1)S(1)} %get-tuple-element.59), channel_id=1, source_target_pairs={{0,16},{8,24},{16,0},{24,8},{1,17},{9,25},{17,1},{25,9},{2,18},{10... | collective-permute-start | bytes 393224 | tf_op jit(solution)/shard_map/ppermute | solution.py:415
  27.1 5.0 %collective-permute-start.8 = (bf16[32,2048]{1,0:T(8,128)(2,1)S(1)}, bf16[32,2048]{1,0:T(8,128)(2,1)S(1)}, u32[]{:S(2)}, u32[]{:S(2)}) collective-permute-start(bf16[32,2048]{1,0:T(8,128)(2,1)S(1)} %get-tuple-element.60), channel_id=1, source_target_pairs={{0,8},{8,0},{16,24},{24,16},{1,9},{9,1},{17,25},{25,17},{2,10},{10... | collective-permute-start | bytes 393224 | tf_op jit(solution)/shard_map/ppermute | solution.py:415
  32.4 5.9 %collective-permute-start.10 = (bf16[32,2048]{1,0:T(8,128)(2,1)S(1)}, bf16[32,2048]{1,0:T(8,128)(2,1)S(1)}, u32[]{:S(2)}, u32[]{:S(2)}) collective-permute-start(bf16[32,2048]{1,0:T(8,128)(2,1)S(1)} %get-tuple-element.63), channel_id=1, source_target_pairs={{0,24},{8,16},{16,8},{24,0},{1,25},{9,17},{17,9},{25,1},{2,26},{10... | collective-permute-start | bytes 393224 | tf_op jit(solution)/shard_map/ppermute | solution.py:415
  34.8 5.0 %collective-permute-start.11 = (bf16[32,2048]{1,0:T(8,128)(2,1)S(1)}, bf16[32,2048]{1,0:T(8,128)(2,1)S(1)}, u32[]{:S(2)}, u32[]{:S(2)}) collective-permute-start(bf16[32,2048]{1,0:T(8,128)(2,1)S(1)} %get-tuple-element.64), channel_id=1, source_target_pairs={{0,16},{8,24},{16,0},{24,8},{1,17},{9,25},{17,1},{25,9},{2,18},{10... | collective-permute-start | bytes 393224 | tf_op jit(solution)/shard_map/ppermute | solution.py:415
  35.1 5.0 %collective-permute-start.9 = (bf16[32,2048]{1,0:T(8,128)(2,1)S(1)}, bf16[32,2048]{1,0:T(8,128)(2,1)S(1)}, u32[]{:S(2)}, u32[]{:S(2)}) collective-permute-start(bf16[32,2048]{1,0:T(8,128)(2,1)S(1)} %get-tuple-element.62), channel_id=1, source_target_pairs={{0,8},{8,0},{16,24},{24,16},{1,9},{9,1},{17,25},{25,17},{2,10},{10... | collective-permute-start | bytes 393224 | tf_op jit(solution)/shard_map/ppermute | solution.py:415
